TPU v7x, 512 devices: a whole 4x4x16 slice. The times are simulated.
512 devices in a mesh: pipe: 16 (over y, x), tp: 32 (over z, core).
Axes of the slice: x: 4, y: 4, z: 16, core: 2. Of those that a mesh axis runs over, the one named last changes fastest.
Arguments:
- x_saved: bfloat16 [16, 128, 8192], P('pipe', None, 'tp'), may hold values from -8 to 8
- gains: float32 [16, 8192], P('pipe', 'tp'), may hold values from 0.1 to 1.9
- w_blocks: bfloat16 [16, 2304, 128, 128], P('pipe', 'tp')
- slot_pos: int32 [16, 2304], P('pipe', 'tp'), may hold values from 0 to 4095, as said below
- slot_live: int32 [16, 2304], P('pipe', 'tp'), may hold values from 0 to 1, as said below
- kl_grads: bfloat16 [2, 128, 8192], P(None, None, 'tp')
- teacher: int32 [128], replicated, may hold values 0 or 1
Outputs:
- w_grads: bfloat16 [16, 2304, 128, 128], P('pipe', 'tp')
- gain_grads: float32 [16, 8192], P('pipe', 'tp')
Inputs may be any that keep to these rules, and one draw needn't show every extreme that they name: `slot_pos`: each slot's block index row_block * 64 + col_block. The slots held by tp device t lie in its own row blocks t * 2 to (t + 1) * 2 - 1, and within a layer all positions are distinct. Every layer holds each block whose row block equals its column block. `slot_live`: in each layer every tp device holds from 56 to 72 live slots, and one device holds exactly 72. The slots of blocks whose row block equals their column block are live.
All inputs are finite; a program needn't handle non-finite values.
Results may differ from a plain program's by a relative error of at most 0.012.
Values may be sent and summed in bfloat16 or wider, within the bound.
No kernel may reach another device: no remote copies, remote signals or barrier semaphores. Data moves between devices by JAX's collectives and lax.ppermute only.
A program may use at most 64 MiB of HBM per device.

v0:
```python
import jax
import jax.numpy as jnp
from jax import lax
from jax.sharding import PartitionSpec as P

norm_epsilon = 1e-05


def from_behind(block, axis, distance):
    devices = range(lax.axis_size(axis))
    route = [(i - distance, i) for i in devices if i - distance in devices]
    return lax.ppermute(block, axis, route)


def expand_rows(kept_blocks, local_pos, row_blocks, col_blocks):
    slot_count, block_size = (kept_blocks.shape[0], kept_blocks.shape[1])
    one_hot = (
        jnp.arange(row_blocks * col_blocks, dtype=jnp.int32)[:, None] == local_pos[None, :]
    ).astype(jnp.bfloat16)
    placed = jnp.dot(
        one_hot,
        kept_blocks.reshape(slot_count, block_size * block_size),
        preferred_element_type=jnp.float32,
    )
    placed = placed.reshape(row_blocks, col_blocks, block_size, block_size).transpose(0, 2, 1, 3)
    return placed.reshape(row_blocks * block_size, col_blocks * block_size).astype(jnp.bfloat16)


def per_device(x_saved, gains, w_blocks, slot_pos, slot_live, kl_grads, teacher):
    sections = lax.axis_size("pipe")
    section_id = lax.axis_index("pipe")
    shard_id = lax.axis_index("tp")
    inputs = x_saved[0].astype(jnp.float32)
    tokens, local_width = inputs.shape
    full_width = local_width * lax.axis_size("tp")
    block_size = w_blocks.shape[2]
    row_blocks = local_width // block_size
    col_blocks = full_width // block_size
    gain_row = gains[0]
    live_slot = slot_live[0]
    slot_count = live_slot.shape[0]
    kept_blocks = w_blocks[0] * live_slot[:, None, None].astype(jnp.bfloat16)
    local_pos = slot_pos[0] - shard_id * (row_blocks * col_blocks)
    row_of = local_pos // col_blocks
    col_of = local_pos % col_blocks
    total_sq = lax.psum(jnp.sum(inputs * inputs, axis=1), "tp")
    inv_rms = lax.rsqrt(total_sq / full_width + norm_epsilon)
    unit_rows = inputs * inv_rms[:, None]
    entry_grads = jnp.where((teacher == 1)[:, None], kl_grads[1], kl_grads[0])
    step_rows = tokens // 4
    nblocks = tokens // step_rows
    expanded_w = expand_rows(kept_blocks, local_pos, row_blocks, col_blocks)

    def add_piece(segment):
        partial_value = lax.dot_general(
            segment, expanded_w, (((1,), (1,)), ((), ())), preferred_element_type=jnp.float32
        )
        return (partial_value, segment)

    def branch(grad_local):
        initial = (
            jnp.zeros((step_rows, local_width), jnp.float32),
            jnp.zeros((step_rows, full_width), jnp.bfloat16),
        )
        return add_piece(lax.all_gather(grad_local, "tp", axis=1, tiled=True))

    def advance(step_idx, running):
        incoming, slot_acc, gain_acc = running
        block_idx = step_idx - (sections - 1 - section_id)
        usable = (block_idx >= 0) & (block_idx < nblocks)
        row_start = jnp.clip(block_idx, 0, nblocks - 1) * step_rows
        first_rows = lax.dynamic_slice_in_dim(entry_grads, row_start, step_rows, 0)
        grad_local = jnp.where(section_id == sections - 1, first_rows, incoming)
        normed_grad, gathered = branch(grad_local)
        unit_block = lax.dynamic_slice_in_dim(unit_rows, row_start, step_rows, 0)
        rms_block = lax.dynamic_slice_in_dim(inv_rms, row_start, step_rows, 0)
        scaled_dn = gain_row * normed_grad
        dot_sums = lax.psum(jnp.sum(scaled_dn * unit_block, axis=1), "tp")
        input_grad = grad_local.astype(jnp.float32) + rms_block[:, None] * (
            scaled_dn - unit_block * (dot_sums / full_width)[:, None]
        )
        passed = from_behind(input_grad.astype(jnp.bfloat16), "pipe", -1)
        normed_block = (unit_block * gain_row).astype(jnp.bfloat16)

        def add_grads(totals):
            left_rows = normed_block.reshape(step_rows, row_blocks, block_size)[:, row_of, :]
            right_rows = gathered.reshape(step_rows, col_blocks, block_size)[:, col_of, :]
            return totals + jnp.einsum(
                "tka,tkb->kab", left_rows, right_rows, preferred_element_type=jnp.float32
            )

        slot_acc = lax.cond(usable, add_grads, lambda totals: totals, slot_acc)
        gain_acc = gain_acc + jnp.where(usable, jnp.sum(normed_grad * unit_block, axis=0), 0.0)
        return (passed, slot_acc, gain_acc)

    initial = (
        jnp.zeros((step_rows, local_width), jnp.bfloat16),
        jnp.zeros((slot_count, block_size, block_size), jnp.float32),
        jnp.zeros((local_width,), jnp.float32),
    )
    passed, slot_acc, gain_acc = lax.fori_loop(0, sections + nblocks - 1, advance, initial)
    live_float = live_slot[:, None, None].astype(jnp.float32)
    slot_grads = slot_acc * live_float
    return (slot_grads.astype(jnp.bfloat16)[None], gain_acc[None])


def solution(mesh):
    in_specs = (
        P("pipe", None, "tp"),
        P("pipe", "tp"),
        P("pipe", "tp", None, None),
        P("pipe", "tp"),
        P("pipe", "tp"),
        P(None, None, "tp"),
        P(),
    )
    out_specs = (P("pipe", "tp", None, None), P("pipe", "tp"))
    return jax.shard_map(
        per_device, mesh=mesh, in_specs=in_specs, out_specs=out_specs, check_vma=False
    )
```

profile of v0, /device:TPU:1, one launch (start us, length us, event | category | flops | bytes accessed | tf_op | source)
XLA Modules:
  0.0 1738.3 jit_solution(11642566038763894354)
XLA Ops:
  2.2 53.3 %psum.20 = f32[128]{0:T(128)S(1)} all-reduce(f32[128]{0:T(128)S(1)} %fusion.5), channel_id=1, replica_groups=mesh['pipe'=16,'tp'=32] {'tp'}, use_global_device_ids=true, to_apply=%region_1.2 | all-reduce | flops 128 | bytes 1024 | tf_op jit(solution)/shard_map/psum | solution.py:46
  75.9 1658.2 %while.23 = (s32[]{:T(128)}, bf16[32,256]{1,0:T(8,128)(2,1)S(1)}, f32[72,128,128]{2,1,0:T(8,128)}, f32[256]{0:T(256)S(1)}, pred[]{:T(512)}, /*index=5*/s32[]{:T(...) while((s32[]{:T(128)}, bf16[32,256]{1,0:T(8,128)(2,1)S(1)}, ...), condition=%wide.region_8.9_spmd.clone, body=%wide.region_2.8_spmd.clone.sunk | while | flops 211020752 | bytes 19629836 | solution.py:101
  110.6 45.3 %psum.23 = f32[32]{0:T(128)S(1)} all-reduce(f32[32]{0:T(128)S(1)} %get-tuple-element.472), channel_id=1, replica_groups=mesh['pipe'=16,'tp'=32] {'tp'}, use_global_device_ids=true, to_apply=%region_4.4 | all-reduce | flops 32 | bytes 256 | tf_op jit(solution)/shard_map/while/body/eval_jaxpr/psum | solution.py:78
  160.6 31.8 %all_gather.11 = bf16[32,8192]{1,0:T(8,128)(2,1)S(1)} all-gather(bf16[32,256]{1,0:T(8,128)(2,1)S(1)} %dynamic-slice_select_fusion.2), channel_id=1, replica_groups=mesh['pipe'=16,'tp'=32] {'tp'}, dimensions={1}, use_global_device_ids=true | all-gather | bytes 540672 | tf_op jit(solution)/shard_map/while/body/eval_jaxpr/all_gather | solution.py:65
  196.0 45.3 %psum.23 = f32[32]{0:T(128)S(1)} all-reduce(f32[32]{0:T(128)S(1)} %get-tuple-element.472), channel_id=1, replica_groups=mesh['pipe'=16,'tp'=32] {'tp'}, use_global_device_ids=true, to_apply=%region_4.4 | all-reduce | flops 32 | bytes 256 | tf_op jit(solution)/shard_map/while/body/eval_jaxpr/psum | solution.py:78
  246.0 31.8 %all_gather.11 = bf16[32,8192]{1,0:T(8,128)(2,1)S(1)} all-gather(bf16[32,256]{1,0:T(8,128)(2,1)S(1)} %dynamic-slice_select_fusion.2), channel_id=1, replica_groups=mesh['pipe'=16,'tp'=32] {'tp'}, dimensions={1}, use_global_device_ids=true | all-gather | bytes 540672 | tf_op jit(solution)/shard_map/while/body/eval_jaxpr/all_gather | solution.py:65
  281.4 45.3 %psum.23 = f32[32]{0:T(128)S(1)} all-reduce(f32[32]{0:T(128)S(1)} %get-tuple-element.472), channel_id=1, replica_groups=mesh['pipe'=16,'tp'=32] {'tp'}, use_global_device_ids=true, to_apply=%region_4.4 | all-reduce | flops 32 | bytes 256 | tf_op jit(solution)/shard_map/while/body/eval_jaxpr/psum | solution.py:78
  331.4 31.8 %all_gather.11 = bf16[32,8192]{1,0:T(8,128)(2,1)S(1)} all-gather(bf16[32,256]{1,0:T(8,128)(2,1)S(1)} %dynamic-slice_select_fusion.2), channel_id=1, replica_groups=mesh['pipe'=16,'tp'=32] {'tp'}, dimensions={1}, use_global_device_ids=true | all-gather | bytes 540672 | tf_op jit(solution)/shard_map/while/body/eval_jaxpr/all_gather | solution.py:65
  366.8 45.3 %psum.23 = f32[32]{0:T(128)S(1)} all-reduce(f32[32]{0:T(128)S(1)} %get-tuple-element.472), channel_id=1, replica_groups=mesh['pipe'=16,'tp'=32] {'tp'}, use_global_device_ids=true, to_apply=%region_4.4 | all-reduce | flops 32 | bytes 256 | tf_op jit(solution)/shard_map/while/body/eval_jaxpr/psum | solution.py:78
  452.4 45.3 %psum.23 = f32[32]{0:T(128)S(1)} all-reduce(f32[32]{0:T(128)S(1)} %get-tuple-element.472), channel_id=1, replica_groups=mesh['pipe'=16,'tp'=32] {'tp'}, use_global_device_ids=true, to_apply=%region_4.4 | all-reduce | flops 32 | bytes 256 | tf_op jit(solution)/shard_map/while/body/eval_jaxpr/psum | solution.py:78
  539.9 45.3 %psum.23 = f32[32]{0:T(128)S(1)} all-reduce(f32[32]{0:T(128)S(1)} %get-tuple-element.472), channel_id=1, replica_groups=mesh['pipe'=16,'tp'=32] {'tp'}, use_global_device_ids=true, to_apply=%region_4.4 | all-reduce | flops 32 | bytes 256 | tf_op jit(solution)/shard_map/while/body/eval_jaxpr/psum | solution.py:78
  627.4 45.3 %psum.23 = f32[32]{0:T(128)S(1)} all-reduce(f32[32]{0:T(128)S(1)} %get-tuple-element.472), channel_id=1, replica_groups=mesh['pipe'=16,'tp'=32] {'tp'}, use_global_device_ids=true, to_apply=%region_4.4 | all-reduce | flops 32 | bytes 256 | tf_op jit(solution)/shard_map/while/body/eval_jaxpr/psum | solution.py:78
  714.9 45.3 %psum.23 = f32[32]{0:T(128)S(1)} all-reduce(f32[32]{0:T(128)S(1)} %get-tuple-element.472), channel_id=1, replica_groups=mesh['pipe'=16,'tp'=32] {'tp'}, use_global_device_ids=true, to_apply=%region_4.4 | all-reduce | flops 32 | bytes 256 | tf_op jit(solution)/shard_map/while/body/eval_jaxpr/psum | solution.py:78
  802.4 45.3 %psum.23 = f32[32]{0:T(128)S(1)} all-reduce(f32[32]{0:T(128)S(1)} %get-tuple-element.472), channel_id=1, replica_groups=mesh['pipe'=16,'tp'=32] {'tp'}, use_global_device_ids=true, to_apply=%region_4.4 | all-reduce | flops 32 | bytes 256 | tf_op jit(solution)/shard_map/while/body/eval_jaxpr/psum | solution.py:78
  889.9 45.3 %psum.23 = f32[32]{0:T(128)S(1)} all-reduce(f32[32]{0:T(128)S(1)} %get-tuple-element.472), channel_id=1, replica_groups=mesh['pipe'=16,'tp'=32] {'tp'}, use_global_device_ids=true, to_apply=%region_4.4 | all-reduce | flops 32 | bytes 256 | tf_op jit(solution)/shard_map/while/body/eval_jaxpr/psum | solution.py:78
  977.4 45.3 %psum.23 = f32[32]{0:T(128)S(1)} all-reduce(f32[32]{0:T(128)S(1)} %get-tuple-element.472), channel_id=1, replica_groups=mesh['pipe'=16,'tp'=32] {'tp'}, use_global_device_ids=true, to_apply=%region_4.4 | all-reduce | flops 32 | bytes 256 | tf_op jit(solution)/shard_map/while/body/eval_jaxpr/psum | solution.py:78
  1064.9 45.3 %psum.23 = f32[32]{0:T(128)S(1)} all-reduce(f32[32]{0:T(128)S(1)} %get-tuple-element.472), channel_id=1, replica_groups=mesh['pipe'=16,'tp'=32] {'tp'}, use_global_device_ids=true, to_apply=%region_4.4 | all-reduce | flops 32 | bytes 256 | tf_op jit(solution)/shard_map/while/body/eval_jaxpr/psum | solution.py:78
  1152.4 45.3 %psum.23 = f32[32]{0:T(128)S(1)} all-reduce(f32[32]{0:T(128)S(1)} %get-tuple-element.472), channel_id=1, replica_groups=mesh['pipe'=16,'tp'=32] {'tp'}, use_global_device_ids=true, to_apply=%region_4.4 | all-reduce | flops 32 | bytes 256 | tf_op jit(solution)/shard_map/while/body/eval_jaxpr/psum | solution.py:78
  1239.9 45.3 %psum.23 = f32[32]{0:T(128)S(1)} all-reduce(f32[32]{0:T(128)S(1)} %get-tuple-element.472), channel_id=1, replica_groups=mesh['pipe'=16,'tp'=32] {'tp'}, use_global_device_ids=true, to_apply=%region_4.4 | all-reduce | flops 32 | bytes 256 | tf_op jit(solution)/shard_map/while/body/eval_jaxpr/psum | solution.py:78
  1327.4 45.3 %psum.23 = f32[32]{0:T(128)S(1)} all-reduce(f32[32]{0:T(128)S(1)} %get-tuple-element.472), channel_id=1, replica_groups=mesh['pipe'=16,'tp'=32] {'tp'}, use_global_device_ids=true, to_apply=%region_4.4 | all-reduce | flops 32 | bytes 256 | tf_op jit(solution)/shard_map/while/body/eval_jaxpr/psum | solution.py:78
  1414.9 45.3 %psum.23 = f32[32]{0:T(128)S(1)} all-reduce(f32[32]{0:T(128)S(1)} %get-tuple-element.472), channel_id=1, replica_groups=mesh['pipe'=16,'tp'=32] {'tp'}, use_global_device_ids=true, to_apply=%region_4.4 | all-reduce | flops 32 | bytes 256 | tf_op jit(solution)/shard_map/while/body/eval_jaxpr/psum | solution.py:78
  1503.5 45.3 %psum.23 = f32[32]{0:T(128)S(1)} all-reduce(f32[32]{0:T(128)S(1)} %get-tuple-element.472), channel_id=1, replica_groups=mesh['pipe'=16,'tp'=32] {'tp'}, use_global_device_ids=true, to_apply=%region_4.4 | all-reduce | flops 32 | bytes 256 | tf_op jit(solution)/shard_map/while/body/eval_jaxpr/psum | solution.py:78
  1592.0 45.3 %psum.23 = f32[32]{0:T(128)S(1)} all-reduce(f32[32]{0:T(128)S(1)} %get-tuple-element.472), channel_id=1, replica_groups=mesh['pipe'=16,'tp'=32] {'tp'}, use_global_device_ids=true, to_apply=%region_4.4 | all-reduce | flops 32 | bytes 256 | tf_op jit(solution)/shard_map/while/body/eval_jaxpr/psum | solution.py:78
  1680.5 45.3 %psum.23 = f32[32]{0:T(128)S(1)} all-reduce(f32[32]{0:T(128)S(1)} %get-tuple-element.472), channel_id=1, replica_groups=mesh['pipe'=16,'tp'=32] {'tp'}, use_global_device_ids=true, to_apply=%region_4.4 | all-reduce | flops 32 | bytes 256 | tf_op jit(solution)/shard_map/while/body/eval_jaxpr/psum | solution.py:78
  (238 shorter events, 754.3 us)
Async XLA Ops:
  73.2 2.7 copy-start
  156.0 4.5 collective-permute-start
  241.4 4.5 collective-permute-start
  326.8 4.5 collective-permute-start
  412.2 5.0 collective-permute-start
  497.8 6.9 collective-permute-start
  585.3 6.9 collective-permute-start
  672.8 6.9 collective-permute-start
  760.3 6.9 collective-permute-start
  847.8 6.9 collective-permute-start
  935.3 6.9 collective-permute-start
  1022.8 6.9 collective-permute-start
  1110.3 6.9 collective-permute-start
  1197.8 6.9 collective-permute-start
  1285.3 6.9 collective-permute-start
  1372.8 6.9 collective-permute-start
  1460.3 8.1 collective-permute-start
  1548.9 8.1 collective-permute-start
  1637.4 8.1 collective-permute-start
  1725.9 8.1 collective-permute-start
  1734.1 4.2 copy-start.1
where the time goes:
time: 1750 us; the launch traced here: 1740 us
  blocking collectives  1510 us (86%)
  matrix products  95 us (5%)
  waiting for transfers between devices  73.8 us (4%)
  starting transfers between devices  24.5 us (1%)
  local copies, waits for them, and re-layouts  20 us (1%)
    psum x19, blocking collectives, advance(): dot_sums = lax.psum(jnp.sum(scaled_dn * unit_block, axis=1), 'tp')  861 us
    all_gather x19, blocking collectives, branch(): return add_piece(lax.all_gather(grad_local, 'tp', axis=1, tiled=True))  598 us
    ppermute x19, waiting for transfers between devices, from_behind(): return lax.ppermute(block, axis, route)  73.8 us
    dot_general x19, matrix products, add_piece(): lax.dot_general(segment, expanded_w, (((1,), (1,)), ((), ())), preferred_...  69.7 us
    psum x1, blocking collectives, per_device(): total_sq = lax.psum(jnp.sum(inputs * inputs, axis=1), 'tp')  53.3 us
  transfers between devices with their start and end apart: 19, of which 15 were waited for; matrix products, arithmetic and copies ran while one was open for 2% of the time, Pallas kernels for 0%

commit v1 on v0

v1 whole, which is shorter than its diff:
```python
import functools

import jax
import jax.numpy as jnp
from jax import lax
from jax.experimental import pallas as pl
from jax.experimental.pallas import tpu as pltpu
from jax.sharding import PartitionSpec as P

norm_epsilon = 1e-05
group = 4
lanes = 128
f32 = jnp.float32
bf16 = jnp.bfloat16
across_last = (((1,), (1,)), ((), ()))


def params(mebibytes):
    return pltpu.CompilerParams(vmem_limit_bytes=mebibytes << 20)


def expand_body(code_ref, blocks_ref, dense_ref, *, col_blocks):
    slots, size = blocks_ref.shape[0], blocks_ref.shape[1]
    dead = 2 * col_blocks
    dense_ref[...] = jnp.zeros_like(dense_ref)

    def place(slot, carry):
        code = code_ref[slot]

        @pl.when(code < dead)
        def _():
            row, col = code // col_blocks, code % col_blocks
            rows = pl.ds(pl.multiple_of(row * size, size), size)
            cols = pl.ds(pl.multiple_of((col % 2) * size, size), size)
            dense_ref[col // 2, rows, cols] = blocks_ref[slot]

        return carry

    lax.fori_loop(0, slots, place, 0)


def expand(codes, blocks, shards):
    width = 2 * blocks.shape[1]
    return pl.pallas_call(
        functools.partial(expand_body, col_blocks=2 * shards),
        out_shape=jax.ShapeDtypeStruct((shards, width, width), bf16),
        in_specs=[
            pl.BlockSpec(memory_space=pltpu.SMEM),
            pl.BlockSpec(memory_space=pltpu.VMEM),
        ],
        out_specs=pl.BlockSpec(memory_space=pltpu.VMEM),
        compiler_params=params(24),
        name="expand",
    )(codes, blocks)


def layer_body(
    gathered, tails, own, above, above_own, above_scale, weight, here, inv_rms, gain,
    full_out, sent_out, own_out, total, shift,
):
    step, last = pl.program_id(0), pl.num_programs(0) - 1
    width = weight.shape[1]

    @pl.when(step == 0)
    def _():
        dots = jnp.sum(jnp.sum(tails[...].astype(f32), axis=0), axis=1, keepdims=True)
        shift[...] = jnp.broadcast_to(above_scale[...] * dots, shift.shape)
        total[...] = jnp.zeros_like(total)

    factor = shift[:, :1]
    acc = total[...]
    for i in range(gathered.shape[0]):
        piece = gathered[i, :, :width].astype(f32) - factor * above[i].astype(f32)
        piece = piece.astype(bf16)
        full_out[i] = piece
        acc += lax.dot_general(piece, weight[i], across_last, preferred_element_type=f32)
    total[...] = acc

    @pl.when(step == last)
    def _():
        grad = own[...] - factor * above_own[...].astype(f32)
        scaled = gain[...] * acc
        rms = inv_rms[...]
        dots = jnp.sum(scaled * (here[...].astype(f32) * rms), axis=1, keepdims=True)
        result = grad + rms * scaled
        own_out[...] = result
        sent_out[:, :width] = result.astype(bf16)
        high = dots.astype(bf16).astype(f32)
        low = (dots - high).astype(bf16).astype(f32)
        lane = lax.broadcasted_iota(jnp.int32, (dots.shape[0], lanes), 1)
        tail = jnp.where(lane == 0, high, jnp.where(lane == 1, low, 0.0))
        sent_out[:, width:] = tail.astype(bf16)


def layer(gathered, own, above, above_at, above_own, above_scale, weight, here, inv_rms, gain):
    shards, tokens, wide = gathered.shape
    width = wide - lanes
    chunk = min(8, shards)

    def whole(*shape):
        return pl.BlockSpec(shape, lambda c: (0,) * len(shape))

    return pl.pallas_call(
        layer_body,
        grid=(shards // chunk,),
        out_shape=(
            jax.ShapeDtypeStruct((shards, tokens, width), bf16),
            jax.ShapeDtypeStruct((tokens, wide), bf16),
            jax.ShapeDtypeStruct((tokens, width), f32),
        ),
        in_specs=[
            pl.BlockSpec((chunk, tokens, wide), lambda c: (c, 0, 0)),
            pl.BlockSpec((shards, tokens, lanes), lambda c: (0, 0, width // lanes)),
            whole(tokens, width),
            pl.BlockSpec((chunk, tokens, width), lambda c: (c, above_at, 0)),
            whole(tokens, width),
            whole(tokens, 1),
            pl.BlockSpec((chunk, width, width), lambda c: (c, 0, 0)),
            whole(tokens, width),
            whole(tokens, 1),
            whole(1, width),
        ],
        out_specs=(
            pl.BlockSpec((chunk, tokens, width), lambda c: (c, 0, 0)),
            whole(tokens, wide),
            whole(tokens, width),
        ),
        scratch_shapes=[pltpu.VMEM((tokens, width), f32), pltpu.VMEM((tokens, lanes), f32)],
        compiler_params=params(16),
        name="layer",
    )(gathered, gathered, own, above, above_own, above_scale, weight, here, inv_rms, gain)


def grads_body(code_ref, came, inputs, gain, blocks, out, gain_out, right, left, totals, *, col_blocks):
    size = blocks.shape[1]
    shards, part = came.shape[1] - 1, came.shape[2]
    rms = []
    for x in range(group):
        rms.append(jnp.sum(came[x, shards].astype(f32), axis=1, keepdims=True))
    rms = jnp.concatenate(rms, axis=0)
    normed = (inputs[...].astype(f32) * rms * gain[...]).astype(bf16).astype(f32)
    for row in range(2):
        left[row] = normed[:, row * size:(row + 1) * size].T.astype(bf16)
        totals[row] = jnp.zeros_like(totals[row])

    def arrange(shard, carry):
        for x in range(group):
            rows = slice(x * part, (x + 1) * part)
            right[2 * shard, rows, :] = came[x, shard, :, :size]
            right[2 * shard + 1, rows, :] = came[x, shard, :, size:]
        return carry

    lax.fori_loop(0, shards, arrange, 0)
    dead = 2 * col_blocks

    def one(slot, carry):
        code = code_ref[slot]
        live = (code < dead).astype(f32)
        place = code % dead
        row, col = place // col_blocks, place % col_blocks
        grad = jnp.dot(left[row], right[col], preferred_element_type=f32) * live
        out[slot] = grad.astype(bf16)
        totals[row] += grad * blocks[slot].astype(f32)
        return carry

    lax.fori_loop(0, blocks.shape[0], one, 0)
    for row in range(2):
        gain_out[row * size:(row + 1) * size, :] = jnp.sum(totals[row], axis=1, keepdims=True)


def slot_grads(codes, came, inputs, gain, blocks):
    slots, size = blocks.shape[0], blocks.shape[1]
    tokens, width = inputs.shape
    shards = came.shape[1] - 1
    vmem = pl.BlockSpec(memory_space=pltpu.VMEM)
    return pl.pallas_call(
        functools.partial(grads_body, col_blocks=2 * shards),
        out_shape=(
            jax.ShapeDtypeStruct(blocks.shape, bf16),
            jax.ShapeDtypeStruct((width, 1), f32),
        ),
        in_specs=[pl.BlockSpec(memory_space=pltpu.SMEM)] + [vmem] * 4,
        out_specs=(vmem, vmem),
        scratch_shapes=[
            pltpu.VMEM((2 * shards, tokens, size), bf16),
            pltpu.VMEM((2, size, tokens), bf16),
            pltpu.VMEM((2, size, size), f32),
        ],
        compiler_params=params(32),
        name="slot_grads",
    )(codes, came, inputs, gain, blocks)


def in_parts(value):
    parts = []
    for _ in range(3):
        part = lax.reduce_precision(value, 8, 7)
        parts.append(part.astype(bf16))
        value = value - part
    return parts


def per_device(x_saved, gains, w_blocks, slot_pos, slot_live, kl_grads, teacher):
    sections, shards = lax.axis_size("pipe"), lax.axis_size("tp")
    section, shard = lax.axis_index("pipe"), lax.axis_index("tp")
    line, block = section // group, section % group
    lines = sections // group
    together = [[i * group + x for x in range(group)] for i in range(lines)]
    down = [(i, i - group) for i in range(group, sections)]
    tokens, width = x_saved.shape[1], x_saved.shape[2]
    part = tokens // group
    full_width = width * shards
    blocks = w_blocks[0]
    slots = blocks.shape[0]
    places = 4 * shards
    codes = slot_pos[0] - shard * places + places * (1 - slot_live[0])

    weights = lax.all_gather(blocks, "pipe", axis_index_groups=together)
    code_row = jnp.zeros((width,), f32).at[:slots].set(codes.astype(f32)).astype(bf16)
    notes = jnp.stack(in_parts(gains[0]) + [code_row])
    notes = jnp.concatenate([notes, jnp.zeros((12, width), bf16)])
    notes = jnp.broadcast_to(notes[None], (group,) + notes.shape)
    told = jnp.concatenate([x_saved[0].reshape(group, part, width), notes], axis=1)
    told = lax.all_to_all(told, "pipe", 0, 0, axis_index_groups=together)
    inputs = told[:, :part]
    gain_rows = jnp.sum(told[:, part:part + 3].astype(f32), axis=1)
    line_codes = told[:, part + 3, :slots].astype(jnp.int32)

    all_inputs = lax.all_gather(inputs.reshape(tokens, width), "tp")
    squares = jnp.sum(jnp.square(all_inputs.astype(f32)), axis=(0, 2))
    inv_rms = lax.rsqrt(squares / full_width + norm_epsilon).reshape(group, part, 1)
    correct = jnp.square(inv_rms) / full_width
    upper = lax.ppermute(all_inputs[:, :part], "pipe", down)
    upper_squares = jnp.sum(jnp.square(upper.astype(f32)), axis=(0, 2))
    upper_correct = (1.0 / (upper_squares / full_width + norm_epsilon) / full_width)[:, None]
    upper_own = lax.dynamic_index_in_dim(upper, shard, 0, keepdims=False)

    entry = jnp.where((teacher == 1)[:, None], kl_grads[1], kl_grads[0])
    entry = lax.dynamic_slice_in_dim(entry, block * part, part, 0)
    sent = jnp.concatenate([entry, jnp.zeros((part, lanes), bf16)], axis=1)
    own = entry.astype(f32)

    dense = [None] * group
    kept = [None] * group
    for step in range(sections):
        phase, place = step // group, group - 1 - step % group
        if phase == 0:
            dense[place] = expand(line_codes[place], weights[place], shards)
        if step == 0:
            above, above_at, above_own = all_inputs, 0, inputs[0]
            scale = jnp.zeros((part, 1), f32)
        elif place == group - 1:
            passed = jnp.concatenate([own, sent[:, width:].astype(f32)], axis=1)
            passed = lax.ppermute(passed, "pipe", down)
            own, sent = passed[:, :width], passed.astype(bf16)
            above, above_at, above_own, scale = upper, 0, upper_own, upper_correct
        else:
            above, above_at = all_inputs, place + 1
            above_own, scale = inputs[place + 1], correct[place + 1]
        gathered = lax.all_gather(sent, "tp")
        full, sent, own = layer(
            gathered, own, above, above_at, above_own, scale, dense[place],
            inputs[place], inv_rms[place], gain_rows[place][None],
        )
        if phase == 0:
            kept[place] = full
        else:
            kept[place] = jnp.where(line == lines - 1 - phase, full, kept[place])

    rms_parts = jnp.concatenate(in_parts(inv_rms), axis=2)
    rms_parts = jnp.pad(rms_parts, ((0, 0), (0, 0), (0, width - 3)))
    came = jnp.concatenate([jnp.stack(kept), rms_parts[:, None]], axis=1)
    came = lax.all_to_all(came, "pipe", 0, 0, axis_index_groups=together)
    w_grads, gain_sums = slot_grads(codes, came, x_saved[0], gains, blocks)
    return (w_grads[None], gain_sums.reshape(1, width) / gains)


def solution(mesh):
    in_specs = (
        P("pipe", None, "tp"),
        P("pipe", "tp"),
        P("pipe", "tp", None, None),
        P("pipe", "tp"),
        P("pipe", "tp"),
        P(None, None, "tp"),
        P(),
    )
    out_specs = (P("pipe", "tp", None, None), P("pipe", "tp"))
    return jax.shard_map(
        per_device, mesh=mesh, in_specs=in_specs, out_specs=out_specs, check_vma=False
    )
```

time: 1750 us -> 779 us (0.45)
  blocking collectives: 1510 us -> 536 us
  matrix products: 95 us -> 0 us
  waiting for transfers between devices: 73.8 us -> 135 us
  Pallas kernels: 0 us -> 60.2 us
  starting transfers between devices: 24.5 us -> 5.24 us
    psum x20 -> x0, blocking collectives: 914 us -> none  [the longest x19 861 us: advance(): dot_sums = lax.psum(jnp.sum(scaled_dn * unit_block, axis=1), 'tp')]
    all_gather x0 -> x2, waiting for transfers between devices: none -> 114 us  [the longest x1 81.2 us: per_device(): weights = lax.all_gather(blocks, 'pipe', axis_index_groups=together)]
    all_gather x19 -> x16, blocking collectives: 598 us -> 497 us  [per_device(): gathered = lax.all_gather(sent, 'tp')]
    dot_general x24 -> x0, matrix products: 95 us -> none  [the longest x19 69.7 us: add_piece(): lax.dot_general(segment, expanded_w, (((1,), (1,)), ((), ())), preferred_...]
    pallas_call x0 -> x21, Pallas kernels: none -> 60.2 us  [the longest x16 35.3 us: layer(): pl.pallas_call(layer_body, grid=(shards // chunk,), out_shape=(jax.ShapeD...]
    ppermute x19 -> x4, waiting for transfers between devices: 73.8 us -> 20.5 us  [the longest x3 11.3 us: per_device(): passed = lax.ppermute(passed, 'pipe', down)]
    all_to_all x0 -> x2, blocking collectives: none -> 39.3 us  [the longest x1 30 us: per_device(): came = lax.all_to_all(came, 'pipe', 0, 0, axis_index_groups=together)]
    ppermute x19 -> x4, starting transfers between devices: 24.5 us -> 5.16 us  [the longest x3 3.87 us: per_device(): passed = lax.ppermute(passed, 'pipe', down)]
  transfers between devices with their start and end apart: 19 -> 6, of which waited for: 15 -> 6; matrix products, arithmetic and copies ran while one was open for 2% -> 1% of each run, Pallas kernels for 0% -> 0%
where the time goes in v1:
time: 779 us; the launch traced here: 778 us
  blocking collectives  536 us (69%)
  waiting for transfers between devices  135 us (17%)
  Pallas kernels  60.2 us (8%)
  local copies, waits for them, and re-layouts  18.3 us (2%)
  between operations  14.7 us (2%)
  other arithmetic  8.44 us (1%)
    all_gather x16, blocking collectives, per_device(): gathered = lax.all_gather(sent, 'tp')  497 us
    all_gather x1, waiting for transfers between devices, per_device(): weights = lax.all_gather(blocks, 'pipe', axis_index_groups=together)  81.2 us
    pallas_call x16, Pallas kernels, layer(): pl.pallas_call(layer_body, grid=(shards // chunk,), out_shape=(jax.ShapeD...  35.3 us
    all_gather x1, waiting for transfers between devices, per_device(): all_inputs = lax.all_gather(inputs.reshape(tokens, width), 'tp')  33 us
    all_to_all x1, blocking collectives, per_device(): came = lax.all_to_all(came, 'pipe', 0, 0, axis_index_groups=together)  30 us
  transfers between devices with their start and end apart: 6, of which 6 were waited for; matrix products, arithmetic and copies ran while one was open for 1% of the time, Pallas kernels for 0%

profile of v1, /device:TPU:1, one launch (start us, length us, event | category | flops | bytes accessed | tf_op | source)
XLA Modules:
  0.0 778.3 jit_solution(10980514871199293979)
XLA Ops:
  10.3 9.3 %all_to_all.10 = bf16[4,48,256]{2,1,0:T(8,128)(2,1)S(1)} all-to-all(bf16[4,48,256]{2,1,0:T(8,128)(2,1)S(1)} %pad_maximum_fusion.1), channel_id=1, replica_groups={{0,32,64,96},{128,160,192,224},{256,288,320,352},{384,416,448,480},{1,3..., dimensions={0} | all-to-all | bytes 196608 | tf_op jit(solution)/shard_map/all_to_all | solution.py:224
  21.8 40.8 %all-gather = bf16[1024,384]{1,0:T(8,128)(2,1)S(1)} all-gather(bf16[32,384]{1,0:T(8,128)(2,1)S(1)} %concatenate.26), channel_id=2, replica_groups=mesh['pipe'=16,'tp'=32] {'tp'}, dimensions={0}, use_global_device_ids=true | all-gather | bytes 811008 | tf_op jit(solution)/shard_map/all_gather | solution.py:260
  63.8 33.0 %all-gather.19.cloned.1.call-done.above = bf16[32,128,256]{2,1,0:T(8,128)(2,1)} async-done(((bf16[1,128,256]{2,1,0:T(8,128)(2,1)}), bf16[32,128,256]{2,1,0:T(8,128)(2,1)}) %all-gather.19.cloned.1.call-update) | async-done | bytes 2097168 | tf_op jit(solution)/shard_map/all_gather | solution.py:229
  103.9 9.2 %collective-permute-done.1.above = bf16[32,32,256]{2,1,0:T(8,128)(2,1)S(1)} collective-permute-done((bf16[32,32,256]{2,1,0:T(8,128)(2,1)S(1)}, bf16[32,32,256]{2,1,0:T(8,128)(2,1)S(1)}, u32[]{:S(2)}, u32[]{:S(2)}) %collective-permute-start.1) | collective-permute-done | bytes 524320 | tf_op jit(solution)/shard_map/ppermute | solution.py:233
  113.8 81.2 %all-gather.21.cloned.1.call-done = bf16[4,72,128,128]{3,2,1,0:T(8,128)(2,1)} async-done(((bf16[1,72,128,128]{3,2,1,0:T(8,128)(2,1)}), bf16[4,72,128,128]{3,2,1,0:T(8,128)(2,1)}) %all-gather.21.cloned.1.call-update) | async-done | bytes 9437200 | tf_op jit(solution)/shard_map/all_gather | solution.py:218
  195.0 4.7 slice_bitcast_fusion
  204.9 33.5 %all-gather.1 = bf16[1024,384]{1,0:T(8,128)(2,1)S(1)} all-gather(bf16[32,384]{1,0:T(8,128)(2,1)S(1)} %get-tuple-element.62), channel_id=3, replica_groups=mesh['pipe'=16,'tp'=32] {'tp'}, dimensions={0}, use_global_device_ids=true | all-gather | bytes 811008 | tf_op jit(solution)/shard_map/all_gather | solution.py:260
  243.5 30.5 %all-gather.2 = bf16[1024,384]{1,0:T(8,128)(2,1)S(1)} all-gather(bf16[32,384]{1,0:T(8,128)(2,1)S(1)} %get-tuple-element.64), channel_id=4, replica_groups=mesh['pipe'=16,'tp'=32] {'tp'}, dimensions={0}, use_global_device_ids=true | all-gather | bytes 811008 | tf_op jit(solution)/shard_map/all_gather | solution.py:260
  279.0 30.8 %all-gather.3 = bf16[1024,384]{1,0:T(8,128)(2,1)S(1)} all-gather(bf16[32,384]{1,0:T(8,128)(2,1)S(1)} %get-tuple-element.66), channel_id=5, replica_groups=mesh['pipe'=16,'tp'=32] {'tp'}, dimensions={0}, use_global_device_ids=true | all-gather | bytes 811008 | tf_op jit(solution)/shard_map/all_gather | solution.py:260
  321.0 30.6 %all-gather.4 = bf16[1024,384]{1,0:T(8,128)(2,1)S(1)} all-gather(bf16[32,384]{1,0:T(8,128)(2,1)S(1)} %convert_element_type.94), channel_id=6, replica_groups=mesh['pipe'=16,'tp'=32] {'tp'}, dimensions={0}, use_global_device_ids=true | all-gather | bytes 811008 | tf_op jit(solution)/shard_map/all_gather | solution.py:260
  355.9 29.8 %all-gather.5 = bf16[1024,384]{1,0:T(8,128)(2,1)S(1)} all-gather(bf16[32,384]{1,0:T(8,128)(2,1)S(1)} %get-tuple-element.70), channel_id=7, replica_groups=mesh['pipe'=16,'tp'=32] {'tp'}, dimensions={0}, use_global_device_ids=true | all-gather | bytes 811008 | tf_op jit(solution)/shard_map/all_gather | solution.py:260
  387.9 30.0 %all-gather.6 = bf16[1024,384]{1,0:T(8,128)(2,1)S(1)} all-gather(bf16[32,384]{1,0:T(8,128)(2,1)S(1)} %get-tuple-element.72), channel_id=8, replica_groups=mesh['pipe'=16,'tp'=32] {'tp'}, dimensions={0}, use_global_device_ids=true | all-gather | bytes 811008 | tf_op jit(solution)/shard_map/all_gather | solution.py:260
  420.1 29.8 %all-gather.7 = bf16[1024,384]{1,0:T(8,128)(2,1)S(1)} all-gather(bf16[32,384]{1,0:T(8,128)(2,1)S(1)} %get-tuple-element.74), channel_id=9, replica_groups=mesh['pipe'=16,'tp'=32] {'tp'}, dimensions={0}, use_global_device_ids=true | all-gather | bytes 811008 | tf_op jit(solution)/shard_map/all_gather | solution.py:260
  454.4 3.8 collective-permute-done.2
  458.3 30.7 %all-gather.8 = bf16[1024,384]{1,0:T(8,128)(2,1)S(1)} all-gather(bf16[32,384]{1,0:T(8,128)(2,1)S(1)} %convert_element_type.97), channel_id=10, replica_groups=mesh['pipe'=16,'tp'=32] {'tp'}, dimensions={0}, use_global_device_ids=true | all-gather | bytes 811008 | tf_op jit(solution)/shard_map/all_gather | solution.py:260
  493.2 29.8 %all-gather.9 = bf16[1024,384]{1,0:T(8,128)(2,1)S(1)} all-gather(bf16[32,384]{1,0:T(8,128)(2,1)S(1)} %get-tuple-element.78), channel_id=11, replica_groups=mesh['pipe'=16,'tp'=32] {'tp'}, dimensions={0}, use_global_device_ids=true | all-gather | bytes 811008 | tf_op jit(solution)/shard_map/all_gather | solution.py:260
  525.1 30.2 %all-gather.10 = bf16[1024,384]{1,0:T(8,128)(2,1)S(1)} all-gather(bf16[32,384]{1,0:T(8,128)(2,1)S(1)} %get-tuple-element.80), channel_id=12, replica_groups=mesh['pipe'=16,'tp'=32] {'tp'}, dimensions={0}, use_global_device_ids=true | all-gather | bytes 811008 | tf_op jit(solution)/shard_map/all_gather | solution.py:260
  557.5 29.8 %all-gather.11 = bf16[1024,384]{1,0:T(8,128)(2,1)S(1)} all-gather(bf16[32,384]{1,0:T(8,128)(2,1)S(1)} %get-tuple-element.82), channel_id=13, replica_groups=mesh['pipe'=16,'tp'=32] {'tp'}, dimensions={0}, use_global_device_ids=true | all-gather | bytes 811008 | tf_op jit(solution)/shard_map/all_gather | solution.py:260
  594.4 31.1 %all-gather.12 = bf16[1024,384]{1,0:T(8,128)(2,1)S(1)} all-gather(bf16[32,384]{1,0:T(8,128)(2,1)S(1)} %convert_element_type.99), channel_id=14, replica_groups=mesh['pipe'=16,'tp'=32] {'tp'}, dimensions={0}, use_global_device_ids=true | all-gather | bytes 811008 | tf_op jit(solution)/shard_map/all_gather | solution.py:260
  627.6 29.7 %all-gather.13 = bf16[1024,384]{1,0:T(8,128)(2,1)S(1)} all-gather(bf16[32,384]{1,0:T(8,128)(2,1)S(1)} %get-tuple-element.86), channel_id=15, replica_groups=mesh['pipe'=16,'tp'=32] {'tp'}, dimensions={0}, use_global_device_ids=true | all-gather | bytes 811008 | tf_op jit(solution)/shard_map/all_gather | solution.py:260
  659.5 30.0 %all-gather.14 = bf16[1024,384]{1,0:T(8,128)(2,1)S(1)} all-gather(bf16[32,384]{1,0:T(8,128)(2,1)S(1)} %get-tuple-element.88), channel_id=16, replica_groups=mesh['pipe'=16,'tp'=32] {'tp'}, dimensions={0}, use_global_device_ids=true | all-gather | bytes 811008 | tf_op jit(solution)/shard_map/all_gather | solution.py:260
  691.7 29.8 %all-gather.15 = bf16[1024,384]{1,0:T(8,128)(2,1)S(1)} all-gather(bf16[32,384]{1,0:T(8,128)(2,1)S(1)} %get-tuple-element.90), channel_id=17, replica_groups=mesh['pipe'=16,'tp'=32] {'tp'}, dimensions={0}, use_global_device_ids=true | all-gather | bytes 811008 | tf_op jit(solution)/shard_map/all_gather | solution.py:260
  727.2 30.0 %all_to_all.11.came = bf16[4,33,32,256]{3,2,1,0:T(8,128)(2,1)S(1)} all-to-all(bf16[4,33,32,256]{3,2,1,0:T(8,128)(2,1)S(1)} %pad_maximum_fusion), channel_id=1, replica_groups={{0,32,64,96},{128,160,192,224},{256,288,320,352},{384,416,448,480},{1,3..., dimensions={0} | all-to-all | bytes 4325376 | tf_op jit(solution)/shard_map/all_to_all | solution.py:273
  757.2 13.6 %slot_grads.1 = (bf16[72,128,128]{2,1,0:T(8,128)(2,1)}, f32[256,1]{1,0:T(8,128)S(1)}) custom-call(s32[72]{0:T(128)S(1)} %copy-done.40, bf16[4,33,32,256]{3,2,1,0:T(8,128)(2,1)S(1)} %all_to_all.11.came, bf16[128,256]{1,0:T(8,128)(2,1)S(1)} %bitcast.115, f32[1,256]{1,0:T(1,128)S(1)} %copy-done.39, bf16[72,128,128]{2,1,0:T(8,128)(2,1)S(1)} %bitcast.81), custom_call_target="tpu_custom_call" | custom-call | tf_op jit(solution)/shard_map/slot_grads/pallas_call | solution.py:176
  (192 shorter events, 82.1 us)
Async XLA Ops:
  7.2 89.6 %all-gather.19.cloned.1.call-start = ((), (), s32[]{:S(2)}) async-start(), calls=%async_computation.2 | async-start | bytes 2162688 | tf_op jit(solution)/shard_map/all_gather | solution.py:229
  20.2 174.8 %all-gather.21.cloned.1.call-start = ((), (), s32[]{:S(2)}) async-start(), calls=%async_computation.3 | async-start | bytes 11796480 | tf_op jit(solution)/shard_map/all_gather | solution.py:218
  97.9 15.1 %collective-permute-start.1 = (bf16[32,32,256]{2,1,0:T(8,128)(2,1)S(1)}, bf16[32,32,256]{2,1,0:T(8,128)(2,1)S(1)}, u32[]{:S(2)}, u32[]{:S(2)}) collective-permute-start(bf16[32,32,256]{2,1,0:T(8,128)(2,1)S(1)} %slice.241), channel_id=1, source_target_pairs={{128,0},{160,32},{192,64},{224,96},{256,128},{288,160},{320,192},{... | collective-permute-start | bytes 1572872 | tf_op jit(solution)/shard_map/ppermute | solution.py:233
  202.7 35.7 %copy-start.43 = (s32[72]{0:T(128)S(1)}, s32[72]{0:T(128)}, u32[]{:S(2)}) copy-start(s32[72]{0:T(128)} %get-tuple-element.130.code_ref) | copy-start | bytes 868
  204.9 33.5 %copy-start.15 = (bf16[32,32,256]{2,1,0:T(8,128)(2,1)}, bf16[32,32,256]{2,1,0:T(8,128)(2,1)S(1)}, u32[]{:S(2)}) copy-start(bf16[32,32,256]{2,1,0:T(8,128)(2,1)S(1)} %get-tuple-element.107) | copy-start | bytes 1572868
  241.3 32.7 %copy-start.42 = (s32[72]{0:T(128)S(1)}, s32[72]{0:T(128)}, u32[]{:S(2)}) copy-start(s32[72]{0:T(128)} %get-tuple-element.129.code_ref) | copy-start | bytes 868
  276.8 33.0 %copy-start.41 = (s32[72]{0:T(128)S(1)}, s32[72]{0:T(128)}, u32[]{:S(2)}) copy-start(s32[72]{0:T(128)} %get-tuple-element.128.code_ref) | copy-start | bytes 868
  279.0 30.8 %copy-start.17 = (bf16[32,32,256]{2,1,0:T(8,128)(2,1)}, bf16[32,32,256]{2,1,0:T(8,128)(2,1)S(1)}, u32[]{:S(2)}) copy-start(bf16[32,32,256]{2,1,0:T(8,128)(2,1)S(1)} %get-tuple-element.99) | copy-start | bytes 1572868
  312.7 38.9 %copy-start.30 = (f32[32,1]{1,0:T(8,128)S(1)}, f32[32,1]{1,0:T(8,128)}, u32[]{:S(2)}) copy-start(f32[32,1]{1,0:T(8,128)} %copy.75.inv_rms) | copy-start | bytes 388
  312.7 38.9 %copy-start.38 = (f32[1,256]{1,0:T(1,128)S(1)}, f32[1,256]{1,0:T(1,128)}, u32[]{:S(2)}) copy-start(f32[1,256]{1,0:T(1,128)} %get-tuple-element.127.gain) | copy-start | bytes 3076
  315.7 5.3 collective-permute-start
  353.8 31.9 %copy-start.12 = (bf16[32,256,256]{2,1,0:T(8,128)(2,1)S(1)}, bf16[32,256,256]{2,1,0:T(8,128)(2,1)}, u32[]{:S(2)}) copy-start(bf16[32,256,256]{2,1,0:T(8,128)(2,1)} %copy-done.11) | copy-start | bytes 12582916
  355.9 32.0 %copy-start.19 = (bf16[32,32,256]{2,1,0:T(8,128)(2,1)}, bf16[32,32,256]{2,1,0:T(8,128)(2,1)S(1)}, u32[]{:S(2)}) copy-start(bf16[32,32,256]{2,1,0:T(8,128)(2,1)S(1)} %get-tuple-element.106) | copy-start | bytes 1572868
  385.7 32.2 %copy-start.5 = (bf16[32,256,256]{2,1,0:T(8,128)(2,1)S(1)}, bf16[32,256,256]{2,1,0:T(8,128)(2,1)}, u32[]{:S(2)}) copy-start(bf16[32,256,256]{2,1,0:T(8,128)(2,1)} %copy-done.4) | copy-start | bytes 12582916
  387.9 32.2 %copy-start.23 = (bf16[32,32,256]{2,1,0:T(8,128)(2,1)}, bf16[32,32,256]{2,1,0:T(8,128)(2,1)S(1)}, u32[]{:S(2)}) copy-start(bf16[32,32,256]{2,1,0:T(8,128)(2,1)S(1)} %get-tuple-element.102) | copy-start | bytes 1572868
  417.9 32.0 %copy-start.2 = (bf16[32,256,256]{2,1,0:T(8,128)(2,1)S(1)}, bf16[32,256,256]{2,1,0:T(8,128)(2,1)}, u32[]{:S(2)}) copy-start(bf16[32,256,256]{2,1,0:T(8,128)(2,1)} %copy-done.1) | copy-start | bytes 12582916
  420.1 32.0 %copy-start.25 = (bf16[32,32,256]{2,1,0:T(8,128)(2,1)}, bf16[32,32,256]{2,1,0:T(8,128)(2,1)S(1)}, u32[]{:S(2)}) copy-start(bf16[32,32,256]{2,1,0:T(8,128)(2,1)S(1)} %get-tuple-element.98) | copy-start | bytes 1572868
  452.9 5.3 collective-permute-start.2
  491.1 31.8 %copy-start.13 = (bf16[32,256,256]{2,1,0:T(8,128)(2,1)S(1)}, bf16[32,256,256]{2,1,0:T(8,128)(2,1)}, u32[]{:S(2)}) copy-start(bf16[32,256,256]{2,1,0:T(8,128)(2,1)} %copy-done.11) | copy-start | bytes 12582916
  523.0 32.4 %copy-start.6 = (bf16[32,256,256]{2,1,0:T(8,128)(2,1)S(1)}, bf16[32,256,256]{2,1,0:T(8,128)(2,1)}, u32[]{:S(2)}) copy-start(bf16[32,256,256]{2,1,0:T(8,128)(2,1)} %copy-done.4) | copy-start | bytes 12582916
  555.3 31.9 %copy-start.3 = (bf16[32,256,256]{2,1,0:T(8,128)(2,1)S(1)}, bf16[32,256,256]{2,1,0:T(8,128)(2,1)}, u32[]{:S(2)}) copy-start(bf16[32,256,256]{2,1,0:T(8,128)(2,1)} %copy-done.1) | copy-start | bytes 12582916
  587.3 38.2 %copy-start.10 = (bf16[32,256,256]{2,1,0:T(8,128)(2,1)S(1)}, bf16[32,256,256]{2,1,0:T(8,128)(2,1)}, u32[]{:S(2)}) copy-start(bf16[32,256,256]{2,1,0:T(8,128)(2,1)} %copy-done.7) | copy-start | bytes 12582916
  589.5 4.9 collective-permute-start.3
  727.1 30.1 %copy-start.14 = (bf16[1,72,128,128]{3,2,1,0:T(8,128)(2,1)S(1)}, bf16[1,72,128,128]{3,2,1,0:T(8,128)(2,1)}, u32[]{:S(2)}) copy-start(bf16[1,72,128,128]{3,2,1,0:T(8,128)(2,1)} %param.11) | copy-start | bytes 7077892
  (33 other events, 189.7 us)
Sparse Core Ops, SparseCore 0:
  20.3 76.4 all-gather.18
  98.9 96.0 all-gather.20

commit v2 on v1

--- a/solution.py
+++ b/solution.py
@@ -19,10 +19,21 @@
     return pltpu.CompilerParams(vmem_limit_bytes=mebibytes << 20)
 
 
-def expand_body(code_ref, blocks_ref, dense_ref, *, col_blocks):
-    slots, size = blocks_ref.shape[0], blocks_ref.shape[1]
+def expand_body(code_ref, from_ref, mine, near, far, wrap, dense_ref, blocks, arrival, *, col_blocks):
+    slots, size = blocks.shape[0], blocks.shape[1]
     dead = 2 * col_blocks
+    for distance, source in enumerate((mine, near, far, wrap)):
+
+        @pl.when(from_ref[0] == distance)
+        def _():
+            pltpu.make_async_copy(source, blocks, arrival.at[distance]).start()
+
     dense_ref[...] = jnp.zeros_like(dense_ref)
+    for distance, source in enumerate((mine, near, far, wrap)):
+
+        @pl.when(from_ref[0] == distance)
+        def _():
+            pltpu.make_async_copy(source, blocks, arrival.at[distance]).wait()
 
     def place(slot, carry):
         code = code_ref[slot]
@@ -32,26 +43,25 @@
             row, col = code // col_blocks, code % col_blocks
             rows = pl.ds(pl.multiple_of(row * size, size), size)
             cols = pl.ds(pl.multiple_of((col % 2) * size, size), size)
-            dense_ref[col // 2, rows, cols] = blocks_ref[slot]
+            dense_ref[col // 2, rows, cols] = blocks[slot]
 
         return carry
 
     lax.fori_loop(0, slots, place, 0)
 
 
-def expand(codes, blocks, shards):
-    width = 2 * blocks.shape[1]
+def expand(codes, distance, copies, shards):
+    width = 2 * copies[0].shape[1]
+    smem = pl.BlockSpec(memory_space=pltpu.SMEM)
     return pl.pallas_call(
         functools.partial(expand_body, col_blocks=2 * shards),
         out_shape=jax.ShapeDtypeStruct((shards, width, width), bf16),
-        in_specs=[
-            pl.BlockSpec(memory_space=pltpu.SMEM),
-            pl.BlockSpec(memory_space=pltpu.VMEM),
-        ],
+        in_specs=[smem, smem] + [pl.BlockSpec(memory_space=pl.ANY)] * group,
         out_specs=pl.BlockSpec(memory_space=pltpu.VMEM),
+        scratch_shapes=[pltpu.VMEM(copies[0].shape, bf16), pltpu.SemaphoreType.DMA((group,))],
         compiler_params=params(24),
         name="expand",
-    )(codes, blocks)
+    )(codes, distance.reshape(1), *copies)
 
 
 def layer_body(
@@ -131,47 +141,58 @@
     )(gathered, gathered, own, above, above_own, above_scale, weight, here, inv_rms, gain)
 
 
-def grads_body(code_ref, came, inputs, gain, blocks, out, gain_out, right, left, totals, *, col_blocks):
+def grads_body(
+    code_ref, came0, came1, came2, came3, inputs, gain, blocks, out, gain_out, right, left, totals,
+    *, col_blocks,
+):
     size = blocks.shape[1]
-    shards, part = came.shape[1] - 1, came.shape[2]
-    rms = []
+    came = (came0, came1, came2, came3)
+    shards, part = came0.shape[0] - 1, came0.shape[1]
     for x in range(group):
-        rms.append(jnp.sum(came[x, shards].astype(f32), axis=1, keepdims=True))
-    rms = jnp.concatenate(rms, axis=0)
-    normed = (inputs[...].astype(f32) * rms * gain[...]).astype(bf16).astype(f32)
+        rms = jnp.sum(came[x][shards].astype(f32), axis=1, keepdims=True)
+        normed = (inputs[x].astype(f32) * rms * gain[...]).astype(bf16)
+        right[0, x * part:(x + 1) * part, :] = normed[:, :size]
+        right[1, x * part:(x + 1) * part, :] = normed[:, size:]
     for row in range(2):
-        left[row] = normed[:, row * size:(row + 1) * size].T.astype(bf16)
+        left[row] = right[row].astype(f32).T.astype(bf16)
         totals[row] = jnp.zeros_like(totals[row])
 
     def arrange(shard, carry):
         for x in range(group):
             rows = slice(x * part, (x + 1) * part)
-            right[2 * shard, rows, :] = came[x, shard, :, :size]
-            right[2 * shard + 1, rows, :] = came[x, shard, :, size:]
+            right[2 * shard, rows, :] = came[x][shard, :, :size]
+            right[2 * shard + 1, rows, :] = came[x][shard, :, size:]
         return carry
 
     lax.fori_loop(0, shards, arrange, 0)
     dead = 2 * col_blocks
-
-    def one(slot, carry):
-        code = code_ref[slot]
-        live = (code < dead).astype(f32)
-        place = code % dead
-        row, col = place // col_blocks, place % col_blocks
-        grad = jnp.dot(left[row], right[col], preferred_element_type=f32) * live
-        out[slot] = grad.astype(bf16)
-        totals[row] += grad * blocks[slot].astype(f32)
+    slots = blocks.shape[0]
+    several = 4 if slots % 4 == 0 else 2
+
+    def some(first, carry):
+        found = []
+        for i in range(several):
+            code = code_ref[first * several + i]
+            live = (code < dead).astype(f32)
+            place = code % dead
+            row, col = place // col_blocks, place % col_blocks
+            grad = jnp.dot(left[row], right[col], preferred_element_type=f32) * live
+            found.append((row, grad))
+        for i, (row, grad) in enumerate(found):
+            slot = first * several + i
+            out[slot] = grad.astype(bf16)
+            totals[row] += grad * blocks[slot].astype(f32)
         return carry
 
-    lax.fori_loop(0, blocks.shape[0], one, 0)
+    lax.fori_loop(0, slots // several, some, 0)
     for row in range(2):
         gain_out[row * size:(row + 1) * size, :] = jnp.sum(totals[row], axis=1, keepdims=True)
 
 
 def slot_grads(codes, came, inputs, gain, blocks):
-    slots, size = blocks.shape[0], blocks.shape[1]
-    tokens, width = inputs.shape
-    shards = came.shape[1] - 1
+    size = blocks.shape[1]
+    parts, part, width = inputs.shape
+    shards = came[0].shape[0] - 1
     vmem = pl.BlockSpec(memory_space=pltpu.VMEM)
     return pl.pallas_call(
         functools.partial(grads_body, col_blocks=2 * shards),
@@ -179,16 +200,16 @@
             jax.ShapeDtypeStruct(blocks.shape, bf16),
             jax.ShapeDtypeStruct((width, 1), f32),
         ),
-        in_specs=[pl.BlockSpec(memory_space=pltpu.SMEM)] + [vmem] * 4,
+        in_specs=[pl.BlockSpec(memory_space=pltpu.SMEM)] + [vmem] * (group + 3),
         out_specs=(vmem, vmem),
         scratch_shapes=[
-            pltpu.VMEM((2 * shards, tokens, size), bf16),
-            pltpu.VMEM((2, size, tokens), bf16),
+            pltpu.VMEM((2 * shards, parts * part, size), bf16),
+            pltpu.VMEM((2, size, parts * part), bf16),
             pltpu.VMEM((2, size, size), f32),
         ],
         compiler_params=params(32),
         name="slot_grads",
-    )(codes, came, inputs, gain, blocks)
+    )(codes, *came, inputs, gain, blocks)
 
 
 def in_parts(value):
@@ -215,7 +236,6 @@
     places = 4 * shards
     codes = slot_pos[0] - shard * places + places * (1 - slot_live[0])
 
-    weights = lax.all_gather(blocks, "pipe", axis_index_groups=together)
     code_row = jnp.zeros((width,), f32).at[:slots].set(codes.astype(f32)).astype(bf16)
     notes = jnp.stack(in_parts(gains[0]) + [code_row])
     notes = jnp.concatenate([notes, jnp.zeros((12, width), bf16)])
@@ -226,42 +246,73 @@
     gain_rows = jnp.sum(told[:, part:part + 3].astype(f32), axis=1)
     line_codes = told[:, part + 3, :slots].astype(jnp.int32)
 
-    all_inputs = lax.all_gather(inputs.reshape(tokens, width), "tp")
-    squares = jnp.sum(jnp.square(all_inputs.astype(f32)), axis=(0, 2))
-    inv_rms = lax.rsqrt(squares / full_width + norm_epsilon).reshape(group, part, 1)
-    correct = jnp.square(inv_rms) / full_width
-    upper = lax.ppermute(all_inputs[:, :part], "pipe", down)
-    upper_squares = jnp.sum(jnp.square(upper.astype(f32)), axis=(0, 2))
-    upper_correct = (1.0 / (upper_squares / full_width + norm_epsilon) / full_width)[:, None]
-    upper_own = lax.dynamic_index_in_dim(upper, shard, 0, keepdims=False)
-
+    def partners(distance, places):
+        return [
+            (i * group + x, i * group + (x ^ distance)) for i in range(lines) for x in places
+        ]
+
+    def spread(array, places):
+        return [lax.ppermute(array, "pipe", partners(d, places)) for d in range(1, group)]
+
+    early = spread(blocks, (3, 2))
+
+    first = group - 1
+    partial = jnp.sum(jnp.square(inputs[first].astype(f32)), axis=1, keepdims=True)
     entry = jnp.where((teacher == 1)[:, None], kl_grads[1], kl_grads[0])
     entry = lax.dynamic_slice_in_dim(entry, block * part, part, 0)
-    sent = jnp.concatenate([entry, jnp.zeros((part, lanes), bf16)], axis=1)
     own = entry.astype(f32)
-
+    tail = jnp.concatenate(in_parts(partial) + [jnp.zeros((part, lanes - 3), bf16)], axis=1)
+    sent = jnp.concatenate([entry, tail], axis=1)
+    gathered = lax.all_gather(sent, "tp")
+    tails = gathered[:, :, width:].astype(f32)
+    first_rms = lax.rsqrt(jnp.sum(tails, axis=(0, 2)) / full_width + norm_epsilon)[:, None]
+
+    all_inputs = lax.all_gather(inputs.reshape(tokens, width), "tp")
     dense = [None] * group
     kept = [None] * group
     for step in range(sections):
-        phase, place = step // group, group - 1 - step % group
+        phase, place = step // group, first - step % group
         if phase == 0:
-            dense[place] = expand(line_codes[place], weights[place], shards)
+            copies = [blocks] + (early if place >= 2 else late)
+            dense[place] = expand(line_codes[place], block ^ place, copies, shards)
+        if step == 1:
+            gathered = lax.all_gather(sent, "tp")
+            gathered, all_inputs = lax.optimization_barrier((gathered, all_inputs))
+            squares = jnp.sum(jnp.square(all_inputs.astype(f32)), axis=(0, 2))
+            inv_rms = lax.rsqrt(squares / full_width + norm_epsilon).reshape(group, part, 1)
+            correct = jnp.square(inv_rms) / full_width
         if step == 0:
-            above, above_at, above_own = all_inputs, 0, inputs[0]
-            scale = jnp.zeros((part, 1), f32)
-        elif place == group - 1:
-            passed = jnp.concatenate([own, sent[:, width:].astype(f32)], axis=1)
+            above, above_at, above_own = jnp.zeros_like(gathered[:, :, :width]), 0, inputs[0]
+            scale, rms = jnp.zeros((part, 1), f32), first_rms
+        elif place == first:
+            notes = jnp.concatenate(
+                [sent[:, width:width + 2].astype(f32), correct[0]], axis=1
+            )
+            notes = jnp.pad(notes, ((0, 0), (0, lanes - 3)))
+            passed = jnp.concatenate([own, notes, inputs[0].astype(f32)], axis=1)
             passed = lax.ppermute(passed, "pipe", down)
-            own, sent = passed[:, :width], passed.astype(bf16)
-            above, above_at, above_own, scale = upper, 0, upper_own, upper_correct
+            own = passed[:, :width]
+            tail = jnp.pad(passed[:, width:width + 2], ((0, 0), (0, lanes - 2)))
+            sent = jnp.concatenate([own, tail], axis=1).astype(bf16)
+            scale = passed[:, width + 2:width + 3]
+            above, above_at, above_own = upper, 0, passed[:, width + lanes:]
+            rms = inv_rms[place]
         else:
             above, above_at = all_inputs, place + 1
-            above_own, scale = inputs[place + 1], correct[place + 1]
-        gathered = lax.all_gather(sent, "tp")
+            above_own, scale, rms = inputs[place + 1], correct[place + 1], inv_rms[place]
+        if step > 1:
+            gathered = lax.all_gather(sent, "tp")
+        if step == 3:
+            gathered, upper = lax.optimization_barrier((gathered, upper))
         full, sent, own = layer(
             gathered, own, above, above_at, above_own, scale, dense[place],
-            inputs[place], inv_rms[place], gain_rows[place][None],
+            inputs[place], rms, gain_rows[place][None],
         )
+        if step == 0:
+            later_blocks, sent = lax.optimization_barrier((blocks, sent))
+            late = spread(later_blocks, (1, 0))
+        if step == 1:
+            upper = lax.ppermute(all_inputs[:, :part], "pipe", down)
         if phase == 0:
             kept[place] = full
         else:
@@ -269,9 +320,17 @@
 
     rms_parts = jnp.concatenate(in_parts(inv_rms), axis=2)
     rms_parts = jnp.pad(rms_parts, ((0, 0), (0, 0), (0, width - 3)))
-    came = jnp.concatenate([jnp.stack(kept), rms_parts[:, None]], axis=1)
-    came = lax.all_to_all(came, "pipe", 0, 0, axis_index_groups=together)
-    w_grads, gain_sums = slot_grads(codes, came, x_saved[0], gains, blocks)
+    leaving = jnp.concatenate([jnp.stack(kept), rms_parts[:, None]], axis=1)
+    native = x_saved[0].reshape(group, part, width)
+    came, order = [], []
+    for distance in range(group):
+        other = block ^ distance
+        piece = lax.dynamic_index_in_dim(leaving, other, 0, keepdims=False)
+        if distance:
+            piece = lax.ppermute(piece, "pipe", partners(distance, range(group)))
+        came.append(piece)
+        order.append(lax.dynamic_index_in_dim(native, other, 0, keepdims=False))
+    w_grads, gain_sums = slot_grads(codes, came, jnp.stack(order), gains, blocks)
     return (w_grads[None], gain_sums.reshape(1, width) / gains)
 
 

time: 779 us -> 766 us (0.983)
  waiting for transfers between devices: 135 us -> 91.1 us
  starting transfers between devices: 5.24 us -> 26.2 us
  local copies, waits for them, and re-layouts: 18.3 us -> 27.1 us
    all_gather x1 -> x0, waiting for transfers between devices: 81.2 us -> none  [per_device(): weights = lax.all_gather(blocks, 'pipe', axis_index_groups=together)]
    ppermute x0 -> x9, waiting for transfers between devices: none -> 77.9 us  [the longest x6 52.1 us: spread(): lax.ppermute(array, 'pipe', partners(d, places))]
    all_gather x1, waiting for transfers between devices: 33 us -> 0.01 us  [per_device(): all_inputs = lax.all_gather(inputs.reshape(tokens, width), 'tp')]
    all_to_all x1 -> x0, blocking collectives: 30 us -> none  [per_device(): came = lax.all_to_all(came, 'pipe', 0, 0, axis_index_groups=together)]
    all_gather x16, blocking collectives: 497 us -> 526 us  [per_device(): gathered = lax.all_gather(sent, 'tp')]
    ppermute x0 -> x9, starting transfers between devices: none -> 21 us  [the longest x6 10.7 us: spread(): lax.ppermute(array, 'pipe', partners(d, places))]
    ppermute x1, waiting for transfers between devices: 9.18 us -> 0.01 us  [per_device(): upper = lax.ppermute(all_inputs[:, :part], 'pipe', down)]
    unnamed x102 -> x116, local copies, waits for them, and re-layouts: 8.25 us -> 16 us
  transfers between devices with their start and end apart: 6 -> 14, of which waited for: 6 -> 7; matrix products, arithmetic and copies ran while one was open for 1% -> 2% of each run, Pallas kernels for 0% -> 3%
where the time goes in v2:
time: 766 us; the launch traced here: 764 us
  blocking collectives  535 us (70%)
  waiting for transfers between devices  91.1 us (12%)
  Pallas kernels  59.5 us (8%)
  local copies, waits for them, and re-layouts  27.1 us (4%)
  starting transfers between devices  26.2 us (3%)
  between operations  14.9 us (2%)
  other arithmetic  10.4 us (1%)
    all_gather x16, blocking collectives, per_device(): gathered = lax.all_gather(sent, 'tp')  526 us
    ppermute x6, waiting for transfers between devices, spread(): lax.ppermute(array, 'pipe', partners(d, places))  52.1 us
    pallas_call x16, Pallas kernels, layer(): pl.pallas_call(layer_body, grid=(shards // chunk,), out_shape=(jax.ShapeD...  35.3 us
    ppermute x3, waiting for transfers between devices, per_device(): piece = lax.ppermute(piece, 'pipe', partners(distance, range(group)))  25.8 us
    pallas_call x4, Pallas kernels, expand(): pl.pallas_call(functools.partial(expand_body, col_blocks=2 * shards), out...  16.9 us
    unnamed x116, local copies, waits for them, and re-layouts  16 us
  transfers between devices with their start and end apart: 14, of which 7 were waited for; matrix products, arithmetic and copies ran while one was open for 2% of the time, Pallas kernels for 3%

profile of v2, /device:TPU:1, one launch (start us, length us, event | category | flops | bytes accessed | tf_op | source)
XLA Modules:
  0.0 764.4 jit_solution(6228156909452999780)
XLA Ops:
  10.2 9.3 %all_to_all.5 = bf16[4,48,256]{2,1,0:T(8,128)(2,1)S(1)} all-to-all(bf16[4,48,256]{2,1,0:T(8,128)(2,1)S(1)} %pad_maximum_fusion.4), channel_id=1, replica_groups={{0,32,64,96},{128,160,192,224},{256,288,320,352},{384,416,448,480},{1,3..., dimensions={0} | all-to-all | bytes 196608 | tf_op jit(solution)/shard_map/all_to_all | solution.py:244
  25.7 40.6 %all-gather = bf16[1024,384]{1,0:T(8,128)(2,1)S(1)} all-gather(bf16[32,384]{1,0:T(8,128)(2,1)S(1)} %concatenate.82), channel_id=2, replica_groups=mesh['pipe'=16,'tp'=32] {'tp'}, dimensions={0}, use_global_device_ids=true | all-gather | bytes 811008 | tf_op jit(solution)/shard_map/all_gather | solution.py:266
  68.4 52.1 %collective-permute-done.1.far = bf16[72,128,128]{2,1,0:T(8,128)(2,1)} collective-permute-done((bf16[72,128,128]{2,1,0:T(8,128)(2,1)}, bf16[72,128,128]{2,1,0:T(8,128)(2,1)}, u32[]{:S(2)}, u32[]{:S(2)}) %collective-permute-start.1) | collective-permute-done | bytes 2359328 | tf_op jit(solution)/shard_map/ppermute | solution.py:255
  142.1 49.1 %all-gather.1 = bf16[1024,384]{1,0:T(8,128)(2,1)S(1)} all-gather(bf16[32,384]{1,0:T(8,128)(2,1)S(1)} %get-tuple-element.69), channel_id=3, replica_groups=mesh['pipe'=16,'tp'=32] {'tp'}, dimensions={0}, use_global_device_ids=true | all-gather | bytes 811008 | tf_op jit(solution)/shard_map/all_gather | solution.py:279
  204.6 29.2 %all-gather.2 = bf16[1024,384]{1,0:T(8,128)(2,1)S(1)} all-gather(bf16[32,384]{1,0:T(8,128)(2,1)S(1)} %get-tuple-element.73), channel_id=4, replica_groups=mesh['pipe'=16,'tp'=32] {'tp'}, dimensions={0}, use_global_device_ids=true | all-gather | bytes 811008 | tf_op jit(solution)/shard_map/all_gather | solution.py:304
  243.9 45.9 %all-gather.3 = bf16[1024,384]{1,0:T(8,128)(2,1)S(1)} all-gather(bf16[32,384]{1,0:T(8,128)(2,1)S(1)} %get-tuple-element.76), channel_id=5, replica_groups=mesh['pipe'=16,'tp'=32] {'tp'}, dimensions={0}, use_global_device_ids=true | all-gather | bytes 811008 | tf_op jit(solution)/shard_map/all_gather | solution.py:304
  298.4 4.8 collective-permute-done.7
  303.2 29.7 %all_gather.102.gathered.tails = bf16[32,32,384]{2,1,0:T(8,128)(2,1)S(1)} all-gather(bf16[1,32,384]{2,1,0:T(8,128)(2,1)S(1)} %pad_maximum_fusion.6), channel_id=1, replica_groups=mesh['pipe'=16,'tp'=32] {'tp'}, dimensions={0}, use_global_device_ids=true | all-gather | bytes 811008 | tf_op jit(solution)/shard_map/all_gather | solution.py:304
  337.3 30.8 %all-gather.4 = bf16[1024,384]{1,0:T(8,128)(2,1)S(1)} all-gather(bf16[32,384]{1,0:T(8,128)(2,1)S(1)} %get-tuple-element.82), channel_id=6, replica_groups=mesh['pipe'=16,'tp'=32] {'tp'}, dimensions={0}, use_global_device_ids=true | all-gather | bytes 811008 | tf_op jit(solution)/shard_map/all_gather | solution.py:304
  370.4 29.2 %all-gather.5 = bf16[1024,384]{1,0:T(8,128)(2,1)S(1)} all-gather(bf16[32,384]{1,0:T(8,128)(2,1)S(1)} %get-tuple-element.84), channel_id=7, replica_groups=mesh['pipe'=16,'tp'=32] {'tp'}, dimensions={0}, use_global_device_ids=true | all-gather | bytes 811008 | tf_op jit(solution)/shard_map/all_gather | solution.py:304
  402.6 30.5 %all-gather.6 = bf16[1024,384]{1,0:T(8,128)(2,1)S(1)} all-gather(bf16[32,384]{1,0:T(8,128)(2,1)S(1)} %get-tuple-element.86), channel_id=8, replica_groups=mesh['pipe'=16,'tp'=32] {'tp'}, dimensions={0}, use_global_device_ids=true | all-gather | bytes 811008 | tf_op jit(solution)/shard_map/all_gather | solution.py:304
  442.9 30.0 %all_gather.109.gathered.tails = bf16[32,32,384]{2,1,0:T(8,128)(2,1)S(1)} all-gather(bf16[1,32,384]{2,1,0:T(8,128)(2,1)S(1)} %pad_maximum_fusion.7), channel_id=1, replica_groups=mesh['pipe'=16,'tp'=32] {'tp'}, dimensions={0}, use_global_device_ids=true | all-gather | bytes 811008 | tf_op jit(solution)/shard_map/all_gather | solution.py:304
  477.3 30.5 %all-gather.7 = bf16[1024,384]{1,0:T(8,128)(2,1)S(1)} all-gather(bf16[32,384]{1,0:T(8,128)(2,1)S(1)} %get-tuple-element.90), channel_id=9, replica_groups=mesh['pipe'=16,'tp'=32] {'tp'}, dimensions={0}, use_global_device_ids=true | all-gather | bytes 811008 | tf_op jit(solution)/shard_map/all_gather | solution.py:304
  510.1 29.4 %all-gather.8 = bf16[1024,384]{1,0:T(8,128)(2,1)S(1)} all-gather(bf16[32,384]{1,0:T(8,128)(2,1)S(1)} %get-tuple-element.92), channel_id=10, replica_groups=mesh['pipe'=16,'tp'=32] {'tp'}, dimensions={0}, use_global_device_ids=true | all-gather | bytes 811008 | tf_op jit(solution)/shard_map/all_gather | solution.py:304
  541.7 30.5 %all-gather.9 = bf16[1024,384]{1,0:T(8,128)(2,1)S(1)} all-gather(bf16[32,384]{1,0:T(8,128)(2,1)S(1)} %get-tuple-element.94), channel_id=11, replica_groups=mesh['pipe'=16,'tp'=32] {'tp'}, dimensions={0}, use_global_device_ids=true | all-gather | bytes 811008 | tf_op jit(solution)/shard_map/all_gather | solution.py:304
  580.3 30.0 %all_gather.116.gathered.tails = bf16[32,32,384]{2,1,0:T(8,128)(2,1)S(1)} all-gather(bf16[1,32,384]{2,1,0:T(8,128)(2,1)S(1)} %pad_maximum_fusion.8), channel_id=1, replica_groups=mesh['pipe'=16,'tp'=32] {'tp'}, dimensions={0}, use_global_device_ids=true | all-gather | bytes 811008 | tf_op jit(solution)/shard_map/all_gather | solution.py:304
  612.5 30.5 %all-gather.10 = bf16[1024,384]{1,0:T(8,128)(2,1)S(1)} all-gather(bf16[32,384]{1,0:T(8,128)(2,1)S(1)} %get-tuple-element.98), channel_id=12, replica_groups=mesh['pipe'=16,'tp'=32] {'tp'}, dimensions={0}, use_global_device_ids=true | all-gather | bytes 811008 | tf_op jit(solution)/shard_map/all_gather | solution.py:304
  645.3 29.2 %all-gather.11 = bf16[1024,384]{1,0:T(8,128)(2,1)S(1)} all-gather(bf16[32,384]{1,0:T(8,128)(2,1)S(1)} %get-tuple-element.100), channel_id=13, replica_groups=mesh['pipe'=16,'tp'=32] {'tp'}, dimensions={0}, use_global_device_ids=true | all-gather | bytes 811008 | tf_op jit(solution)/shard_map/all_gather | solution.py:304
  676.7 30.5 %all-gather.12 = bf16[1024,384]{1,0:T(8,128)(2,1)S(1)} all-gather(bf16[32,384]{1,0:T(8,128)(2,1)S(1)} %get-tuple-element.102), channel_id=14, replica_groups=mesh['pipe'=16,'tp'=32] {'tp'}, dimensions={0}, use_global_device_ids=true | all-gather | bytes 811008 | tf_op jit(solution)/shard_map/all_gather | solution.py:304
  716.7 5.1 collective-permute-start.11
  723.8 5.2 collective-permute-done.10.came1
  729.0 14.8 %collective-permute-done.11.came2 = bf16[33,32,256]{2,1,0:T(8,128)(2,1)S(1)} collective-permute-done((bf16[33,32,256]{2,1,0:T(8,128)(2,1)S(1)}, bf16[33,32,256]{2,1,0:T(8,128)(2,1)S(1)}, u32[]{:S(2)}, u32[]{:S(2)}) %collective-permute-start.11) | collective-permute-done | bytes 540704 | tf_op jit(solution)/shard_map/ppermute | solution.py:330
  743.7 5.8 collective-permute-done.12.came3
  749.6 7.3 slot_grads.1
  (244 shorter events, 119.2 us)
Async XLA Ops:
  7.2 184.1 %all-gather.15.cloned.1.call-start = ((), (), s32[]{:S(2)}) async-start(), calls=%async_computation.1 | async-start | bytes 2162688 | tf_op jit(solution)/shard_map/all_gather | solution.py:270
  20.1 48.3 %collective-permute-start = (bf16[72,128,128]{2,1,0:T(8,128)(2,1)}, bf16[72,128,128]{2,1,0:T(8,128)(2,1)S(1)}, u32[]{:S(2)}, u32[]{:S(2)}) collective-permute-start(bf16[72,128,128]{2,1,0:T(8,128)(2,1)} %bitcast.1.mine.blocks), channel_id=1, source_target_pairs={{96,64},{64,96},{224,192},{192,224},{352,320},{320,352},{480,448},... | collective-permute-start | bytes 7077896 | tf_op jit(solution)/shard_map/ppermute | solution.py:255
  21.0 99.6 %collective-permute-start.1 = (bf16[72,128,128]{2,1,0:T(8,128)(2,1)}, bf16[72,128,128]{2,1,0:T(8,128)(2,1)}, u32[]{:S(2)}, u32[]{:S(2)}) collective-permute-start(bf16[72,128,128]{2,1,0:T(8,128)(2,1)} %bitcast.1.mine.blocks), channel_id=1, source_target_pairs={{96,32},{64,0},{224,160},{192,128},{352,288},{320,256},{480,416},{... | collective-permute-start | bytes 7077896 | tf_op jit(solution)/shard_map/ppermute | solution.py:255
  22.3 98.3 %collective-permute-start.2 = (bf16[72,128,128]{2,1,0:T(8,128)(2,1)}, bf16[72,128,128]{2,1,0:T(8,128)(2,1)}, u32[]{:S(2)}, u32[]{:S(2)}) collective-permute-start(bf16[72,128,128]{2,1,0:T(8,128)(2,1)} %bitcast.1.mine.blocks), channel_id=1, source_target_pairs={{96,0},{64,32},{224,128},{192,160},{352,256},{320,288},{480,384},{... | collective-permute-start | bytes 7077896 | tf_op jit(solution)/shard_map/ppermute | solution.py:255
  67.8 57.2 %copy-start.44 = (f32[1,256]{1,0:T(1,128)}, f32[1,256]{1,0:T(1,128)S(1)}, u32[]{:S(2)}) copy-start(f32[1,256]{1,0:T(1,128)S(1)} %get-tuple-element.153.gain) | copy-start | bytes 3076
  67.8 130.8 %copy-start.41 = (f32[1,256]{1,0:T(1,128)}, f32[1,256]{1,0:T(1,128)S(1)}, u32[]{:S(2)}) copy-start(f32[1,256]{1,0:T(1,128)S(1)} %get-tuple-element.152.gain) | copy-start | bytes 3076
  128.5 108.2 %collective-permute-start.3 = (bf16[72,128,128]{2,1,0:T(8,128)(2,1)}, bf16[72,128,128]{2,1,0:T(8,128)(2,1)}, u32[]{:S(2)}, u32[]{:S(2)}) collective-permute-start(bf16[72,128,128]{2,1,0:T(8,128)(2,1)} %bitcast.1.mine.blocks), channel_id=1, source_target_pairs={{32,0},{0,32},{160,128},{128,160},{288,256},{256,288},{416,384},{3... | collective-permute-start | bytes 7077896 | tf_op jit(solution)/shard_map/ppermute | solution.py:255
  130.4 106.3 %collective-permute-start.4 = (bf16[72,128,128]{2,1,0:T(8,128)(2,1)}, bf16[72,128,128]{2,1,0:T(8,128)(2,1)}, u32[]{:S(2)}, u32[]{:S(2)}) collective-permute-start(bf16[72,128,128]{2,1,0:T(8,128)(2,1)} %bitcast.1.mine.blocks), channel_id=1, source_target_pairs={{32,96},{0,64},{160,224},{128,192},{288,352},{256,320},{416,480},{... | collective-permute-start | bytes 7077896 | tf_op jit(solution)/shard_map/ppermute | solution.py:255
  133.2 103.6 %collective-permute-start.5 = (bf16[72,128,128]{2,1,0:T(8,128)(2,1)}, bf16[72,128,128]{2,1,0:T(8,128)(2,1)}, u32[]{:S(2)}, u32[]{:S(2)}) collective-permute-start(bf16[72,128,128]{2,1,0:T(8,128)(2,1)} %bitcast.1.mine.blocks), channel_id=1, source_target_pairs={{32,64},{0,96},{160,192},{128,224},{288,320},{256,352},{416,448},{... | collective-permute-start | bytes 7077896 | tf_op jit(solution)/shard_map/ppermute | solution.py:255
  197.4 92.4 %collective-permute-start.6 = (bf16[32,32,256]{2,1,0:T(8,128)(2,1)}, bf16[32,32,256]{2,1,0:T(8,128)(2,1)S(1)}, u32[]{:S(2)}, u32[]{:S(2)}) collective-permute-start(bf16[32,32,256]{2,1,0:T(8,128)(2,1)} %slice.235), channel_id=1, source_target_pairs={{128,0},{160,32},{192,64},{224,96},{256,128},{288,160},{320,192},{... | collective-permute-start | bytes 1572872 | tf_op jit(solution)/shard_map/ppermute | solution.py:315
  241.7 48.1 %copy-start.47 = (s32[72]{0:T(128)S(1)}, s32[72]{0:T(128)}, u32[]{:S(2)}) copy-start(s32[72]{0:T(128)} %get-tuple-element.158.code_ref) | copy-start | bytes 868
  243.9 45.9 %copy-start.19 = (bf16[32,32,256]{2,1,0:T(8,128)(2,1)}, bf16[32,32,256]{2,1,0:T(8,128)(2,1)S(1)}, u32[]{:S(2)}) copy-start(bf16[32,32,256]{2,1,0:T(8,128)(2,1)S(1)} %get-tuple-element.111) | copy-start | bytes 1572868
  294.0 39.0 %copy-start.45 = (f32[1,256]{1,0:T(1,128)S(1)}, f32[1,256]{1,0:T(1,128)}, u32[]{:S(2)}) copy-start(f32[1,256]{1,0:T(1,128)} %copy-done.44) | copy-start | bytes 3076
  297.0 6.2 collective-permute-start.7
  335.2 32.9 %copy-start.42 = (f32[1,256]{1,0:T(1,128)S(1)}, f32[1,256]{1,0:T(1,128)}, u32[]{:S(2)}) copy-start(f32[1,256]{1,0:T(1,128)} %copy-done.41) | copy-start | bytes 3076
  399.6 33.5 %copy-start.13 = (bf16[32,256,256]{2,1,0:T(8,128)(2,1)S(1)}, bf16[32,256,256]{2,1,0:T(8,128)(2,1)}, u32[]{:S(2)}) copy-start(bf16[32,256,256]{2,1,0:T(8,128)(2,1)} %copy-done.12) | copy-start | bytes 12582916
  436.9 6.0 collective-permute-start.8
  572.2 38.2 %copy-start.4 = (bf16[32,256,256]{2,1,0:T(8,128)(2,1)S(1)}, bf16[32,256,256]{2,1,0:T(8,128)(2,1)}, u32[]{:S(2)}) copy-start(bf16[32,256,256]{2,1,0:T(8,128)(2,1)} %copy-done.1) | copy-start | bytes 12582916
  574.5 5.8 collective-permute-start.9
  713.1 36.5 %copy-start.46 = (f32[1,256]{1,0:T(1,128)S(1)}, f32[1,256]{1,0:T(1,128)}, u32[]{:S(2)}) copy-start(f32[1,256]{1,0:T(1,128)} %gain.1) | copy-start | bytes 3076
  713.1 36.5 %copy-start.49 = (s32[72]{0:T(128)S(1)}, s32[72]{0:T(128)}, u32[]{:S(2)}) copy-start(s32[72]{0:T(128)} %get-tuple-element.125.code_ref) | copy-start | bytes 868
  713.3 15.6 %collective-permute-start.10 = (bf16[33,32,256]{2,1,0:T(8,128)(2,1)S(1)}, bf16[33,32,256]{2,1,0:T(8,128)(2,1)S(1)}, u32[]{:S(2)}, u32[]{:S(2)}) collective-permute-start(bf16[33,32,256]{2,1,0:T(8,128)(2,1)S(1)} %get-tuple-element.128), channel_id=1, source_target_pairs={{0,32},{32,0},{64,96},{96,64},{128,160},{160,128},{192,224},{224,1... | collective-permute-start | bytes 1622024 | tf_op jit(solution)/shard_map/ppermute | solution.py:330
  716.7 27.0 %collective-permute-start.11 = (bf16[33,32,256]{2,1,0:T(8,128)(2,1)S(1)}, bf16[33,32,256]{2,1,0:T(8,128)(2,1)S(1)}, u32[]{:S(2)}, u32[]{:S(2)}) collective-permute-start(bf16[33,32,256]{2,1,0:T(8,128)(2,1)S(1)} %get-tuple-element.127), channel_id=1, source_target_pairs={{0,64},{32,96},{64,0},{96,32},{128,192},{160,224},{192,128},{224,1... | collective-permute-start | bytes 1622024 | tf_op jit(solution)/shard_map/ppermute | solution.py:330
  721.8 27.8 %collective-permute-start.12 = (bf16[33,32,256]{2,1,0:T(8,128)(2,1)S(1)}, bf16[33,32,256]{2,1,0:T(8,128)(2,1)S(1)}, u32[]{:S(2)}, u32[]{:S(2)}) collective-permute-start(bf16[33,32,256]{2,1,0:T(8,128)(2,1)S(1)} %get-tuple-element.126), channel_id=1, source_target_pairs={{0,96},{32,64},{64,32},{96,0},{128,224},{160,192},{192,160},{224,1... | collective-permute-start | bytes 1622024 | tf_op jit(solution)/shard_map/ppermute | solution.py:330
  (48 other events, 535.5 us)
Sparse Core Ops, SparseCore 0:
  20.3 76.2 all-gather.14

commit v3 on v2

--- a/solution.py
+++ b/solution.py
@@ -19,23 +19,15 @@
     return pltpu.CompilerParams(vmem_limit_bytes=mebibytes << 20)
 
 
-def expand_body(code_ref, from_ref, mine, near, far, wrap, dense_ref, blocks, arrival, *, col_blocks):
+def expand_body(code_ref, came, dense_ref, blocks, arrival, *, place, col_blocks):
     slots, size = blocks.shape[0], blocks.shape[1]
     dead = 2 * col_blocks
-    for distance, source in enumerate((mine, near, far, wrap)):
-
-        @pl.when(from_ref[0] == distance)
-        def _():
-            pltpu.make_async_copy(source, blocks, arrival.at[distance]).start()
-
+    fetch = pltpu.make_async_copy(came.at[place], blocks, arrival)
+    fetch.start()
     dense_ref[...] = jnp.zeros_like(dense_ref)
-    for distance, source in enumerate((mine, near, far, wrap)):
-
-        @pl.when(from_ref[0] == distance)
-        def _():
-            pltpu.make_async_copy(source, blocks, arrival.at[distance]).wait()
-
-    def place(slot, carry):
+    fetch.wait()
+
+    def put(slot, carry):
         code = code_ref[slot]
 
         @pl.when(code < dead)
@@ -47,21 +39,20 @@
 
         return carry
 
-    lax.fori_loop(0, slots, place, 0)
-
-
-def expand(codes, distance, copies, shards):
-    width = 2 * copies[0].shape[1]
-    smem = pl.BlockSpec(memory_space=pltpu.SMEM)
+    lax.fori_loop(0, slots, put, 0)
+
+
+def expand(codes, weights, place, shards):
+    width = 2 * weights.shape[2]
     return pl.pallas_call(
-        functools.partial(expand_body, col_blocks=2 * shards),
+        functools.partial(expand_body, place=place, col_blocks=2 * shards),
         out_shape=jax.ShapeDtypeStruct((shards, width, width), bf16),
-        in_specs=[smem, smem] + [pl.BlockSpec(memory_space=pl.ANY)] * group,
+        in_specs=[pl.BlockSpec(memory_space=pltpu.SMEM), pl.BlockSpec(memory_space=pl.ANY)],
         out_specs=pl.BlockSpec(memory_space=pltpu.VMEM),
-        scratch_shapes=[pltpu.VMEM(copies[0].shape, bf16), pltpu.SemaphoreType.DMA((group,))],
+        scratch_shapes=[pltpu.VMEM(weights.shape[1:], bf16), pltpu.SemaphoreType.DMA],
         compiler_params=params(24),
         name="expand",
-    )(codes, distance.reshape(1), *copies)
+    )(codes, weights)
 
 
 def layer_body(
@@ -142,14 +133,15 @@
 
 
 def grads_body(
-    code_ref, came0, came1, came2, came3, inputs, gain, blocks, out, gain_out, right, left, totals,
+    code_ref, mine, other, inputs, gain, blocks, out, gain_out, right, left, totals,
     *, col_blocks,
 ):
     size = blocks.shape[1]
-    came = (came0, came1, came2, came3)
-    shards, part = came0.shape[0] - 1, came0.shape[1]
+    half, part = mine.shape[1] - 1, mine.shape[2]
+    slots = blocks.shape[0]
+    core = code_ref[slots]
     for x in range(group):
-        rms = jnp.sum(came[x][shards].astype(f32), axis=1, keepdims=True)
+        rms = jnp.sum(mine[x, half].astype(f32), axis=1, keepdims=True)
         normed = (inputs[x].astype(f32) * rms * gain[...]).astype(bf16)
         right[0, x * part:(x + 1) * part, :] = normed[:, :size]
         right[1, x * part:(x + 1) * part, :] = normed[:, size:]
@@ -157,16 +149,17 @@
         left[row] = right[row].astype(f32).T.astype(bf16)
         totals[row] = jnp.zeros_like(totals[row])
 
-    def arrange(shard, carry):
-        for x in range(group):
-            rows = slice(x * part, (x + 1) * part)
-            right[2 * shard, rows, :] = came[x][shard, :, :size]
-            right[2 * shard + 1, rows, :] = came[x][shard, :, size:]
+    def arrange(place, carry):
+        for came, base in ((mine, core * half), (other, (1 - core) * half)):
+            col = 2 * (base + place)
+            for x in range(group):
+                rows = slice(x * part, (x + 1) * part)
+                right[col, rows, :] = came[x, place, :, :size]
+                right[col + 1, rows, :] = came[x, place, :, size:]
         return carry
 
-    lax.fori_loop(0, shards, arrange, 0)
+    lax.fori_loop(0, half, arrange, 0)
     dead = 2 * col_blocks
-    slots = blocks.shape[0]
     several = 4 if slots % 4 == 0 else 2
 
     def some(first, carry):
@@ -189,10 +182,10 @@
         gain_out[row * size:(row + 1) * size, :] = jnp.sum(totals[row], axis=1, keepdims=True)
 
 
-def slot_grads(codes, came, inputs, gain, blocks):
+def slot_grads(codes, mine, other, inputs, gain, blocks):
     size = blocks.shape[1]
     parts, part, width = inputs.shape
-    shards = came[0].shape[0] - 1
+    shards = 2 * (mine.shape[1] - 1)
     vmem = pl.BlockSpec(memory_space=pltpu.VMEM)
     return pl.pallas_call(
         functools.partial(grads_body, col_blocks=2 * shards),
@@ -200,7 +193,7 @@
             jax.ShapeDtypeStruct(blocks.shape, bf16),
             jax.ShapeDtypeStruct((width, 1), f32),
         ),
-        in_specs=[pl.BlockSpec(memory_space=pltpu.SMEM)] + [vmem] * (group + 3),
+        in_specs=[pl.BlockSpec(memory_space=pltpu.SMEM)] + [vmem] * 5,
         out_specs=(vmem, vmem),
         scratch_shapes=[
             pltpu.VMEM((2 * shards, parts * part, size), bf16),
@@ -209,7 +202,7 @@
         ],
         compiler_params=params(32),
         name="slot_grads",
-    )(codes, *came, inputs, gain, blocks)
+    )(codes, mine, other, inputs, gain, blocks)
 
 
 def in_parts(value):
@@ -246,44 +239,41 @@
     gain_rows = jnp.sum(told[:, part:part + 3].astype(f32), axis=1)
     line_codes = told[:, part + 3, :slots].astype(jnp.int32)
 
-    def partners(distance, places):
-        return [
-            (i * group + x, i * group + (x ^ distance)) for i in range(lines) for x in places
-        ]
-
-    def spread(array, places):
-        return [lax.ppermute(array, "pipe", partners(d, places)) for d in range(1, group)]
-
-    early = spread(blocks, (3, 2))
-
     first = group - 1
-    partial = jnp.sum(jnp.square(inputs[first].astype(f32)), axis=1, keepdims=True)
+    weights = lax.all_gather(blocks, "pipe", axis_index_groups=together)
+    second_inputs = lax.all_gather(inputs[first], "tp")
+
+    partial = jnp.sum(jnp.square(inputs.astype(f32)), axis=2)
+    partial = jnp.concatenate([p.T for p in in_parts(partial)], axis=1)
+    partial = jnp.pad(partial, ((0, 0), (0, lanes - 3 * group)))
     entry = jnp.where((teacher == 1)[:, None], kl_grads[1], kl_grads[0])
     entry = lax.dynamic_slice_in_dim(entry, block * part, part, 0)
     own = entry.astype(f32)
-    tail = jnp.concatenate(in_parts(partial) + [jnp.zeros((part, lanes - 3), bf16)], axis=1)
-    sent = jnp.concatenate([entry, tail], axis=1)
+    sent = jnp.concatenate([entry, partial], axis=1)
+    sent, second_inputs = lax.optimization_barrier((sent, second_inputs))
     gathered = lax.all_gather(sent, "tp")
-    tails = gathered[:, :, width:].astype(f32)
-    first_rms = lax.rsqrt(jnp.sum(tails, axis=(0, 2)) / full_width + norm_epsilon)[:, None]
-
-    all_inputs = lax.all_gather(inputs.reshape(tokens, width), "tp")
+    squares = jnp.sum(gathered[:, :, width:].astype(f32), axis=0)[:, :3 * group]
+    squares = jnp.sum(squares.reshape(part, 3, group), axis=1).T
+    inv_rms = lax.rsqrt(squares / full_width + norm_epsilon)[:, :, None]
+    correct = jnp.square(inv_rms) / full_width
+
+    third, gathered = lax.optimization_barrier((inputs[first - 1], gathered))
+    third_inputs = lax.all_gather(third, "tp")
+    weights, third_inputs = lax.optimization_barrier((weights, third_inputs))
+    rest, weights = lax.optimization_barrier((inputs[:first - 1], weights))
+    rest_inputs = lax.all_gather(rest.reshape((first - 1) * part, width), "tp")
+
+    found = {first: (second_inputs, 0), first - 1: (third_inputs, 0)}
     dense = [None] * group
     kept = [None] * group
+    half = shards // 2
     for step in range(sections):
         phase, place = step // group, first - step % group
         if phase == 0:
-            copies = [blocks] + (early if place >= 2 else late)
-            dense[place] = expand(line_codes[place], block ^ place, copies, shards)
-        if step == 1:
-            gathered = lax.all_gather(sent, "tp")
-            gathered, all_inputs = lax.optimization_barrier((gathered, all_inputs))
-            squares = jnp.sum(jnp.square(all_inputs.astype(f32)), axis=(0, 2))
-            inv_rms = lax.rsqrt(squares / full_width + norm_epsilon).reshape(group, part, 1)
-            correct = jnp.square(inv_rms) / full_width
+            dense[place] = expand(line_codes[place], weights, place, shards)
         if step == 0:
-            above, above_at, above_own = jnp.zeros_like(gathered[:, :, :width]), 0, inputs[0]
-            scale, rms = jnp.zeros((part, 1), f32), first_rms
+            (above, above_at), above_own = found[first], inputs[first]
+            scale = jnp.zeros((part, 1), f32)
         elif place == first:
             notes = jnp.concatenate(
                 [sent[:, width:width + 2].astype(f32), correct[0]], axis=1
@@ -296,23 +286,22 @@
             sent = jnp.concatenate([own, tail], axis=1).astype(bf16)
             scale = passed[:, width + 2:width + 3]
             above, above_at, above_own = upper, 0, passed[:, width + lanes:]
-            rms = inv_rms[place]
         else:
-            above, above_at = all_inputs, place + 1
-            above_own, scale, rms = inputs[place + 1], correct[place + 1], inv_rms[place]
-        if step > 1:
+            (above, above_at), above_own = found[place + 1], inputs[place + 1]
+            scale = correct[place + 1]
+        if step > 0:
             gathered = lax.all_gather(sent, "tp")
+        if step == 2:
+            gathered, rest_inputs = lax.optimization_barrier((gathered, rest_inputs))
+            found[1], found[0] = (rest_inputs, 1), (rest_inputs, 0)
+            upper = lax.ppermute(rest_inputs[:, :part], "pipe", down)
         if step == 3:
             gathered, upper = lax.optimization_barrier((gathered, upper))
         full, sent, own = layer(
             gathered, own, above, above_at, above_own, scale, dense[place],
-            inputs[place], rms, gain_rows[place][None],
+            inputs[place], inv_rms[place], gain_rows[place][None],
         )
-        if step == 0:
-            later_blocks, sent = lax.optimization_barrier((blocks, sent))
-            late = spread(later_blocks, (1, 0))
-        if step == 1:
-            upper = lax.ppermute(all_inputs[:, :part], "pipe", down)
+        full = lax.dynamic_slice_in_dim(full, (shard % 2) * half, half, 0)
         if phase == 0:
             kept[place] = full
         else:
@@ -321,16 +310,11 @@
     rms_parts = jnp.concatenate(in_parts(inv_rms), axis=2)
     rms_parts = jnp.pad(rms_parts, ((0, 0), (0, 0), (0, width - 3)))
     leaving = jnp.concatenate([jnp.stack(kept), rms_parts[:, None]], axis=1)
+    came = lax.all_to_all(leaving, "pipe", 0, 0, axis_index_groups=together)
+    other = lax.ppermute(came, "tp", [(i, i ^ 1) for i in range(shards)])
     native = x_saved[0].reshape(group, part, width)
-    came, order = [], []
-    for distance in range(group):
-        other = block ^ distance
-        piece = lax.dynamic_index_in_dim(leaving, other, 0, keepdims=False)
-        if distance:
-            piece = lax.ppermute(piece, "pipe", partners(distance, range(group)))
-        came.append(piece)
-        order.append(lax.dynamic_index_in_dim(native, other, 0, keepdims=False))
-    w_grads, gain_sums = slot_grads(codes, came, jnp.stack(order), gains, blocks)
+    codes = jnp.concatenate([codes, (shard % 2).astype(jnp.int32)[None]])
+    w_grads, gain_sums = slot_grads(codes, came, other, native, gains, blocks)
     return (w_grads[None], gain_sums.reshape(1, width) / gains)
 
 

time: 766 us -> 703 us (0.918)
  waiting for transfers between devices: 91.1 us -> 21.7 us
  blocking collectives: 535 us -> 569 us
  starting transfers between devices: 26.2 us -> 13.5 us
    ppermute x10 -> x2, waiting for transfers between devices: 77.9 us -> 2.27 us  [the longest x1 2.27 us: per_device(): other = lax.ppermute(came, 'tp', [(i, i ^ 1) for i in range(shards)])]
    all_gather x0 -> x2, blocking collectives: none -> 69.4 us  [the longest x1 39.6 us: per_device(): second_inputs = lax.all_gather(inputs[first], 'tp')]
    all_gather x16, blocking collectives: 526 us -> 480 us  [per_device(): gathered = lax.all_gather(sent, 'tp')]
    ppermute x10 -> x2, starting transfers between devices: 22.3 us -> 4.76 us  [the longest x1 3.48 us: per_device(): other = lax.ppermute(came, 'tp', [(i, i ^ 1) for i in range(shards)])]
    all_to_all x1, blocking collectives: 9.28 us -> 18.8 us  [per_device(): came = lax.all_to_all(leaving, 'pipe', 0, 0, axis_index_groups=together)]
    unnamed x116 -> x128, local copies, waits for them, and re-layouts: 16 us -> 18.6 us
  transfers between devices with their start and end apart: 14 -> 8, of which waited for: 7 -> 5; matrix products, arithmetic and copies ran while one was open for 2% -> 1% of each run, Pallas kernels for 3% -> 3%
where the time goes in v3:
time: 703 us; the launch traced here: 702 us
  blocking collectives  569 us (81%)
  Pallas kernels  52.8 us (8%)
  local copies, waits for them, and re-layouts  25 us (4%)
  waiting for transfers between devices  21.7 us (3%)
  between operations  14.9 us (2%)
  starting transfers between devices  13.5 us (2%)
    all_gather x16, blocking collectives, per_device(): gathered = lax.all_gather(sent, 'tp')  480 us
    all_gather x1, blocking collectives, per_device(): second_inputs = lax.all_gather(inputs[first], 'tp')  39.6 us
    pallas_call x16, Pallas kernels, layer(): pl.pallas_call(layer_body, grid=(shards // chunk,), out_shape=(jax.ShapeD...  34.7 us
    all_gather x1, blocking collectives, per_device(): third_inputs = lax.all_gather(third, 'tp')  29.8 us
    all_to_all x1, blocking collectives, per_device(): came = lax.all_to_all(leaving, 'pipe', 0, 0, axis_index_groups=together)  18.8 us
    unnamed x128, local copies, waits for them, and re-layouts  18.6 us
    ppermute x3, waiting for transfers between devices, per_device(): passed = lax.ppermute(passed, 'pipe', down)  14.3 us
  transfers between devices with their start and end apart: 8, of which 5 were waited for; matrix products, arithmetic and copies ran while one was open for 1% of the time, Pallas kernels for 3%

profile of v3, /device:TPU:1, one launch (start us, length us, event | category | flops | bytes accessed | tf_op | source)
XLA Modules:
  0.0 702.1 jit_solution(7429290081968546008)
XLA Ops:
  9.3 4.8 all-to-all-start
  14.4 4.5 all-to-all-done
  19.8 39.6 %all_gather.105.above = bf16[32,32,256]{2,1,0:T(8,128)(2,1)S(1)} all-gather(bf16[1,32,256]{2,1,0:T(8,128)(2,1)S(1)} %get-tuple-element.144), channel_id=1, replica_groups=mesh['pipe'=16,'tp'=32] {'tp'}, dimensions={0}, use_global_device_ids=true | all-gather | bytes 540672 | tf_op jit(solution)/shard_map/all_gather | solution.py:244
  59.3 29.2 %all-gather = bf16[1024,384]{1,0:T(8,128)(2,1)S(1)} all-gather(bf16[32,384]{1,0:T(8,128)(2,1)S(1)} %pad_maximum_fusion.5), channel_id=2, replica_groups=mesh['pipe'=16,'tp'=32] {'tp'}, dimensions={0}, use_global_device_ids=true | all-gather | bytes 811008 | tf_op jit(solution)/shard_map/all_gather | solution.py:254
  89.9 29.8 %all-gather.1 = bf16[1024,256]{1,0:T(8,128)(2,1)S(1)} all-gather(bf16[32,256]{1,0:T(8,128)(2,1)S(1)} %get-tuple-element.77.here.above_own), channel_id=3, replica_groups=mesh['pipe'=16,'tp'=32] {'tp'}, dimensions={0}, use_global_device_ids=true | all-gather | bytes 540672 | tf_op jit(solution)/shard_map/all_gather | solution.py:261
  134.0 29.4 %all-gather.2 = bf16[1024,384]{1,0:T(8,128)(2,1)S(1)} all-gather(bf16[32,384]{1,0:T(8,128)(2,1)S(1)} %get-tuple-element.80), channel_id=4, replica_groups=mesh['pipe'=16,'tp'=32] {'tp'}, dimensions={0}, use_global_device_ids=true | all-gather | bytes 811008 | tf_op jit(solution)/shard_map/all_gather | solution.py:293
  166.9 30.8 %all-gather.3 = bf16[1024,384]{1,0:T(8,128)(2,1)S(1)} all-gather(bf16[32,384]{1,0:T(8,128)(2,1)S(1)} %get-tuple-element.82), channel_id=5, replica_groups=mesh['pipe'=16,'tp'=32] {'tp'}, dimensions={0}, use_global_device_ids=true | all-gather | bytes 811008 | tf_op jit(solution)/shard_map/all_gather | solution.py:293
  214.5 30.1 %all-gather.4 = bf16[1024,384]{1,0:T(8,128)(2,1)S(1)} all-gather(bf16[32,384]{1,0:T(8,128)(2,1)S(1)} %get-tuple-element.87), channel_id=6, replica_groups=mesh['pipe'=16,'tp'=32] {'tp'}, dimensions={0}, use_global_device_ids=true | all-gather | bytes 811008 | tf_op jit(solution)/shard_map/all_gather | solution.py:293
  249.0 5.9 collective-permute-done.1
  254.9 30.3 %all_gather.118.gathered.tails = bf16[32,32,384]{2,1,0:T(8,128)(2,1)S(1)} all-gather(bf16[1,32,384]{2,1,0:T(8,128)(2,1)S(1)} %pad_maximum_fusion.6), channel_id=1, replica_groups=mesh['pipe'=16,'tp'=32] {'tp'}, dimensions={0}, use_global_device_ids=true | all-gather | bytes 811008 | tf_op jit(solution)/shard_map/all_gather | solution.py:293
  289.6 30.1 %all-gather.5 = bf16[1024,384]{1,0:T(8,128)(2,1)S(1)} all-gather(bf16[32,384]{1,0:T(8,128)(2,1)S(1)} %get-tuple-element.94), channel_id=7, replica_groups=mesh['pipe'=16,'tp'=32] {'tp'}, dimensions={0}, use_global_device_ids=true | all-gather | bytes 811008 | tf_op jit(solution)/shard_map/all_gather | solution.py:293
  321.8 29.7 %all-gather.6 = bf16[1024,384]{1,0:T(8,128)(2,1)S(1)} all-gather(bf16[32,384]{1,0:T(8,128)(2,1)S(1)} %get-tuple-element.96), channel_id=8, replica_groups=mesh['pipe'=16,'tp'=32] {'tp'}, dimensions={0}, use_global_device_ids=true | all-gather | bytes 811008 | tf_op jit(solution)/shard_map/all_gather | solution.py:293
  354.6 30.0 %all-gather.7 = bf16[1024,384]{1,0:T(8,128)(2,1)S(1)} all-gather(bf16[32,384]{1,0:T(8,128)(2,1)S(1)} %get-tuple-element.98), channel_id=9, replica_groups=mesh['pipe'=16,'tp'=32] {'tp'}, dimensions={0}, use_global_device_ids=true | all-gather | bytes 811008 | tf_op jit(solution)/shard_map/all_gather | solution.py:293
  394.4 30.5 %all_gather.125.gathered.tails = bf16[32,32,384]{2,1,0:T(8,128)(2,1)S(1)} all-gather(bf16[1,32,384]{2,1,0:T(8,128)(2,1)S(1)} %pad_maximum_fusion.7), channel_id=1, replica_groups=mesh['pipe'=16,'tp'=32] {'tp'}, dimensions={0}, use_global_device_ids=true | all-gather | bytes 811008 | tf_op jit(solution)/shard_map/all_gather | solution.py:293
  429.3 30.1 %all-gather.8 = bf16[1024,384]{1,0:T(8,128)(2,1)S(1)} all-gather(bf16[32,384]{1,0:T(8,128)(2,1)S(1)} %get-tuple-element.102), channel_id=10, replica_groups=mesh['pipe'=16,'tp'=32] {'tp'}, dimensions={0}, use_global_device_ids=true | all-gather | bytes 811008 | tf_op jit(solution)/shard_map/all_gather | solution.py:293
  461.4 29.7 %all-gather.9 = bf16[1024,384]{1,0:T(8,128)(2,1)S(1)} all-gather(bf16[32,384]{1,0:T(8,128)(2,1)S(1)} %get-tuple-element.104), channel_id=11, replica_groups=mesh['pipe'=16,'tp'=32] {'tp'}, dimensions={0}, use_global_device_ids=true | all-gather | bytes 811008 | tf_op jit(solution)/shard_map/all_gather | solution.py:293
  493.3 30.2 %all-gather.10 = bf16[1024,384]{1,0:T(8,128)(2,1)S(1)} all-gather(bf16[32,384]{1,0:T(8,128)(2,1)S(1)} %get-tuple-element.106), channel_id=12, replica_groups=mesh['pipe'=16,'tp'=32] {'tp'}, dimensions={0}, use_global_device_ids=true | all-gather | bytes 811008 | tf_op jit(solution)/shard_map/all_gather | solution.py:293
  527.1 4.5 collective-permute-done.3
  531.6 30.5 %all_gather.132.gathered.tails = bf16[32,32,384]{2,1,0:T(8,128)(2,1)S(1)} all-gather(bf16[1,32,384]{2,1,0:T(8,128)(2,1)S(1)} %pad_maximum_fusion.8), channel_id=1, replica_groups=mesh['pipe'=16,'tp'=32] {'tp'}, dimensions={0}, use_global_device_ids=true | all-gather | bytes 811008 | tf_op jit(solution)/shard_map/all_gather | solution.py:293
  564.4 30.1 %all-gather.11 = bf16[1024,384]{1,0:T(8,128)(2,1)S(1)} all-gather(bf16[32,384]{1,0:T(8,128)(2,1)S(1)} %get-tuple-element.110), channel_id=13, replica_groups=mesh['pipe'=16,'tp'=32] {'tp'}, dimensions={0}, use_global_device_ids=true | all-gather | bytes 811008 | tf_op jit(solution)/shard_map/all_gather | solution.py:293
  596.5 29.7 %all-gather.12 = bf16[1024,384]{1,0:T(8,128)(2,1)S(1)} all-gather(bf16[32,384]{1,0:T(8,128)(2,1)S(1)} %get-tuple-element.112), channel_id=14, replica_groups=mesh['pipe'=16,'tp'=32] {'tp'}, dimensions={0}, use_global_device_ids=true | all-gather | bytes 811008 | tf_op jit(solution)/shard_map/all_gather | solution.py:293
  628.3 30.1 %all-gather.13 = bf16[1024,384]{1,0:T(8,128)(2,1)S(1)} all-gather(bf16[32,384]{1,0:T(8,128)(2,1)S(1)} %get-tuple-element.114), channel_id=15, replica_groups=mesh['pipe'=16,'tp'=32] {'tp'}, dimensions={0}, use_global_device_ids=true | all-gather | bytes 811008 | tf_op jit(solution)/shard_map/all_gather | solution.py:293
  663.8 18.8 %all_to_all.10.mine = bf16[4,17,32,256]{3,2,1,0:T(8,128)(2,1)S(1)} all-to-all(bf16[4,17,32,256]{3,2,1,0:T(8,128)(2,1)S(1)} %pad_maximum_fusion), channel_id=1, replica_groups={{0,32,64,96},{128,160,192,224},{256,288,320,352},{384,416,448,480},{1,3..., dimensions={0} | all-to-all | bytes 2228224 | tf_op jit(solution)/shard_map/all_to_all | solution.py:313
  688.5 6.1 slot_grads.1
  (241 shorter events, 92.8 us)
Async XLA Ops:
  7.2 112.5 %all-gather.17.cloned.1.call-start = ((), (), s32[]{:S(2)}) async-start(), calls=%async_computation.2 | async-start | bytes 11796480 | tf_op jit(solution)/shard_map/all_gather | solution.py:243
  9.3 9.5 %all-to-all-start = ((bf16[4,48,256]{2,1,0:T(8,128)(2,1)}), bf16[4,48,256]{2,1,0:T(8,128)(2,1)S(1)}, u32[]{:S(2)}, u32[]{:S(2)}) async-start(bf16[4,48,256]{2,1,0:T(8,128)(2,1)} %pad_maximum_fusion.4), calls=%async_computation | async-start | bytes 196608 | tf_op jit(solution)/shard_map/all_to_all | solution.py:237
  14.2 183.5 %all-gather.19.cloned.1.call-start = ((), (), s32[]{:S(2)}) async-start(), calls=%async_computation.3 | async-start | bytes 1081344 | tf_op jit(solution)/shard_map/all_gather | solution.py:264
  120.7 42.7 %copy-start.46 = (f32[1,256]{1,0:T(1,128)}, f32[1,256]{1,0:T(1,128)S(1)}, u32[]{:S(2)}) copy-start(f32[1,256]{1,0:T(1,128)S(1)} %get-tuple-element.157.gain) | copy-start | bytes 3076
  127.3 36.1 %copy-start.3 = (bf16[32,256,256]{2,1,0:T(8,128)(2,1)}, bf16[32,256,256]{2,1,0:T(8,128)(2,1)S(1)}, u32[]{:S(2)}) copy-start(bf16[32,256,256]{2,1,0:T(8,128)(2,1)S(1)} %expand.5.weight) | copy-start | bytes 12582916
  199.5 45.1 %collective-permute-start = (bf16[32,32,256]{2,1,0:T(8,128)(2,1)}, bf16[32,32,256]{2,1,0:T(8,128)(2,1)S(1)}, u32[]{:S(2)}, u32[]{:S(2)}) collective-permute-start(bf16[32,32,256]{2,1,0:T(8,128)(2,1)} %slice.250), channel_id=1, source_target_pairs={{128,0},{160,32},{192,64},{224,96},{256,128},{288,160},{320,192},{... | collective-permute-start | bytes 1572872 | tf_op jit(solution)/shard_map/ppermute | solution.py:297
  209.2 35.4 %copy-start.6 = (bf16[32,256,256]{2,1,0:T(8,128)(2,1)}, bf16[32,256,256]{2,1,0:T(8,128)(2,1)S(1)}, u32[]{:S(2)}) copy-start(bf16[32,256,256]{2,1,0:T(8,128)(2,1)S(1)} %expand.7.weight) | copy-start | bytes 12582916
  212.4 32.3 %copy-start.16 = (bf16[32,64,256]{2,1,0:T(8,128)(2,1)S(1)}, bf16[32,64,256]{2,1,0:T(8,128)(2,1)}, u32[]{:S(2)}) copy-start(bf16[32,64,256]{2,1,0:T(8,128)(2,1)} %all-gather.19.cloned.1.call-done.above) | copy-start | bytes 3145732
  212.4 32.3 %copy-start.20 = (bf16[32,256]{1,0:T(8,128)(2,1)S(1)}, bf16[32,256]{1,0:T(8,128)(2,1)}, u32[]{:S(2)}) copy-start(bf16[32,256]{1,0:T(8,128)(2,1)} %get-tuple-element.140.here) | copy-start | bytes 49156
  212.4 32.3 %copy-start.40 = (f32[1,256]{1,0:T(1,128)S(1)}, f32[1,256]{1,0:T(1,128)}, u32[]{:S(2)}) copy-start(f32[1,256]{1,0:T(1,128)} %get-tuple-element.155.gain) | copy-start | bytes 3076
  246.9 38.4 %copy-start.50 = (f32[1,256]{1,0:T(1,128)S(1)}, f32[1,256]{1,0:T(1,128)}, u32[]{:S(2)}) copy-start(f32[1,256]{1,0:T(1,128)} %copy-done.49) | copy-start | bytes 3076
  247.6 7.2 %collective-permute-start.1 = (f32[32,640]{1,0:T(8,128)}, f32[32,640]{1,0:T(8,128)S(1)}, u32[]{:S(2)}, u32[]{:S(2)}) collective-permute-start(f32[32,640]{1,0:T(8,128)} %pad_maximum_fusion.3), channel_id=1, source_target_pairs={{128,0},{160,32},{192,64},{224,96},{256,128},{288,160},{320,192},{... | collective-permute-start | bytes 245768 | tf_op jit(solution)/shard_map/ppermute | solution.py:283
  287.5 32.2 %copy-start.4 = (bf16[32,256,256]{2,1,0:T(8,128)(2,1)S(1)}, bf16[32,256,256]{2,1,0:T(8,128)(2,1)}, u32[]{:S(2)}) copy-start(bf16[32,256,256]{2,1,0:T(8,128)(2,1)} %copy-done.3) | copy-start | bytes 12582916
  287.5 32.2 %copy-start.47 = (f32[1,256]{1,0:T(1,128)S(1)}, f32[1,256]{1,0:T(1,128)}, u32[]{:S(2)}) copy-start(f32[1,256]{1,0:T(1,128)} %copy-done.46) | copy-start | bytes 3076
  351.6 33.0 %copy-start.7 = (bf16[32,256,256]{2,1,0:T(8,128)(2,1)S(1)}, bf16[32,256,256]{2,1,0:T(8,128)(2,1)}, u32[]{:S(2)}) copy-start(bf16[32,256,256]{2,1,0:T(8,128)(2,1)} %copy-done.6) | copy-start | bytes 12582916
  351.6 33.0 %copy-start.21 = (bf16[32,256]{1,0:T(8,128)(2,1)S(1)}, bf16[32,256]{1,0:T(8,128)(2,1)}, u32[]{:S(2)}) copy-start(bf16[32,256]{1,0:T(8,128)(2,1)} %get-tuple-element.140.here) | copy-start | bytes 49156
  351.6 33.0 %copy-start.41 = (f32[1,256]{1,0:T(1,128)S(1)}, f32[1,256]{1,0:T(1,128)}, u32[]{:S(2)}) copy-start(f32[1,256]{1,0:T(1,128)} %get-tuple-element.155.gain) | copy-start | bytes 3076
  388.4 6.0 collective-permute-start.2
  491.2 32.3 %copy-start.8 = (bf16[32,256,256]{2,1,0:T(8,128)(2,1)S(1)}, bf16[32,256,256]{2,1,0:T(8,128)(2,1)}, u32[]{:S(2)}) copy-start(bf16[32,256,256]{2,1,0:T(8,128)(2,1)} %copy-done.6) | copy-start | bytes 12582916
  523.5 38.7 %copy-start.12 = (bf16[32,256,256]{2,1,0:T(8,128)(2,1)S(1)}, bf16[32,256,256]{2,1,0:T(8,128)(2,1)}, u32[]{:S(2)}) copy-start(bf16[32,256,256]{2,1,0:T(8,128)(2,1)} %copy-done.9) | copy-start | bytes 12582916
  525.8 5.8 collective-permute-start.3
  562.2 32.2 %copy-start.48 = (f32[1,256]{1,0:T(1,128)S(1)}, f32[1,256]{1,0:T(1,128)}, u32[]{:S(2)}) copy-start(f32[1,256]{1,0:T(1,128)} %copy-done.46) | copy-start | bytes 3076
  626.2 32.2 %copy-start.42 = (f32[1,256]{1,0:T(1,128)S(1)}, f32[1,256]{1,0:T(1,128)}, u32[]{:S(2)}) copy-start(f32[1,256]{1,0:T(1,128)} %get-tuple-element.155.gain) | copy-start | bytes 3076
  682.6 5.8 collective-permute-start.4
  (48 other events, 474.8 us)
Sparse Core Ops, SparseCore 0:
  10.2 104.9 all-gather.16
  119.9 69.6 all-gather.18

commit v4 on v3

--- a/solution.py
+++ b/solution.py
@@ -47,7 +47,7 @@
     return pl.pallas_call(
         functools.partial(expand_body, place=place, col_blocks=2 * shards),
         out_shape=jax.ShapeDtypeStruct((shards, width, width), bf16),
-        in_specs=[pl.BlockSpec(memory_space=pltpu.SMEM), pl.BlockSpec(memory_space=pl.ANY)],
+        in_specs=[pl.BlockSpec(memory_space=pltpu.SMEM), pl.BlockSpec(memory_space=pltpu.HBM)],
         out_specs=pl.BlockSpec(memory_space=pltpu.VMEM),
         scratch_shapes=[pltpu.VMEM(weights.shape[1:], bf16), pltpu.SemaphoreType.DMA],
         compiler_params=params(24),
@@ -56,80 +56,85 @@
 
 
 def layer_body(
-    gathered, tails, own, above, above_own, above_scale, weight, here, inv_rms, gain,
-    full_out, sent_out, own_out, total, shift,
+    flags, gathered, own, above, above_own, above_scale, weight, here, inv_rms, gain, *rest,
+    above_at, told, tell, phase,
 ):
-    step, last = pl.program_id(0), pl.num_programs(0) - 1
-    width = weight.shape[1]
-
-    @pl.when(step == 0)
-    def _():
-        dots = jnp.sum(jnp.sum(tails[...].astype(f32), axis=0), axis=1, keepdims=True)
-        shift[...] = jnp.broadcast_to(above_scale[...] * dots, shift.shape)
-        total[...] = jnp.zeros_like(total)
-
-    factor = shift[:, :1]
-    acc = total[...]
-    for i in range(gathered.shape[0]):
-        piece = gathered[i, :, :width].astype(f32) - factor * above[i].astype(f32)
+    rest = list(rest)
+    before = None if told else rest.pop(0)
+    kept = rest.pop(0) if phase else None
+    full_out, sent_out, own_out, kept_out = rest
+    shards, width = weight.shape[0], weight.shape[1]
+    tokens = own.shape[0]
+    rows = slice(above_at * tokens, (above_at + 1) * tokens)
+
+    if told:
+        total = gathered[0, :, width:].astype(f32)
+        for i in range(1, shards):
+            total += gathered[i, :, width:].astype(f32)
+    else:
+        total = jnp.zeros((tokens, width), f32)
+        for i in range(shards):
+            change = gathered[i].astype(f32) - before[i].astype(f32)
+            total += change * above[i, rows, :].astype(f32)
+    factor = above_scale[...] * jnp.sum(total, axis=1, keepdims=True)
+
+    acc = jnp.zeros((tokens, width), f32)
+    for i in range(shards):
+        piece = gathered[i, :, :width].astype(f32) - factor * above[i, rows, :].astype(f32)
         piece = piece.astype(bf16)
         full_out[i] = piece
         acc += lax.dot_general(piece, weight[i], across_last, preferred_element_type=f32)
-    total[...] = acc
-
-    @pl.when(step == last)
-    def _():
-        grad = own[...] - factor * above_own[...].astype(f32)
-        scaled = gain[...] * acc
-        rms = inv_rms[...]
+
+    grad = own[...] - factor * above_own[...].astype(f32)
+    scaled = gain[...] * acc
+    rms = inv_rms[...]
+    result = grad + rms * scaled
+    own_out[...] = result
+    sent_out[:, :width] = result.astype(bf16)
+    if tell:
         dots = jnp.sum(scaled * (here[...].astype(f32) * rms), axis=1, keepdims=True)
-        result = grad + rms * scaled
-        own_out[...] = result
-        sent_out[:, :width] = result.astype(bf16)
         high = dots.astype(bf16).astype(f32)
         low = (dots - high).astype(bf16).astype(f32)
-        lane = lax.broadcasted_iota(jnp.int32, (dots.shape[0], lanes), 1)
+        lane = lax.broadcasted_iota(jnp.int32, (tokens, lanes), 1)
         tail = jnp.where(lane == 0, high, jnp.where(lane == 1, low, 0.0))
         sent_out[:, width:] = tail.astype(bf16)
 
-
-def layer(gathered, own, above, above_at, above_own, above_scale, weight, here, inv_rms, gain):
-    shards, tokens, wide = gathered.shape
-    width = wide - lanes
-    chunk = min(8, shards)
-
-    def whole(*shape):
-        return pl.BlockSpec(shape, lambda c: (0,) * len(shape))
-
+    half = shards // 2
+    mine = pl.ds(flags[0] * half, half)
+    if phase:
+
+        @pl.when(flags[phase] == 1)
+        def _():
+            kept_out[...] = full_out[mine]
+
+        @pl.when(flags[phase] == 0)
+        def _():
+            kept_out[...] = kept[...]
+    else:
+        kept_out[...] = full_out[mine]
+
+
+def layer(flags, operands, before, kept, above_at, tell, phase):
+    weight, own = operands[5], operands[1]
+    shards, width, tokens = weight.shape[0], weight.shape[1], own.shape[0]
+    extra = [] if before is None else [before]
+    extra += [] if kept is None else [kept]
+    vmem = pl.BlockSpec(memory_space=pltpu.VMEM)
     return pl.pallas_call(
-        layer_body,
-        grid=(shards // chunk,),
+        functools.partial(
+            layer_body, above_at=above_at, told=before is None, tell=tell, phase=phase
+        ),
         out_shape=(
             jax.ShapeDtypeStruct((shards, tokens, width), bf16),
-            jax.ShapeDtypeStruct((tokens, wide), bf16),
+            jax.ShapeDtypeStruct((tokens, width + (lanes if tell else 0)), bf16),
             jax.ShapeDtypeStruct((tokens, width), f32),
+            jax.ShapeDtypeStruct((shards // 2, tokens, width), bf16),
         ),
-        in_specs=[
-            pl.BlockSpec((chunk, tokens, wide), lambda c: (c, 0, 0)),
-            pl.BlockSpec((shards, tokens, lanes), lambda c: (0, 0, width // lanes)),
-            whole(tokens, width),
-            pl.BlockSpec((chunk, tokens, width), lambda c: (c, above_at, 0)),
-            whole(tokens, width),
-            whole(tokens, 1),
-            pl.BlockSpec((chunk, width, width), lambda c: (c, 0, 0)),
-            whole(tokens, width),
-            whole(tokens, 1),
-            whole(1, width),
-        ],
-        out_specs=(
-            pl.BlockSpec((chunk, tokens, width), lambda c: (c, 0, 0)),
-            whole(tokens, wide),
-            whole(tokens, width),
-        ),
-        scratch_shapes=[pltpu.VMEM((tokens, width), f32), pltpu.VMEM((tokens, lanes), f32)],
+        in_specs=[pl.BlockSpec(memory_space=pltpu.SMEM)] + [vmem] * (len(operands) + len(extra)),
+        out_specs=(vmem,) * 4,
         compiler_params=params(16),
         name="layer",
-    )(gathered, gathered, own, above, above_own, above_scale, weight, here, inv_rms, gain)
+    )(flags, *operands, *extra)
 
 
 def grads_body(
@@ -240,6 +245,7 @@
     line_codes = told[:, part + 3, :slots].astype(jnp.int32)
 
     first = group - 1
+    upper_own = lax.ppermute(inputs[0], "pipe", down)
     weights = lax.all_gather(blocks, "pipe", axis_index_groups=together)
     second_inputs = lax.all_gather(inputs[first], "tp")
 
@@ -260,17 +266,21 @@
     third, gathered = lax.optimization_barrier((inputs[first - 1], gathered))
     third_inputs = lax.all_gather(third, "tp")
     weights, third_inputs = lax.optimization_barrier((weights, third_inputs))
-    rest, weights = lax.optimization_barrier((inputs[:first - 1], weights))
-    rest_inputs = lax.all_gather(rest.reshape((first - 1) * part, width), "tp")
+    rest = jnp.concatenate([inputs[:first - 1].reshape(-1, width), upper_own])
+    rest, weights = lax.optimization_barrier((rest, weights))
+    rest_inputs = lax.all_gather(rest, "tp")
 
     found = {first: (second_inputs, 0), first - 1: (third_inputs, 0)}
+    flags = [shard % 2] + [line == lines - 1 - phase for phase in range(1, lines)]
+    flags = jnp.stack([flag.astype(jnp.int32) for flag in flags])
     dense = [None] * group
     kept = [None] * group
-    half = shards // 2
+    full = None
     for step in range(sections):
         phase, place = step // group, first - step % group
         if phase == 0:
             dense[place] = expand(line_codes[place], weights, place, shards)
+        before = full
         if step == 0:
             (above, above_at), above_own = found[first], inputs[first]
             scale = jnp.zeros((part, 1), f32)
@@ -279,13 +289,14 @@
                 [sent[:, width:width + 2].astype(f32), correct[0]], axis=1
             )
             notes = jnp.pad(notes, ((0, 0), (0, lanes - 3)))
-            passed = jnp.concatenate([own, notes, inputs[0].astype(f32)], axis=1)
+            passed = jnp.concatenate([own, notes], axis=1)
             passed = lax.ppermute(passed, "pipe", down)
             own = passed[:, :width]
             tail = jnp.pad(passed[:, width:width + 2], ((0, 0), (0, lanes - 2)))
             sent = jnp.concatenate([own, tail], axis=1).astype(bf16)
             scale = passed[:, width + 2:width + 3]
-            above, above_at, above_own = upper, 0, passed[:, width + lanes:]
+            above, above_at, above_own = rest_inputs, 2, upper_own
+            before = None
         else:
             (above, above_at), above_own = found[place + 1], inputs[place + 1]
             scale = correct[place + 1]
@@ -294,18 +305,14 @@
         if step == 2:
             gathered, rest_inputs = lax.optimization_barrier((gathered, rest_inputs))
             found[1], found[0] = (rest_inputs, 1), (rest_inputs, 0)
-            upper = lax.ppermute(rest_inputs[:, :part], "pipe", down)
-        if step == 3:
-            gathered, upper = lax.optimization_barrier((gathered, upper))
-        full, sent, own = layer(
-            gathered, own, above, above_at, above_own, scale, dense[place],
+        operands = (
+            gathered, own, above, above_own, scale, dense[place],
             inputs[place], inv_rms[place], gain_rows[place][None],
         )
-        full = lax.dynamic_slice_in_dim(full, (shard % 2) * half, half, 0)
-        if phase == 0:
-            kept[place] = full
-        else:
-            kept[place] = jnp.where(line == lines - 1 - phase, full, kept[place])
+        tell = place == 0 and step < sections - 1
+        full, sent, own, kept[place] = layer(
+            flags, operands, before, kept[place], above_at, tell, phase
+        )
 
     rms_parts = jnp.concatenate(in_parts(inv_rms), axis=2)
     rms_parts = jnp.pad(rms_parts, ((0, 0), (0, 0), (0, width - 3)))

time: 703 us -> 685 us (0.974)
  blocking collectives: 569 us -> 561 us
  local copies, waits for them, and re-layouts: 25 us -> 17.7 us
    all_gather x16, blocking collectives: 480 us -> 473 us  [per_device(): gathered = lax.all_gather(sent, 'tp')]
    unnamed x128 -> x80, local copies, waits for them, and re-layouts: 18.6 us -> 16.1 us
  transfers between devices with their start and end apart: 8 -> 8, of which waited for: 5 -> 5; matrix products, arithmetic and copies ran while one was open for 1% -> 0% of each run, Pallas kernels for 3% -> 2%
where the time goes in v4:
time: 685 us; the launch traced here: 684 us
  blocking collectives  561 us (82%)
  Pallas kernels  55 us (8%)
  waiting for transfers between devices  18.9 us (3%)
  local copies, waits for them, and re-layouts  17.7 us (3%)
  between operations  14.8 us (2%)
  starting transfers between devices  13.5 us (2%)
    all_gather x16, blocking collectives, per_device(): gathered = lax.all_gather(sent, 'tp')  473 us
    all_gather x1, blocking collectives, per_device(): second_inputs = lax.all_gather(inputs[first], 'tp')  39.6 us
    pallas_call x16, Pallas kernels, layer(): pl.pallas_call(functools.partial(layer_body, above_at=above_at, told=befo...  36.7 us
    all_gather x1, blocking collectives, per_device(): third_inputs = lax.all_gather(third, 'tp')  29.8 us
    all_to_all x1, blocking collectives, per_device(): came = lax.all_to_all(leaving, 'pipe', 0, 0, axis_index_groups=together)  18.5 us
    unnamed x80, local copies, waits for them, and re-layouts  16.1 us
  transfers between devices with their start and end apart: 8, of which 5 were waited for; matrix products, arithmetic and copies ran while one was open for 0% of the time, Pallas kernels for 2%

profile of v4, /device:TPU:1, one launch (start us, length us, event | category | flops | bytes accessed | tf_op | source)
XLA Modules:
  0.0 684.0 jit_solution(12460994263615655783)
XLA Ops:
  8.9 4.8 all-to-all-start
  13.9 4.5 all-to-all-done
  20.0 39.6 %all_gather.108.above = bf16[32,32,256]{2,1,0:T(8,128)(2,1)S(1)} all-gather(bf16[1,32,256]{2,1,0:T(8,128)(2,1)S(1)} %get-tuple-element.163), channel_id=1, replica_groups=mesh['pipe'=16,'tp'=32] {'tp'}, dimensions={0}, use_global_device_ids=true | all-gather | bytes 540672 | tf_op jit(solution)/shard_map/all_gather | solution.py:250
  59.6 29.2 %all-gather = bf16[1024,384]{1,0:T(8,128)(2,1)S(1)} all-gather(bf16[32,384]{1,0:T(8,128)(2,1)S(1)} %pad_maximum_fusion.3), channel_id=2, replica_groups=mesh['pipe'=16,'tp'=32] {'tp'}, dimensions={0}, use_global_device_ids=true | all-gather | bytes 811008 | tf_op jit(solution)/shard_map/all_gather | solution.py:260
  88.8 29.8 %all-gather.1 = bf16[1024,256]{1,0:T(8,128)(2,1)S(1)} all-gather(bf16[32,256]{1,0:T(8,128)(2,1)S(1)} %get-tuple-element.87.here.above_own), channel_id=3, replica_groups=mesh['pipe'=16,'tp'=32] {'tp'}, dimensions={0}, use_global_device_ids=true | all-gather | bytes 540672 | tf_op jit(solution)/shard_map/all_gather | solution.py:267
  120.4 3.7 copy-done
  142.4 29.5 %all-gather.2 = bf16[1024,256]{1,0:T(8,128)(2,1)S(1)} all-gather(bf16[32,256]{1,0:T(8,128)(2,1)S(1)} %get-tuple-element.90), channel_id=4, replica_groups=mesh['pipe'=16,'tp'=32] {'tp'}, dimensions={0}, use_global_device_ids=true | all-gather | bytes 540672 | tf_op jit(solution)/shard_map/all_gather | solution.py:304
  175.6 29.3 %all-gather.3 = bf16[1024,256]{1,0:T(8,128)(2,1)S(1)} all-gather(bf16[32,256]{1,0:T(8,128)(2,1)S(1)} %get-tuple-element.93), channel_id=5, replica_groups=mesh['pipe'=16,'tp'=32] {'tp'}, dimensions={0}, use_global_device_ids=true | all-gather | bytes 540672 | tf_op jit(solution)/shard_map/all_gather | solution.py:304
  210.3 30.0 %all-gather.5 = bf16[1024,256]{1,0:T(8,128)(2,1)S(1)} all-gather(bf16[32,256]{1,0:T(8,128)(2,1)S(1)} %get-tuple-element.99), channel_id=7, replica_groups=mesh['pipe'=16,'tp'=32] {'tp'}, dimensions={0}, use_global_device_ids=true | all-gather | bytes 540672 | tf_op jit(solution)/shard_map/all_gather | solution.py:304
  243.9 4.3 collective-permute-done.1
  248.3 30.3 %all_gather.122.gathered = bf16[32,32,384]{2,1,0:T(8,128)(2,1)S(1)} all-gather(bf16[1,32,384]{2,1,0:T(8,128)(2,1)S(1)} %pad_maximum_fusion.4), channel_id=1, replica_groups=mesh['pipe'=16,'tp'=32] {'tp'}, dimensions={0}, use_global_device_ids=true | all-gather | bytes 811008 | tf_op jit(solution)/shard_map/all_gather | solution.py:304
  280.9 29.3 %all-gather.6 = bf16[1024,256]{1,0:T(8,128)(2,1)S(1)} all-gather(bf16[32,256]{1,0:T(8,128)(2,1)S(1)} %get-tuple-element.106), channel_id=8, replica_groups=mesh['pipe'=16,'tp'=32] {'tp'}, dimensions={0}, use_global_device_ids=true | all-gather | bytes 540672 | tf_op jit(solution)/shard_map/all_gather | solution.py:304
  312.4 29.2 %all-gather.7 = bf16[1024,256]{1,0:T(8,128)(2,1)S(1)} all-gather(bf16[32,256]{1,0:T(8,128)(2,1)S(1)} %get-tuple-element.110), channel_id=9, replica_groups=mesh['pipe'=16,'tp'=32] {'tp'}, dimensions={0}, use_global_device_ids=true | all-gather | bytes 540672 | tf_op jit(solution)/shard_map/all_gather | solution.py:304
  344.5 29.3 %all-gather.8 = bf16[1024,256]{1,0:T(8,128)(2,1)S(1)} all-gather(bf16[32,256]{1,0:T(8,128)(2,1)S(1)} %get-tuple-element.114), channel_id=10, replica_groups=mesh['pipe'=16,'tp'=32] {'tp'}, dimensions={0}, use_global_device_ids=true | all-gather | bytes 540672 | tf_op jit(solution)/shard_map/all_gather | solution.py:304
  382.5 30.8 %all_gather.129.gathered = bf16[32,32,384]{2,1,0:T(8,128)(2,1)S(1)} all-gather(bf16[1,32,384]{2,1,0:T(8,128)(2,1)S(1)} %pad_maximum_fusion.5), channel_id=1, replica_groups=mesh['pipe'=16,'tp'=32] {'tp'}, dimensions={0}, use_global_device_ids=true | all-gather | bytes 811008 | tf_op jit(solution)/shard_map/all_gather | solution.py:304
  417.7 29.3 %all-gather.9 = bf16[1024,256]{1,0:T(8,128)(2,1)S(1)} all-gather(bf16[32,256]{1,0:T(8,128)(2,1)S(1)} %get-tuple-element.121), channel_id=11, replica_groups=mesh['pipe'=16,'tp'=32] {'tp'}, dimensions={0}, use_global_device_ids=true | all-gather | bytes 540672 | tf_op jit(solution)/shard_map/all_gather | solution.py:304
  449.2 29.0 %all-gather.10 = bf16[1024,256]{1,0:T(8,128)(2,1)S(1)} all-gather(bf16[32,256]{1,0:T(8,128)(2,1)S(1)} %get-tuple-element.125), channel_id=12, replica_groups=mesh['pipe'=16,'tp'=32] {'tp'}, dimensions={0}, use_global_device_ids=true | all-gather | bytes 540672 | tf_op jit(solution)/shard_map/all_gather | solution.py:304
  480.4 29.3 %all-gather.11 = bf16[1024,256]{1,0:T(8,128)(2,1)S(1)} all-gather(bf16[32,256]{1,0:T(8,128)(2,1)S(1)} %get-tuple-element.129), channel_id=13, replica_groups=mesh['pipe'=16,'tp'=32] {'tp'}, dimensions={0}, use_global_device_ids=true | all-gather | bytes 540672 | tf_op jit(solution)/shard_map/all_gather | solution.py:304
  517.8 30.8 %all_gather.136.gathered = bf16[32,32,384]{2,1,0:T(8,128)(2,1)S(1)} all-gather(bf16[1,32,384]{2,1,0:T(8,128)(2,1)S(1)} %pad_maximum_fusion.6), channel_id=1, replica_groups=mesh['pipe'=16,'tp'=32] {'tp'}, dimensions={0}, use_global_device_ids=true | all-gather | bytes 811008 | tf_op jit(solution)/shard_map/all_gather | solution.py:304
  550.8 29.3 %all-gather.12 = bf16[1024,256]{1,0:T(8,128)(2,1)S(1)} all-gather(bf16[32,256]{1,0:T(8,128)(2,1)S(1)} %get-tuple-element.136), channel_id=14, replica_groups=mesh['pipe'=16,'tp'=32] {'tp'}, dimensions={0}, use_global_device_ids=true | all-gather | bytes 540672 | tf_op jit(solution)/shard_map/all_gather | solution.py:304
  582.3 29.0 %all-gather.13 = bf16[1024,256]{1,0:T(8,128)(2,1)S(1)} all-gather(bf16[32,256]{1,0:T(8,128)(2,1)S(1)} %get-tuple-element.140), channel_id=15, replica_groups=mesh['pipe'=16,'tp'=32] {'tp'}, dimensions={0}, use_global_device_ids=true | all-gather | bytes 540672 | tf_op jit(solution)/shard_map/all_gather | solution.py:304
  613.5 29.3 %all-gather.14 = bf16[1024,256]{1,0:T(8,128)(2,1)S(1)} all-gather(bf16[32,256]{1,0:T(8,128)(2,1)S(1)} %get-tuple-element.144), channel_id=16, replica_groups=mesh['pipe'=16,'tp'=32] {'tp'}, dimensions={0}, use_global_device_ids=true | all-gather | bytes 540672 | tf_op jit(solution)/shard_map/all_gather | solution.py:304
  645.9 18.5 %all_to_all.10.mine = bf16[4,17,32,256]{3,2,1,0:T(8,128)(2,1)S(1)} all-to-all(bf16[4,17,32,256]{3,2,1,0:T(8,128)(2,1)S(1)} %pad_maximum_fusion), channel_id=1, replica_groups={{0,32,64,96},{128,160,192,224},{256,288,320,352},{384,416,448,480},{1,3..., dimensions={0} | all-to-all | bytes 2228224 | tf_op jit(solution)/shard_map/all_to_all | solution.py:320
  670.3 6.1 slot_grads.1
  (191 shorter events, 84.6 us)
Async XLA Ops:
  7.2 112.0 %all-gather.18.cloned.1.call-start = ((), (), s32[]{:S(2)}) async-start(), calls=%async_computation.2 | async-start | bytes 11796480 | tf_op jit(solution)/shard_map/all_gather | solution.py:249
  8.9 9.5 %all-to-all-start = ((bf16[4,48,256]{2,1,0:T(8,128)(2,1)}), bf16[4,48,256]{2,1,0:T(8,128)(2,1)S(1)}, u32[]{:S(2)}, u32[]{:S(2)}) async-start(bf16[4,48,256]{2,1,0:T(8,128)(2,1)} %pad_maximum_fusion.1), calls=%async_computation | async-start | bytes 196608 | tf_op jit(solution)/shard_map/all_to_all | solution.py:242
  13.7 191.2 %all-gather.20.cloned.1.call-start = ((), (), s32[]{:S(2)}) async-start(), calls=%async_computation.3 | async-start | bytes 1622016 | tf_op jit(solution)/shard_map/all_gather | solution.py:271
  18.6 100.0 %collective-permute-start = (bf16[32,256]{1,0:T(8,128)(2,1)S(1)}, bf16[32,256]{1,0:T(8,128)(2,1)S(1)}, u32[]{:S(2)}, u32[]{:S(2)}) collective-permute-start(bf16[32,256]{1,0:T(8,128)(2,1)S(1)} %get-tuple-element.162.here), channel_id=1, source_target_pairs={{128,0},{160,32},{192,64},{224,96},{256,128},{288,160},{320,192},{... | collective-permute-start | bytes 49160 | tf_op jit(solution)/shard_map/ppermute | solution.py:248
  137.2 34.8 %copy-start.12 = (bf16[32,256,256]{2,1,0:T(8,128)(2,1)}, bf16[32,256,256]{2,1,0:T(8,128)(2,1)S(1)}, u32[]{:S(2)}) copy-start(bf16[32,256,256]{2,1,0:T(8,128)(2,1)S(1)} %expand.5.weight) | copy-start | bytes 12582916
  142.4 31.7 %copy-start.22 = (bf16[16,32,256]{2,1,0:T(8,128)(2,1)}, bf16[16,32,256]{2,1,0:T(8,128)(2,1)S(1)}, u32[]{:S(2)}) copy-start(bf16[16,32,256]{2,1,0:T(8,128)(2,1)S(1)} %get-tuple-element.105.rest_0_) | copy-start | bytes 786436
  208.2 32.1 %copy-start.6 = (bf16[32,256,256]{2,1,0:T(8,128)(2,1)S(1)}, bf16[32,256,256]{2,1,0:T(8,128)(2,1)}, u32[]{:S(2)}) copy-start(bf16[32,256,256]{2,1,0:T(8,128)(2,1)} %copy-done.5) | copy-start | bytes 12582916
  208.2 32.1 %copy-start.15 = (bf16[3072,256]{1,0:T(8,128)(2,1)S(1)}, bf16[3072,256]{1,0:T(8,128)(2,1)}, u32[]{:S(2)}) copy-start(bf16[3072,256]{1,0:T(8,128)(2,1)} %all-gather.20.cloned.1.call-done) | copy-start | bytes 4718596
  240.3 38.4 %copy-start.2 = (bf16[32,256,256]{2,1,0:T(8,128)(2,1)S(1)}, bf16[32,256,256]{2,1,0:T(8,128)(2,1)}, u32[]{:S(2)}) copy-start(bf16[32,256,256]{2,1,0:T(8,128)(2,1)} %copy-done.1) | copy-start | bytes 12582916
  242.5 36.2 %copy-start.23 = (bf16[16,32,256]{2,1,0:T(8,128)(2,1)S(1)}, bf16[16,32,256]{2,1,0:T(8,128)(2,1)}, u32[]{:S(2)}) copy-start(bf16[16,32,256]{2,1,0:T(8,128)(2,1)} %copy-done.22) | copy-start | bytes 786436
  242.7 5.6 collective-permute-start.1
  278.7 31.5 %copy-start.13 = (bf16[32,256,256]{2,1,0:T(8,128)(2,1)S(1)}, bf16[32,256,256]{2,1,0:T(8,128)(2,1)}, u32[]{:S(2)}) copy-start(bf16[32,256,256]{2,1,0:T(8,128)(2,1)} %copy-done.12) | copy-start | bytes 12582916
  278.7 31.5 %copy-start.31 = (bf16[16,32,256]{2,1,0:T(8,128)(2,1)S(1)}, bf16[16,32,256]{2,1,0:T(8,128)(2,1)}, u32[]{:S(2)}) copy-start(bf16[16,32,256]{2,1,0:T(8,128)(2,1)} %copy-done.30) | copy-start | bytes 786436
  310.2 31.4 %copy-start.10 = (bf16[32,256,256]{2,1,0:T(8,128)(2,1)S(1)}, bf16[32,256,256]{2,1,0:T(8,128)(2,1)}, u32[]{:S(2)}) copy-start(bf16[32,256,256]{2,1,0:T(8,128)(2,1)} %copy-done.8) | copy-start | bytes 12582916
  377.5 35.9 %copy-start.21 = (bf16[16,32,256]{2,1,0:T(8,128)(2,1)S(1)}, bf16[16,32,256]{2,1,0:T(8,128)(2,1)}, u32[]{:S(2)}) copy-start(bf16[16,32,256]{2,1,0:T(8,128)(2,1)} %copy-done.20) | copy-start | bytes 786436
  377.6 4.9 collective-permute-start.2
  415.6 31.4 %copy-start.14 = (bf16[32,256,256]{2,1,0:T(8,128)(2,1)S(1)}, bf16[32,256,256]{2,1,0:T(8,128)(2,1)}, u32[]{:S(2)}) copy-start(bf16[32,256,256]{2,1,0:T(8,128)(2,1)} %copy-done.12) | copy-start | bytes 12582916
  415.6 31.4 %copy-start.25 = (bf16[16,32,256]{2,1,0:T(8,128)(2,1)S(1)}, bf16[16,32,256]{2,1,0:T(8,128)(2,1)}, u32[]{:S(2)}) copy-start(bf16[16,32,256]{2,1,0:T(8,128)(2,1)} %copy-done.24) | copy-start | bytes 786436
  447.0 31.2 %copy-start.27 = (bf16[16,32,256]{2,1,0:T(8,128)(2,1)S(1)}, bf16[16,32,256]{2,1,0:T(8,128)(2,1)}, u32[]{:S(2)}) copy-start(bf16[16,32,256]{2,1,0:T(8,128)(2,1)} %copy-done.26) | copy-start | bytes 786436
  478.2 31.5 %copy-start.7 = (bf16[32,256,256]{2,1,0:T(8,128)(2,1)S(1)}, bf16[32,256,256]{2,1,0:T(8,128)(2,1)}, u32[]{:S(2)}) copy-start(bf16[32,256,256]{2,1,0:T(8,128)(2,1)} %copy-done.5) | copy-start | bytes 12582916
  478.2 31.5 %copy-start.29 = (bf16[16,32,256]{2,1,0:T(8,128)(2,1)S(1)}, bf16[16,32,256]{2,1,0:T(8,128)(2,1)}, u32[]{:S(2)}) copy-start(bf16[16,32,256]{2,1,0:T(8,128)(2,1)} %copy-done.28) | copy-start | bytes 786436
  509.8 38.9 %copy-start.4 = (bf16[32,256,256]{2,1,0:T(8,128)(2,1)S(1)}, bf16[32,256,256]{2,1,0:T(8,128)(2,1)}, u32[]{:S(2)}) copy-start(bf16[32,256,256]{2,1,0:T(8,128)(2,1)} %copy-done.1) | copy-start | bytes 12582916
  512.9 4.9 collective-permute-start.3
  664.4 5.8 collective-permute-start.4
  (24 other events, 168.1 us)
Sparse Core Ops, SparseCore 0:
  10.2 104.9 all-gather.17
  119.4 70.8 all-gather.19

commit v5 on v4

--- a/solution.py
+++ b/solution.py
@@ -19,40 +19,48 @@
     return pltpu.CompilerParams(vmem_limit_bytes=mebibytes << 20)
 
 
-def expand_body(code_ref, came, dense_ref, blocks, arrival, *, place, col_blocks):
-    slots, size = blocks.shape[0], blocks.shape[1]
-    dead = 2 * col_blocks
-    fetch = pltpu.make_async_copy(came.at[place], blocks, arrival)
-    fetch.start()
-    dense_ref[...] = jnp.zeros_like(dense_ref)
-    fetch.wait()
-
-    def put(slot, carry):
-        code = code_ref[slot]
-
-        @pl.when(code < dead)
-        def _():
-            row, col = code // col_blocks, code % col_blocks
-            rows = pl.ds(pl.multiple_of(row * size, size), size)
-            cols = pl.ds(pl.multiple_of((col % 2) * size, size), size)
-            dense_ref[col // 2, rows, cols] = blocks[slot]
-
-        return carry
-
-    lax.fori_loop(0, slots, put, 0)
-
-
-def expand(codes, weights, place, shards):
+def block_of(code, col_blocks):
+    row = lax.shift_right_logical(code, col_blocks.bit_length() - 1) & 1
+    return row, code & (col_blocks - 1)
+
+
+def at_once(slots, most):
+    return max(n for n in range(1, most + 1) if slots % n == 0)
+
+
+def expand_body(code_ref, came, *dense, col_blocks):
+    slots, size = came.shape[1], came.shape[2]
+    several = at_once(slots, 8)
+    for place in reversed(range(group)):
+        rows_of = dense[place]
+        rows_of[...] = jnp.zeros_like(rows_of)
+
+        def some(first, carry):
+            for i in range(several):
+                slot = first * several + i
+                code = code_ref[place * slots + slot]
+                row, col = block_of(code, col_blocks)
+                rows = pl.ds(pl.multiple_of(row * size, size), size)
+                cols = pl.ds(pl.multiple_of((col & 1) * size, size), size)
+                block = came[place, slot]
+                block = jnp.where(code < 2 * col_blocks, block, jnp.zeros_like(block))
+                rows_of[lax.shift_right_logical(col, 1), rows, cols] = block
+            return carry
+
+        lax.fori_loop(0, slots // several, some, 0)
+
+
+def expand(codes, weights, shards):
     width = 2 * weights.shape[2]
+    vmem = pl.BlockSpec(memory_space=pltpu.VMEM)
     return pl.pallas_call(
-        functools.partial(expand_body, place=place, col_blocks=2 * shards),
-        out_shape=jax.ShapeDtypeStruct((shards, width, width), bf16),
-        in_specs=[pl.BlockSpec(memory_space=pltpu.SMEM), pl.BlockSpec(memory_space=pltpu.HBM)],
-        out_specs=pl.BlockSpec(memory_space=pltpu.VMEM),
-        scratch_shapes=[pltpu.VMEM(weights.shape[1:], bf16), pltpu.SemaphoreType.DMA],
-        compiler_params=params(24),
+        functools.partial(expand_body, col_blocks=2 * shards),
+        out_shape=(jax.ShapeDtypeStruct((shards, width, width), bf16),) * group,
+        in_specs=[pl.BlockSpec(memory_space=pltpu.SMEM), vmem],
+        out_specs=(vmem,) * group,
+        compiler_params=params(32),
         name="expand",
-    )(codes, weights)
+    )(codes.reshape(-1), weights)
 
 
 def layer_body(
@@ -132,7 +140,7 @@
         ),
         in_specs=[pl.BlockSpec(memory_space=pltpu.SMEM)] + [vmem] * (len(operands) + len(extra)),
         out_specs=(vmem,) * 4,
-        compiler_params=params(16),
+        compiler_params=params(12),
         name="layer",
     )(flags, *operands, *extra)
 
@@ -165,15 +173,14 @@
 
     lax.fori_loop(0, half, arrange, 0)
     dead = 2 * col_blocks
-    several = 4 if slots % 4 == 0 else 2
+    several = at_once(slots, 4)
 
     def some(first, carry):
         found = []
         for i in range(several):
             code = code_ref[first * several + i]
             live = (code < dead).astype(f32)
-            place = code % dead
-            row, col = place // col_blocks, place % col_blocks
+            row, col = block_of(code, col_blocks)
             grad = jnp.dot(left[row], right[col], preferred_element_type=f32) * live
             found.append((row, grad))
         for i, (row, grad) in enumerate(found):
@@ -205,7 +212,7 @@
             pltpu.VMEM((2, size, parts * part), bf16),
             pltpu.VMEM((2, size, size), f32),
         ],
-        compiler_params=params(32),
+        compiler_params=params(20),
         name="slot_grads",
     )(codes, mine, other, inputs, gain, blocks)
 
@@ -273,13 +280,11 @@
     found = {first: (second_inputs, 0), first - 1: (third_inputs, 0)}
     flags = [shard % 2] + [line == lines - 1 - phase for phase in range(1, lines)]
     flags = jnp.stack([flag.astype(jnp.int32) for flag in flags])
-    dense = [None] * group
+    dense = expand(line_codes, weights, shards)
     kept = [None] * group
     full = None
     for step in range(sections):
         phase, place = step // group, first - step % group
-        if phase == 0:
-            dense[place] = expand(line_codes[place], weights, place, shards)
         before = full
         if step == 0:
             (above, above_at), above_own = found[first], inputs[first]

time: 685 us -> 682 us (level)
    unnamed x80 -> x68, local copies, waits for them, and re-layouts: 16.1 us -> 13.7 us
where the time goes in v5:
time: 682 us
  blocking collectives  562 us (82%)
  Pallas kernels  51.3 us (8%)
  local copies, waits for them, and re-layouts  18.3 us (3%)
  waiting for transfers between devices  18.2 us (3%)
  between operations  14.6 us (2%)
  starting transfers between devices  13.5 us (2%)
    all_gather x16, blocking collectives, per_device(): gathered = lax.all_gather(sent, 'tp')  474 us
    all_gather x1, blocking collectives, per_device(): second_inputs = lax.all_gather(inputs[first], 'tp')  39.6 us
    pallas_call x16, Pallas kernels, layer(): pl.pallas_call(functools.partial(layer_body, above_at=above_at, told=befo...  36.7 us
    all_gather x1, blocking collectives, per_device(): third_inputs = lax.all_gather(third, 'tp')  29.8 us
    all_to_all x1, blocking collectives, per_device(): came = lax.all_to_all(leaving, 'pipe', 0, 0, axis_index_groups=together)  18.6 us
    unnamed x68, local copies, waits for them, and re-layouts  13.7 us
  transfers between devices with their start and end apart: 8, of which 5 were waited for; matrix products, arithmetic and copies ran while one was open for 0% of the time, Pallas kernels for 2%

profile of v5, /device:TPU:1, one launch (start us, length us, event | category | flops | bytes accessed | tf_op | source)
XLA Modules:
  0.0 681.5 jit_solution(520366528471718910)
XLA Ops:
  8.9 4.8 all-to-all-start
  13.9 4.5 all-to-all-done
  18.7 39.6 %all_gather.108.above = bf16[32,32,256]{2,1,0:T(8,128)(2,1)S(1)} all-gather(bf16[1,32,256]{2,1,0:T(8,128)(2,1)S(1)} %get-tuple-element.171), channel_id=1, replica_groups=mesh['pipe'=16,'tp'=32] {'tp'}, dimensions={0}, use_global_device_ids=true | all-gather | bytes 540672 | tf_op jit(solution)/shard_map/all_gather | solution.py:257
  58.3 29.2 %all-gather = bf16[1024,384]{1,0:T(8,128)(2,1)S(1)} all-gather(bf16[32,384]{1,0:T(8,128)(2,1)S(1)} %pad_maximum_fusion.3), channel_id=2, replica_groups=mesh['pipe'=16,'tp'=32] {'tp'}, dimensions={0}, use_global_device_ids=true | all-gather | bytes 811008 | tf_op jit(solution)/shard_map/all_gather | solution.py:267
  88.8 29.8 %all-gather.1 = bf16[1024,256]{1,0:T(8,128)(2,1)S(1)} all-gather(bf16[32,256]{1,0:T(8,128)(2,1)S(1)} %get-tuple-element.91.here.above_own), channel_id=3, replica_groups=mesh['pipe'=16,'tp'=32] {'tp'}, dimensions={0}, use_global_device_ids=true | all-gather | bytes 540672 | tf_op jit(solution)/shard_map/all_gather | solution.py:274
  120.5 7.8 %expand.1 = (bf16[32,256,256]{2,1,0:T(8,128)(2,1)S(1)}, bf16[32,256,256]{2,1,0:T(8,128)(2,1)S(1)}, bf16[32,256,256]{2,1,0:T(8,128)(2,1)S(1)}, bf16[32,256,256]{2,1,0:T(8,128)(2,1)S(1)}) custom-call(s32[288]{0:T(512)S(1)} %reshape.173.code_ref, bf16[4,72,128,128]{3,2,1,0:T(8,128)(2,1)} %all-gather.18.cloned.1.call-done.came), custom_call_target="tpu_custom_call" | custom-call | tf_op jit(solution)/shard_map/expand/pallas_call | solution.py:56
  134.4 29.1 %all-gather.2 = bf16[1024,256]{1,0:T(8,128)(2,1)S(1)} all-gather(bf16[32,256]{1,0:T(8,128)(2,1)S(1)} %get-tuple-element.95), channel_id=4, replica_groups=mesh['pipe'=16,'tp'=32] {'tp'}, dimensions={0}, use_global_device_ids=true | all-gather | bytes 540672 | tf_op jit(solution)/shard_map/all_gather | solution.py:309
  169.2 29.7 %all-gather.3 = bf16[1024,256]{1,0:T(8,128)(2,1)S(1)} all-gather(bf16[32,256]{1,0:T(8,128)(2,1)S(1)} %get-tuple-element.99), channel_id=5, replica_groups=mesh['pipe'=16,'tp'=32] {'tp'}, dimensions={0}, use_global_device_ids=true | all-gather | bytes 540672 | tf_op jit(solution)/shard_map/all_gather | solution.py:309
  204.2 29.9 %all-gather.5 = bf16[1024,256]{1,0:T(8,128)(2,1)S(1)} all-gather(bf16[32,256]{1,0:T(8,128)(2,1)S(1)} %get-tuple-element.106), channel_id=7, replica_groups=mesh['pipe'=16,'tp'=32] {'tp'}, dimensions={0}, use_global_device_ids=true | all-gather | bytes 540672 | tf_op jit(solution)/shard_map/all_gather | solution.py:309
  241.4 31.2 %all_gather.122.gathered = bf16[32,32,384]{2,1,0:T(8,128)(2,1)S(1)} all-gather(bf16[1,32,384]{2,1,0:T(8,128)(2,1)S(1)} %pad_maximum_fusion.4), channel_id=1, replica_groups=mesh['pipe'=16,'tp'=32] {'tp'}, dimensions={0}, use_global_device_ids=true | all-gather | bytes 811008 | tf_op jit(solution)/shard_map/all_gather | solution.py:309
  274.8 29.0 %all-gather.6 = bf16[1024,256]{1,0:T(8,128)(2,1)S(1)} all-gather(bf16[32,256]{1,0:T(8,128)(2,1)S(1)} %get-tuple-element.114), channel_id=8, replica_groups=mesh['pipe'=16,'tp'=32] {'tp'}, dimensions={0}, use_global_device_ids=true | all-gather | bytes 540672 | tf_op jit(solution)/shard_map/all_gather | solution.py:309
  306.0 29.5 %all-gather.7 = bf16[1024,256]{1,0:T(8,128)(2,1)S(1)} all-gather(bf16[32,256]{1,0:T(8,128)(2,1)S(1)} %get-tuple-element.118), channel_id=9, replica_groups=mesh['pipe'=16,'tp'=32] {'tp'}, dimensions={0}, use_global_device_ids=true | all-gather | bytes 540672 | tf_op jit(solution)/shard_map/all_gather | solution.py:309
  338.4 29.0 %all-gather.8 = bf16[1024,256]{1,0:T(8,128)(2,1)S(1)} all-gather(bf16[32,256]{1,0:T(8,128)(2,1)S(1)} %get-tuple-element.122), channel_id=10, replica_groups=mesh['pipe'=16,'tp'=32] {'tp'}, dimensions={0}, use_global_device_ids=true | all-gather | bytes 540672 | tf_op jit(solution)/shard_map/all_gather | solution.py:309
  372.5 3.7 collective-permute-done.2
  377.7 31.2 %all_gather.129.gathered = bf16[32,32,384]{2,1,0:T(8,128)(2,1)S(1)} all-gather(bf16[1,32,384]{2,1,0:T(8,128)(2,1)S(1)} %pad_maximum_fusion.5), channel_id=1, replica_groups=mesh['pipe'=16,'tp'=32] {'tp'}, dimensions={0}, use_global_device_ids=true | all-gather | bytes 811008 | tf_op jit(solution)/shard_map/all_gather | solution.py:309
  414.7 29.0 %all-gather.9 = bf16[1024,256]{1,0:T(8,128)(2,1)S(1)} all-gather(bf16[32,256]{1,0:T(8,128)(2,1)S(1)} %get-tuple-element.129), channel_id=11, replica_groups=mesh['pipe'=16,'tp'=32] {'tp'}, dimensions={0}, use_global_device_ids=true | all-gather | bytes 540672 | tf_op jit(solution)/shard_map/all_gather | solution.py:309
  445.9 29.4 %all-gather.10 = bf16[1024,256]{1,0:T(8,128)(2,1)S(1)} all-gather(bf16[32,256]{1,0:T(8,128)(2,1)S(1)} %get-tuple-element.133), channel_id=12, replica_groups=mesh['pipe'=16,'tp'=32] {'tp'}, dimensions={0}, use_global_device_ids=true | all-gather | bytes 540672 | tf_op jit(solution)/shard_map/all_gather | solution.py:309
  477.5 29.0 %all-gather.11 = bf16[1024,256]{1,0:T(8,128)(2,1)S(1)} all-gather(bf16[32,256]{1,0:T(8,128)(2,1)S(1)} %get-tuple-element.137), channel_id=13, replica_groups=mesh['pipe'=16,'tp'=32] {'tp'}, dimensions={0}, use_global_device_ids=true | all-gather | bytes 540672 | tf_op jit(solution)/shard_map/all_gather | solution.py:309
  514.5 31.2 %all_gather.136.gathered = bf16[32,32,384]{2,1,0:T(8,128)(2,1)S(1)} all-gather(bf16[1,32,384]{2,1,0:T(8,128)(2,1)S(1)} %pad_maximum_fusion.6), channel_id=1, replica_groups=mesh['pipe'=16,'tp'=32] {'tp'}, dimensions={0}, use_global_device_ids=true | all-gather | bytes 811008 | tf_op jit(solution)/shard_map/all_gather | solution.py:309
  547.8 29.0 %all-gather.12 = bf16[1024,256]{1,0:T(8,128)(2,1)S(1)} all-gather(bf16[32,256]{1,0:T(8,128)(2,1)S(1)} %get-tuple-element.144), channel_id=14, replica_groups=mesh['pipe'=16,'tp'=32] {'tp'}, dimensions={0}, use_global_device_ids=true | all-gather | bytes 540672 | tf_op jit(solution)/shard_map/all_gather | solution.py:309
  579.0 29.4 %all-gather.13 = bf16[1024,256]{1,0:T(8,128)(2,1)S(1)} all-gather(bf16[32,256]{1,0:T(8,128)(2,1)S(1)} %get-tuple-element.148), channel_id=15, replica_groups=mesh['pipe'=16,'tp'=32] {'tp'}, dimensions={0}, use_global_device_ids=true | all-gather | bytes 540672 | tf_op jit(solution)/shard_map/all_gather | solution.py:309
  610.5 29.0 %all-gather.14 = bf16[1024,256]{1,0:T(8,128)(2,1)S(1)} all-gather(bf16[32,256]{1,0:T(8,128)(2,1)S(1)} %get-tuple-element.152), channel_id=16, replica_groups=mesh['pipe'=16,'tp'=32] {'tp'}, dimensions={0}, use_global_device_ids=true | all-gather | bytes 540672 | tf_op jit(solution)/shard_map/all_gather | solution.py:309
  642.7 18.6 %all_to_all.10.mine = bf16[4,17,32,256]{3,2,1,0:T(8,128)(2,1)S(1)} all-to-all(bf16[4,17,32,256]{3,2,1,0:T(8,128)(2,1)S(1)} %pad_maximum_fusion), channel_id=1, replica_groups={{0,32,64,96},{128,160,192,224},{256,288,320,352},{384,416,448,480},{1,3..., dimensions={0} | all-to-all | bytes 2228224 | tf_op jit(solution)/shard_map/all_to_all | solution.py:325
  667.1 6.8 %slot_grads.1 = (bf16[72,128,128]{2,1,0:T(8,128)(2,1)}, f32[256,1]{1,0:T(8,128)S(1)}) custom-call(s32[73]{0:T(128)S(1)} %pad_add_fusion.code_ref, bf16[4,17,32,256]{3,2,1,0:T(8,128)(2,1)S(1)} %all_to_all.10.mine, bf16[4,17,32,256]{3,2,1,0:T(8,128)(2,1)S(1)} %collective-permute-done.4.other, bf16[4,32,256]{2,1,0:T(8,128)(2,1)S(1)} %bitcast.126, ...), custom_call_target="tpu_custom_call" | custom-call | tf_op jit(solution)/shard_map/slot_grads/pallas_call | solution.py:202
  (175 shorter events, 77.3 us)
Async XLA Ops:
  7.2 112.0 %all-gather.18.cloned.1.call-start = ((), (), s32[]{:S(2)}) async-start(), calls=%async_computation.2 | async-start | bytes 11796480 | tf_op jit(solution)/shard_map/all_gather | solution.py:256
  8.9 9.5 %all-to-all-start = ((bf16[4,48,256]{2,1,0:T(8,128)(2,1)}), bf16[4,48,256]{2,1,0:T(8,128)(2,1)S(1)}, u32[]{:S(2)}, u32[]{:S(2)}) async-start(bf16[4,48,256]{2,1,0:T(8,128)(2,1)} %pad_maximum_fusion.1), calls=%async_computation | async-start | bytes 196608 | tf_op jit(solution)/shard_map/all_to_all | solution.py:249
  13.7 185.1 %all-gather.20.cloned.1.call-start = ((), (), s32[]{:S(2)}) async-start(), calls=%async_computation.3 | async-start | bytes 1622016 | tf_op jit(solution)/shard_map/all_gather | solution.py:278
  87.5 31.1 %collective-permute-start = (bf16[32,256]{1,0:T(8,128)(2,1)S(1)}, bf16[32,256]{1,0:T(8,128)(2,1)S(1)}, u32[]{:S(2)}, u32[]{:S(2)}) collective-permute-start(bf16[32,256]{1,0:T(8,128)(2,1)S(1)} %get-tuple-element.170.here), channel_id=1, source_target_pairs={{128,0},{160,32},{192,64},{224,96},{256,128},{288,160},{320,192},{... | collective-permute-start | bytes 49160 | tf_op jit(solution)/shard_map/ppermute | solution.py:255
  202.1 32.1 %copy-start = (bf16[3072,256]{1,0:T(8,128)(2,1)S(1)}, bf16[3072,256]{1,0:T(8,128)(2,1)}, u32[]{:S(2)}) copy-start(bf16[3072,256]{1,0:T(8,128)(2,1)} %all-gather.20.cloned.1.call-done) | copy-start | bytes 4718596
  202.1 32.1 %copy-start.6 = (bf16[32,256,256]{2,1,0:T(8,128)(2,1)S(1)}, bf16[32,256,256]{2,1,0:T(8,128)(2,1)}, u32[]{:S(2)}) copy-start(bf16[32,256,256]{2,1,0:T(8,128)(2,1)} %copy-done.5) | copy-start | bytes 12582916
  234.1 38.5 %copy-start.2 = (bf16[32,256,256]{2,1,0:T(8,128)(2,1)S(1)}, bf16[32,256,256]{2,1,0:T(8,128)(2,1)}, u32[]{:S(2)}) copy-start(bf16[32,256,256]{2,1,0:T(8,128)(2,1)} %copy-done.1) | copy-start | bytes 12582916
  236.4 36.3 %copy-start.20 = (bf16[16,32,256]{2,1,0:T(8,128)(2,1)S(1)}, bf16[16,32,256]{2,1,0:T(8,128)(2,1)}, u32[]{:S(2)}) copy-start(bf16[16,32,256]{2,1,0:T(8,128)(2,1)} %copy-done.19) | copy-start | bytes 786436
  236.5 4.8 collective-permute-start.1
  272.7 31.1 %copy-start.13 = (bf16[32,256,256]{2,1,0:T(8,128)(2,1)S(1)}, bf16[32,256,256]{2,1,0:T(8,128)(2,1)}, u32[]{:S(2)}) copy-start(bf16[32,256,256]{2,1,0:T(8,128)(2,1)} %copy-done.12) | copy-start | bytes 12582916
  272.7 31.1 %copy-start.28 = (bf16[16,32,256]{2,1,0:T(8,128)(2,1)S(1)}, bf16[16,32,256]{2,1,0:T(8,128)(2,1)}, u32[]{:S(2)}) copy-start(bf16[16,32,256]{2,1,0:T(8,128)(2,1)} %copy-done.27) | copy-start | bytes 786436
  303.8 31.7 %copy-start.10 = (bf16[32,256,256]{2,1,0:T(8,128)(2,1)S(1)}, bf16[32,256,256]{2,1,0:T(8,128)(2,1)}, u32[]{:S(2)}) copy-start(bf16[32,256,256]{2,1,0:T(8,128)(2,1)} %copy-done.8) | copy-start | bytes 12582916
  305.9 29.6 %copy-start.21 = (bf16[16,32,256]{2,1,0:T(8,128)(2,1)}, bf16[16,32,256]{2,1,0:T(8,128)(2,1)S(1)}, u32[]{:S(2)}) copy-start(bf16[16,32,256]{2,1,0:T(8,128)(2,1)S(1)} %get-tuple-element.132.rest_1_) | copy-start | bytes 786436
  370.4 40.1 %copy-start.25 = (bf16[16,32,256]{2,1,0:T(8,128)(2,1)}, bf16[16,32,256]{2,1,0:T(8,128)(2,1)S(1)}, u32[]{:S(2)}) copy-start(bf16[16,32,256]{2,1,0:T(8,128)(2,1)S(1)} %get-tuple-element.140.rest_1_) | copy-start | bytes 786436
  371.1 5.1 collective-permute-start.2
  412.7 31.1 %copy-start.14 = (bf16[32,256,256]{2,1,0:T(8,128)(2,1)S(1)}, bf16[32,256,256]{2,1,0:T(8,128)(2,1)}, u32[]{:S(2)}) copy-start(bf16[32,256,256]{2,1,0:T(8,128)(2,1)} %copy-done.12) | copy-start | bytes 12582916
  412.7 31.1 %copy-start.22 = (bf16[16,32,256]{2,1,0:T(8,128)(2,1)S(1)}, bf16[16,32,256]{2,1,0:T(8,128)(2,1)}, u32[]{:S(2)}) copy-start(bf16[16,32,256]{2,1,0:T(8,128)(2,1)} %copy-done.21) | copy-start | bytes 786436
  443.8 31.5 %copy-start.11 = (bf16[32,256,256]{2,1,0:T(8,128)(2,1)S(1)}, bf16[32,256,256]{2,1,0:T(8,128)(2,1)}, u32[]{:S(2)}) copy-start(bf16[32,256,256]{2,1,0:T(8,128)(2,1)} %copy-done.8) | copy-start | bytes 12582916
  443.8 31.5 %copy-start.24 = (bf16[16,32,256]{2,1,0:T(8,128)(2,1)S(1)}, bf16[16,32,256]{2,1,0:T(8,128)(2,1)}, u32[]{:S(2)}) copy-start(bf16[16,32,256]{2,1,0:T(8,128)(2,1)} %copy-done.23) | copy-start | bytes 786436
  475.3 31.2 %copy-start.7 = (bf16[32,256,256]{2,1,0:T(8,128)(2,1)S(1)}, bf16[32,256,256]{2,1,0:T(8,128)(2,1)}, u32[]{:S(2)}) copy-start(bf16[32,256,256]{2,1,0:T(8,128)(2,1)} %copy-done.5) | copy-start | bytes 12582916
  475.3 31.2 %copy-start.26 = (bf16[16,32,256]{2,1,0:T(8,128)(2,1)S(1)}, bf16[16,32,256]{2,1,0:T(8,128)(2,1)}, u32[]{:S(2)}) copy-start(bf16[16,32,256]{2,1,0:T(8,128)(2,1)} %copy-done.25) | copy-start | bytes 786436
  506.5 39.3 %copy-start.4 = (bf16[32,256,256]{2,1,0:T(8,128)(2,1)S(1)}, bf16[32,256,256]{2,1,0:T(8,128)(2,1)}, u32[]{:S(2)}) copy-start(bf16[32,256,256]{2,1,0:T(8,128)(2,1)} %copy-done.1) | copy-start | bytes 12582916
  509.6 4.8 collective-permute-start.3
  661.3 5.8 collective-permute-start.4
  (18 other events, 86.2 us)
Sparse Core Ops, SparseCore 0:
  10.2 104.9 all-gather.17
  119.4 70.8 all-gather.19

commit v6 on v5

--- a/solution.py
+++ b/solution.py
@@ -28,37 +28,61 @@
     return max(n for n in range(1, most + 1) if slots % n == 0)
 
 
-def expand_body(code_ref, came, *dense, col_blocks):
+def expand_body(code_ref, came, *rest, col_blocks):
+    dense, (blocks, filled, arrival, leaving) = rest[:group], rest[group:]
     slots, size = came.shape[1], came.shape[2]
     several = at_once(slots, 8)
-    for place in reversed(range(group)):
-        rows_of = dense[place]
+    order = list(reversed(range(group)))
+    fetches = [
+        pltpu.make_async_copy(came.at[place], blocks.at[place], arrival.at[place])
+        for place in order
+    ]
+    stores = [
+        pltpu.make_async_copy(filled.at[i % 2], dense[place], leaving.at[place])
+        for i, place in enumerate(order)
+    ]
+    for fetch in fetches:
+        fetch.start()
+    for i, place in enumerate(order):
+        if i >= 2:
+            stores[i - 2].wait()
+        rows_of = filled.at[i % 2]
         rows_of[...] = jnp.zeros_like(rows_of)
+        fetches[i].wait()
 
         def some(first, carry):
-            for i in range(several):
-                slot = first * several + i
+            for j in range(several):
+                slot = first * several + j
                 code = code_ref[place * slots + slot]
                 row, col = block_of(code, col_blocks)
                 rows = pl.ds(pl.multiple_of(row * size, size), size)
                 cols = pl.ds(pl.multiple_of((col & 1) * size, size), size)
-                block = came[place, slot]
+                block = blocks[place, slot]
                 block = jnp.where(code < 2 * col_blocks, block, jnp.zeros_like(block))
                 rows_of[lax.shift_right_logical(col, 1), rows, cols] = block
             return carry
 
         lax.fori_loop(0, slots // several, some, 0)
+        stores[i].start()
+    for store in stores[-2:]:
+        store.wait()
 
 
 def expand(codes, weights, shards):
     width = 2 * weights.shape[2]
-    vmem = pl.BlockSpec(memory_space=pltpu.VMEM)
+    hbm = pl.BlockSpec(memory_space=pltpu.HBM)
     return pl.pallas_call(
         functools.partial(expand_body, col_blocks=2 * shards),
         out_shape=(jax.ShapeDtypeStruct((shards, width, width), bf16),) * group,
-        in_specs=[pl.BlockSpec(memory_space=pltpu.SMEM), vmem],
-        out_specs=(vmem,) * group,
-        compiler_params=params(32),
+        in_specs=[pl.BlockSpec(memory_space=pltpu.SMEM), hbm],
+        out_specs=(hbm,) * group,
+        scratch_shapes=[
+            pltpu.VMEM(weights.shape, bf16),
+            pltpu.VMEM((2, shards, width, width), bf16),
+            pltpu.SemaphoreType.DMA((group,)),
+            pltpu.SemaphoreType.DMA((group,)),
+        ],
+        compiler_params=params(44),
         name="expand",
     )(codes.reshape(-1), weights)
 
@@ -212,7 +236,7 @@
             pltpu.VMEM((2, size, parts * part), bf16),
             pltpu.VMEM((2, size, size), f32),
         ],
-        compiler_params=params(20),
+        compiler_params=params(32),
         name="slot_grads",
     )(codes, mine, other, inputs, gain, blocks)
 

time: 682 us -> 683 us (level)
  no operation moved by 1% of the time
where the time goes in v6:
time: 683 us; the launch traced here: 682 us
  blocking collectives  562 us (82%)
  Pallas kernels  51.4 us (8%)
  waiting for transfers between devices  18.2 us (3%)
  local copies, waits for them, and re-layouts  18 us (3%)
  between operations  14.6 us (2%)
  starting transfers between devices  13.5 us (2%)
    all_gather x16, blocking collectives, per_device(): gathered = lax.all_gather(sent, 'tp')  474 us
    all_gather x1, blocking collectives, per_device(): second_inputs = lax.all_gather(inputs[first], 'tp')  39.6 us
    pallas_call x16, Pallas kernels, layer(): pl.pallas_call(functools.partial(layer_body, above_at=above_at, told=befo...  36.7 us
    all_gather x1, blocking collectives, per_device(): third_inputs = lax.all_gather(third, 'tp')  29.8 us
    all_to_all x1, blocking collectives, per_device(): came = lax.all_to_all(leaving, 'pipe', 0, 0, axis_index_groups=together)  18.7 us
  transfers between devices with their start and end apart: 8, of which 5 were waited for; matrix products, arithmetic and copies ran while one was open for 0% of the time, Pallas kernels for 2%

profile of v6, /device:TPU:1, one launch (start us, length us, event | category | flops | bytes accessed | tf_op | source)
XLA Modules:
  0.0 681.6 jit_solution(5067993700810488672)
XLA Ops:
  8.9 4.8 all-to-all-start
  13.9 4.5 all-to-all-done
  18.7 39.6 %all_gather.108.above = bf16[32,32,256]{2,1,0:T(8,128)(2,1)S(1)} all-gather(bf16[1,32,256]{2,1,0:T(8,128)(2,1)S(1)} %get-tuple-element.171), channel_id=1, replica_groups=mesh['pipe'=16,'tp'=32] {'tp'}, dimensions={0}, use_global_device_ids=true | all-gather | bytes 540672 | tf_op jit(solution)/shard_map/all_gather | solution.py:281
  58.3 29.2 %all-gather = bf16[1024,384]{1,0:T(8,128)(2,1)S(1)} all-gather(bf16[32,384]{1,0:T(8,128)(2,1)S(1)} %pad_maximum_fusion.3), channel_id=2, replica_groups=mesh['pipe'=16,'tp'=32] {'tp'}, dimensions={0}, use_global_device_ids=true | all-gather | bytes 811008 | tf_op jit(solution)/shard_map/all_gather | solution.py:291
  88.8 29.8 %all-gather.1 = bf16[1024,256]{1,0:T(8,128)(2,1)S(1)} all-gather(bf16[32,256]{1,0:T(8,128)(2,1)S(1)} %get-tuple-element.91.here.above_own), channel_id=3, replica_groups=mesh['pipe'=16,'tp'=32] {'tp'}, dimensions={0}, use_global_device_ids=true | all-gather | bytes 540672 | tf_op jit(solution)/shard_map/all_gather | solution.py:298
  120.5 7.8 %expand.1 = (bf16[32,256,256]{2,1,0:T(8,128)(2,1)S(1)}, bf16[32,256,256]{2,1,0:T(8,128)(2,1)S(1)}, bf16[32,256,256]{2,1,0:T(8,128)(2,1)}, bf16[32,256,256]{2,1,0:T(8,128)(2,1)}) custom-call(s32[288]{0:T(512)S(1)} %reshape.173.code_ref, bf16[4,72,128,128]{3,2,1,0:T(8,128)(2,1)} %all-gather.18.cloned.1.call-done.came), custom_call_target="tpu_custom_call" | custom-call | tf_op jit(solution)/shard_map/expand/pallas_call | solution.py:74
  136.1 29.3 %all-gather.2 = bf16[1024,256]{1,0:T(8,128)(2,1)S(1)} all-gather(bf16[32,256]{1,0:T(8,128)(2,1)S(1)} %get-tuple-element.95), channel_id=4, replica_groups=mesh['pipe'=16,'tp'=32] {'tp'}, dimensions={0}, use_global_device_ids=true | all-gather | bytes 540672 | tf_op jit(solution)/shard_map/all_gather | solution.py:333
  169.1 29.6 %all-gather.3 = bf16[1024,256]{1,0:T(8,128)(2,1)S(1)} all-gather(bf16[32,256]{1,0:T(8,128)(2,1)S(1)} %get-tuple-element.99), channel_id=5, replica_groups=mesh['pipe'=16,'tp'=32] {'tp'}, dimensions={0}, use_global_device_ids=true | all-gather | bytes 540672 | tf_op jit(solution)/shard_map/all_gather | solution.py:333
  204.1 30.1 %all-gather.5 = bf16[1024,256]{1,0:T(8,128)(2,1)S(1)} all-gather(bf16[32,256]{1,0:T(8,128)(2,1)S(1)} %get-tuple-element.106), channel_id=7, replica_groups=mesh['pipe'=16,'tp'=32] {'tp'}, dimensions={0}, use_global_device_ids=true | all-gather | bytes 540672 | tf_op jit(solution)/shard_map/all_gather | solution.py:333
  241.4 31.1 %all_gather.122.gathered = bf16[32,32,384]{2,1,0:T(8,128)(2,1)S(1)} all-gather(bf16[1,32,384]{2,1,0:T(8,128)(2,1)S(1)} %pad_maximum_fusion.4), channel_id=1, replica_groups=mesh['pipe'=16,'tp'=32] {'tp'}, dimensions={0}, use_global_device_ids=true | all-gather | bytes 811008 | tf_op jit(solution)/shard_map/all_gather | solution.py:333
  274.7 29.2 %all-gather.6 = bf16[1024,256]{1,0:T(8,128)(2,1)S(1)} all-gather(bf16[32,256]{1,0:T(8,128)(2,1)S(1)} %get-tuple-element.114), channel_id=8, replica_groups=mesh['pipe'=16,'tp'=32] {'tp'}, dimensions={0}, use_global_device_ids=true | all-gather | bytes 540672 | tf_op jit(solution)/shard_map/all_gather | solution.py:333
  306.0 29.4 %all-gather.7 = bf16[1024,256]{1,0:T(8,128)(2,1)S(1)} all-gather(bf16[32,256]{1,0:T(8,128)(2,1)S(1)} %get-tuple-element.118), channel_id=9, replica_groups=mesh['pipe'=16,'tp'=32] {'tp'}, dimensions={0}, use_global_device_ids=true | all-gather | bytes 540672 | tf_op jit(solution)/shard_map/all_gather | solution.py:333
  338.3 29.2 %all-gather.8 = bf16[1024,256]{1,0:T(8,128)(2,1)S(1)} all-gather(bf16[32,256]{1,0:T(8,128)(2,1)S(1)} %get-tuple-element.122), channel_id=10, replica_groups=mesh['pipe'=16,'tp'=32] {'tp'}, dimensions={0}, use_global_device_ids=true | all-gather | bytes 540672 | tf_op jit(solution)/shard_map/all_gather | solution.py:333
  372.6 3.7 collective-permute-done.2
  377.8 31.0 %all_gather.129.gathered = bf16[32,32,384]{2,1,0:T(8,128)(2,1)S(1)} all-gather(bf16[1,32,384]{2,1,0:T(8,128)(2,1)S(1)} %pad_maximum_fusion.5), channel_id=1, replica_groups=mesh['pipe'=16,'tp'=32] {'tp'}, dimensions={0}, use_global_device_ids=true | all-gather | bytes 811008 | tf_op jit(solution)/shard_map/all_gather | solution.py:333
  414.7 29.2 %all-gather.9 = bf16[1024,256]{1,0:T(8,128)(2,1)S(1)} all-gather(bf16[32,256]{1,0:T(8,128)(2,1)S(1)} %get-tuple-element.129), channel_id=11, replica_groups=mesh['pipe'=16,'tp'=32] {'tp'}, dimensions={0}, use_global_device_ids=true | all-gather | bytes 540672 | tf_op jit(solution)/shard_map/all_gather | solution.py:333
  446.0 29.2 %all-gather.10 = bf16[1024,256]{1,0:T(8,128)(2,1)S(1)} all-gather(bf16[32,256]{1,0:T(8,128)(2,1)S(1)} %get-tuple-element.133), channel_id=12, replica_groups=mesh['pipe'=16,'tp'=32] {'tp'}, dimensions={0}, use_global_device_ids=true | all-gather | bytes 540672 | tf_op jit(solution)/shard_map/all_gather | solution.py:333
  477.4 29.2 %all-gather.11 = bf16[1024,256]{1,0:T(8,128)(2,1)S(1)} all-gather(bf16[32,256]{1,0:T(8,128)(2,1)S(1)} %get-tuple-element.137), channel_id=13, replica_groups=mesh['pipe'=16,'tp'=32] {'tp'}, dimensions={0}, use_global_device_ids=true | all-gather | bytes 540672 | tf_op jit(solution)/shard_map/all_gather | solution.py:333
  514.5 31.1 %all_gather.136.gathered = bf16[32,32,384]{2,1,0:T(8,128)(2,1)S(1)} all-gather(bf16[1,32,384]{2,1,0:T(8,128)(2,1)S(1)} %pad_maximum_fusion.6), channel_id=1, replica_groups=mesh['pipe'=16,'tp'=32] {'tp'}, dimensions={0}, use_global_device_ids=true | all-gather | bytes 811008 | tf_op jit(solution)/shard_map/all_gather | solution.py:333
  547.8 29.2 %all-gather.12 = bf16[1024,256]{1,0:T(8,128)(2,1)S(1)} all-gather(bf16[32,256]{1,0:T(8,128)(2,1)S(1)} %get-tuple-element.144), channel_id=14, replica_groups=mesh['pipe'=16,'tp'=32] {'tp'}, dimensions={0}, use_global_device_ids=true | all-gather | bytes 540672 | tf_op jit(solution)/shard_map/all_gather | solution.py:333
  579.1 29.2 %all-gather.13 = bf16[1024,256]{1,0:T(8,128)(2,1)S(1)} all-gather(bf16[32,256]{1,0:T(8,128)(2,1)S(1)} %get-tuple-element.148), channel_id=15, replica_groups=mesh['pipe'=16,'tp'=32] {'tp'}, dimensions={0}, use_global_device_ids=true | all-gather | bytes 540672 | tf_op jit(solution)/shard_map/all_gather | solution.py:333
  610.4 29.2 %all-gather.14 = bf16[1024,256]{1,0:T(8,128)(2,1)S(1)} all-gather(bf16[32,256]{1,0:T(8,128)(2,1)S(1)} %get-tuple-element.152), channel_id=16, replica_groups=mesh['pipe'=16,'tp'=32] {'tp'}, dimensions={0}, use_global_device_ids=true | all-gather | bytes 540672 | tf_op jit(solution)/shard_map/all_gather | solution.py:333
  642.7 18.7 %all_to_all.10.mine = bf16[4,17,32,256]{3,2,1,0:T(8,128)(2,1)S(1)} all-to-all(bf16[4,17,32,256]{3,2,1,0:T(8,128)(2,1)S(1)} %pad_maximum_fusion), channel_id=1, replica_groups={{0,32,64,96},{128,160,192,224},{256,288,320,352},{384,416,448,480},{1,3..., dimensions={0} | all-to-all | bytes 2228224 | tf_op jit(solution)/shard_map/all_to_all | solution.py:349
  667.2 6.8 %slot_grads.1 = (bf16[72,128,128]{2,1,0:T(8,128)(2,1)}, f32[256,1]{1,0:T(8,128)S(1)}) custom-call(s32[73]{0:T(128)S(1)} %pad_add_fusion.code_ref, bf16[4,17,32,256]{3,2,1,0:T(8,128)(2,1)S(1)} %all_to_all.10.mine, bf16[4,17,32,256]{3,2,1,0:T(8,128)(2,1)S(1)} %collective-permute-done.4.other, bf16[4,32,256]{2,1,0:T(8,128)(2,1)S(1)} %bitcast.126, ...), custom_call_target="tpu_custom_call" | custom-call | tf_op jit(solution)/shard_map/slot_grads/pallas_call | solution.py:226
  (175 shorter events, 77.0 us)
Async XLA Ops:
  7.2 112.0 %all-gather.18.cloned.1.call-start = ((), (), s32[]{:S(2)}) async-start(), calls=%async_computation.2 | async-start | bytes 11796480 | tf_op jit(solution)/shard_map/all_gather | solution.py:280
  8.9 9.5 %all-to-all-start = ((bf16[4,48,256]{2,1,0:T(8,128)(2,1)}), bf16[4,48,256]{2,1,0:T(8,128)(2,1)S(1)}, u32[]{:S(2)}, u32[]{:S(2)}) async-start(bf16[4,48,256]{2,1,0:T(8,128)(2,1)} %pad_maximum_fusion.1), calls=%async_computation | async-start | bytes 196608 | tf_op jit(solution)/shard_map/all_to_all | solution.py:273
  13.7 185.0 %all-gather.20.cloned.1.call-start = ((), (), s32[]{:S(2)}) async-start(), calls=%async_computation.3 | async-start | bytes 1622016 | tf_op jit(solution)/shard_map/all_gather | solution.py:302
  87.5 31.1 %collective-permute-start = (bf16[32,256]{1,0:T(8,128)(2,1)S(1)}, bf16[32,256]{1,0:T(8,128)(2,1)S(1)}, u32[]{:S(2)}, u32[]{:S(2)}) collective-permute-start(bf16[32,256]{1,0:T(8,128)(2,1)S(1)} %get-tuple-element.170.here), channel_id=1, source_target_pairs={{128,0},{160,32},{192,64},{224,96},{256,128},{288,160},{320,192},{... | collective-permute-start | bytes 49160 | tf_op jit(solution)/shard_map/ppermute | solution.py:279
  134.0 31.5 %copy-start.12 = (bf16[32,256,256]{2,1,0:T(8,128)(2,1)S(1)}, bf16[32,256,256]{2,1,0:T(8,128)(2,1)}, u32[]{:S(2)}) copy-start(bf16[32,256,256]{2,1,0:T(8,128)(2,1)} %get-tuple-element.97.weight) | copy-start | bytes 12582916
  202.0 32.2 %copy-start = (bf16[3072,256]{1,0:T(8,128)(2,1)S(1)}, bf16[3072,256]{1,0:T(8,128)(2,1)}, u32[]{:S(2)}) copy-start(bf16[3072,256]{1,0:T(8,128)(2,1)} %all-gather.20.cloned.1.call-done) | copy-start | bytes 4718596
  202.0 32.2 %copy-start.6 = (bf16[32,256,256]{2,1,0:T(8,128)(2,1)S(1)}, bf16[32,256,256]{2,1,0:T(8,128)(2,1)}, u32[]{:S(2)}) copy-start(bf16[32,256,256]{2,1,0:T(8,128)(2,1)} %copy-done.5) | copy-start | bytes 12582916
  234.2 38.4 %copy-start.2 = (bf16[32,256,256]{2,1,0:T(8,128)(2,1)S(1)}, bf16[32,256,256]{2,1,0:T(8,128)(2,1)}, u32[]{:S(2)}) copy-start(bf16[32,256,256]{2,1,0:T(8,128)(2,1)} %get-tuple-element.94.weight) | copy-start | bytes 12582916
  236.4 36.1 %copy-start.20 = (bf16[16,32,256]{2,1,0:T(8,128)(2,1)S(1)}, bf16[16,32,256]{2,1,0:T(8,128)(2,1)}, u32[]{:S(2)}) copy-start(bf16[16,32,256]{2,1,0:T(8,128)(2,1)} %copy-done.19) | copy-start | bytes 786436
  236.6 4.8 collective-permute-start.1
  272.6 31.3 %copy-start.13 = (bf16[32,256,256]{2,1,0:T(8,128)(2,1)S(1)}, bf16[32,256,256]{2,1,0:T(8,128)(2,1)}, u32[]{:S(2)}) copy-start(bf16[32,256,256]{2,1,0:T(8,128)(2,1)} %get-tuple-element.97.weight) | copy-start | bytes 12582916
  272.6 31.3 %copy-start.28 = (bf16[16,32,256]{2,1,0:T(8,128)(2,1)S(1)}, bf16[16,32,256]{2,1,0:T(8,128)(2,1)}, u32[]{:S(2)}) copy-start(bf16[16,32,256]{2,1,0:T(8,128)(2,1)} %copy-done.27) | copy-start | bytes 786436
  303.9 31.5 %copy-start.10 = (bf16[32,256,256]{2,1,0:T(8,128)(2,1)S(1)}, bf16[32,256,256]{2,1,0:T(8,128)(2,1)}, u32[]{:S(2)}) copy-start(bf16[32,256,256]{2,1,0:T(8,128)(2,1)} %copy-done.8) | copy-start | bytes 12582916
  370.4 39.9 %copy-start.25 = (bf16[16,32,256]{2,1,0:T(8,128)(2,1)}, bf16[16,32,256]{2,1,0:T(8,128)(2,1)S(1)}, u32[]{:S(2)}) copy-start(bf16[16,32,256]{2,1,0:T(8,128)(2,1)S(1)} %get-tuple-element.140.rest_1_) | copy-start | bytes 786436
  371.2 5.1 collective-permute-start.2
  412.6 31.3 %copy-start.14 = (bf16[32,256,256]{2,1,0:T(8,128)(2,1)S(1)}, bf16[32,256,256]{2,1,0:T(8,128)(2,1)}, u32[]{:S(2)}) copy-start(bf16[32,256,256]{2,1,0:T(8,128)(2,1)} %get-tuple-element.97.weight) | copy-start | bytes 12582916
  412.6 31.3 %copy-start.22 = (bf16[16,32,256]{2,1,0:T(8,128)(2,1)S(1)}, bf16[16,32,256]{2,1,0:T(8,128)(2,1)}, u32[]{:S(2)}) copy-start(bf16[16,32,256]{2,1,0:T(8,128)(2,1)} %copy-done.21) | copy-start | bytes 786436
  443.9 31.4 %copy-start.11 = (bf16[32,256,256]{2,1,0:T(8,128)(2,1)S(1)}, bf16[32,256,256]{2,1,0:T(8,128)(2,1)}, u32[]{:S(2)}) copy-start(bf16[32,256,256]{2,1,0:T(8,128)(2,1)} %copy-done.8) | copy-start | bytes 12582916
  443.9 31.4 %copy-start.24 = (bf16[16,32,256]{2,1,0:T(8,128)(2,1)S(1)}, bf16[16,32,256]{2,1,0:T(8,128)(2,1)}, u32[]{:S(2)}) copy-start(bf16[16,32,256]{2,1,0:T(8,128)(2,1)} %copy-done.23) | copy-start | bytes 786436
  475.2 31.4 %copy-start.7 = (bf16[32,256,256]{2,1,0:T(8,128)(2,1)S(1)}, bf16[32,256,256]{2,1,0:T(8,128)(2,1)}, u32[]{:S(2)}) copy-start(bf16[32,256,256]{2,1,0:T(8,128)(2,1)} %copy-done.5) | copy-start | bytes 12582916
  475.2 31.4 %copy-start.26 = (bf16[16,32,256]{2,1,0:T(8,128)(2,1)S(1)}, bf16[16,32,256]{2,1,0:T(8,128)(2,1)}, u32[]{:S(2)}) copy-start(bf16[16,32,256]{2,1,0:T(8,128)(2,1)} %copy-done.25) | copy-start | bytes 786436
  506.6 39.1 %copy-start.4 = (bf16[32,256,256]{2,1,0:T(8,128)(2,1)S(1)}, bf16[32,256,256]{2,1,0:T(8,128)(2,1)}, u32[]{:S(2)}) copy-start(bf16[32,256,256]{2,1,0:T(8,128)(2,1)} %get-tuple-element.94.weight) | copy-start | bytes 12582916
  509.7 4.8 collective-permute-start.3
  661.4 5.8 collective-permute-start.4
  (18 other events, 119.2 us)
Sparse Core Ops, SparseCore 0:
  10.2 104.9 all-gather.17
  119.4 70.8 all-gather.19

commit v7 on v6

--- a/solution.py
+++ b/solution.py
@@ -94,6 +94,7 @@
     rest = list(rest)
     before = None if told else rest.pop(0)
     kept = rest.pop(0) if phase else None
+    next_scale = rest.pop(0) if tell else None
     full_out, sent_out, own_out, kept_out = rest
     shards, width = weight.shape[0], weight.shape[1]
     tokens = own.shape[0]
@@ -108,7 +109,11 @@
         for i in range(shards):
             change = gathered[i].astype(f32) - before[i].astype(f32)
             total += change * above[i, rows, :].astype(f32)
-    factor = above_scale[...] * jnp.sum(total, axis=1, keepdims=True)
+    if told:
+        dots, scale = total[:, 0:1] + total[:, 1:2], own[:, width + 2:width + 3]
+    else:
+        dots, scale = jnp.sum(total, axis=1, keepdims=True), above_scale[...]
+    factor = scale * dots
 
     acc = jnp.zeros((tokens, width), f32)
     for i in range(shards):
@@ -117,19 +122,21 @@
         full_out[i] = piece
         acc += lax.dot_general(piece, weight[i], across_last, preferred_element_type=f32)
 
-    grad = own[...] - factor * above_own[...].astype(f32)
+    grad = own[:, :width] - factor * above_own[...].astype(f32)
     scaled = gain[...] * acc
     rms = inv_rms[...]
     result = grad + rms * scaled
-    own_out[...] = result
-    sent_out[:, :width] = result.astype(bf16)
+    own_out[:, :width] = result
+    if not tell:
+        sent_out[...] = result.astype(bf16)
     if tell:
         dots = jnp.sum(scaled * (here[...].astype(f32) * rms), axis=1, keepdims=True)
         high = dots.astype(bf16).astype(f32)
         low = (dots - high).astype(bf16).astype(f32)
         lane = lax.broadcasted_iota(jnp.int32, (tokens, lanes), 1)
-        tail = jnp.where(lane == 0, high, jnp.where(lane == 1, low, 0.0))
-        sent_out[:, width:] = tail.astype(bf16)
+        tail = jnp.where(lane == 1, low, jnp.where(lane == 2, next_scale[...], 0.0))
+        own_out[:, width:] = jnp.where(lane == 0, high, tail)
+        sent_out[...] = own_out[...].astype(bf16)
 
     half = shards // 2
     mine = pl.ds(flags[0] * half, half)
@@ -146,11 +153,14 @@
         kept_out[...] = full_out[mine]
 
 
-def layer(flags, operands, before, kept, above_at, tell, phase):
+def layer(flags, operands, before, kept, next_scale, above_at, phase):
     weight, own = operands[5], operands[1]
     shards, width, tokens = weight.shape[0], weight.shape[1], own.shape[0]
     extra = [] if before is None else [before]
     extra += [] if kept is None else [kept]
+    extra += [] if next_scale is None else [next_scale]
+    tell = next_scale is not None
+    wide = width + (lanes if tell else 0)
     vmem = pl.BlockSpec(memory_space=pltpu.VMEM)
     return pl.pallas_call(
         functools.partial(
@@ -158,8 +168,8 @@
         ),
         out_shape=(
             jax.ShapeDtypeStruct((shards, tokens, width), bf16),
-            jax.ShapeDtypeStruct((tokens, width + (lanes if tell else 0)), bf16),
-            jax.ShapeDtypeStruct((tokens, width), f32),
+            jax.ShapeDtypeStruct((tokens, wide), bf16),
+            jax.ShapeDtypeStruct((tokens, wide), f32),
             jax.ShapeDtypeStruct((shards // 2, tokens, width), bf16),
         ),
         in_specs=[pl.BlockSpec(memory_space=pltpu.SMEM)] + [vmem] * (len(operands) + len(extra)),
@@ -285,7 +295,8 @@
     partial = jnp.pad(partial, ((0, 0), (0, lanes - 3 * group)))
     entry = jnp.where((teacher == 1)[:, None], kl_grads[1], kl_grads[0])
     entry = lax.dynamic_slice_in_dim(entry, block * part, part, 0)
-    own = entry.astype(f32)
+    own = jnp.pad(entry.astype(f32), ((0, 0), (0, lanes)))
+    no_scale = jnp.zeros((part, 1), f32)
     sent = jnp.concatenate([entry, partial], axis=1)
     sent, second_inputs = lax.optimization_barrier((sent, second_inputs))
     gathered = lax.all_gather(sent, "tp")
@@ -312,18 +323,10 @@
         before = full
         if step == 0:
             (above, above_at), above_own = found[first], inputs[first]
-            scale = jnp.zeros((part, 1), f32)
+            scale = no_scale
         elif place == first:
-            notes = jnp.concatenate(
-                [sent[:, width:width + 2].astype(f32), correct[0]], axis=1
-            )
-            notes = jnp.pad(notes, ((0, 0), (0, lanes - 3)))
-            passed = jnp.concatenate([own, notes], axis=1)
-            passed = lax.ppermute(passed, "pipe", down)
-            own = passed[:, :width]
-            tail = jnp.pad(passed[:, width:width + 2], ((0, 0), (0, lanes - 2)))
-            sent = jnp.concatenate([own, tail], axis=1).astype(bf16)
-            scale = passed[:, width + 2:width + 3]
+            own = lax.ppermute(own, "pipe", down)
+            sent, scale = own.astype(bf16), no_scale
             above, above_at, above_own = rest_inputs, 2, upper_own
             before = None
         else:
@@ -338,9 +341,9 @@
             gathered, own, above, above_own, scale, dense[place],
             inputs[place], inv_rms[place], gain_rows[place][None],
         )
-        tell = place == 0 and step < sections - 1
+        next_scale = correct[0] if place == 0 and step < sections - 1 else None
         full, sent, own, kept[place] = layer(
-            flags, operands, before, kept[place], above_at, tell, phase
+            flags, operands, before, kept[place], next_scale, above_at, phase
         )
 
     rms_parts = jnp.concatenate(in_parts(inv_rms), axis=2)

time: 683 us -> 679 us (level)
  no operation moved by 1% of the time
where the time goes in v7:
time: 679 us; the launch traced here: 678 us
  blocking collectives  562 us (83%)
  Pallas kernels  52.2 us (8%)
  waiting for transfers between devices  18.1 us (3%)
  local copies, waits for them, and re-layouts  14.8 us (2%)
  between operations  14.5 us (2%)
  starting transfers between devices  13.5 us (2%)
    all_gather x16, blocking collectives, per_device(): gathered = lax.all_gather(sent, 'tp')  474 us
    all_gather x1, blocking collectives, per_device(): second_inputs = lax.all_gather(inputs[first], 'tp')  39.6 us
    pallas_call x16, Pallas kernels, layer(): pl.pallas_call(functools.partial(layer_body, above_at=above_at, told=befo...  37.5 us
    all_gather x1, blocking collectives, per_device(): third_inputs = lax.all_gather(third, 'tp')  29.8 us
    all_to_all x1, blocking collectives, per_device(): came = lax.all_to_all(leaving, 'pipe', 0, 0, axis_index_groups=together)  18.7 us
  transfers between devices with their start and end apart: 8, of which 5 were waited for; matrix products, arithmetic and copies ran while one was open for 0% of the time, Pallas kernels for 2%

profile of v7, /device:TPU:1, one launch (start us, length us, event | category | flops | bytes accessed | tf_op | source)
XLA Modules:
  0.0 678.1 jit_solution(7007906834258154640)
XLA Ops:
  8.9 4.8 all-to-all-start
  13.9 4.5 all-to-all-done
  18.7 39.6 %all_gather.114.above = bf16[32,32,256]{2,1,0:T(8,128)(2,1)S(1)} all-gather(bf16[1,32,256]{2,1,0:T(8,128)(2,1)S(1)} %get-tuple-element.163), channel_id=1, replica_groups=mesh['pipe'=16,'tp'=32] {'tp'}, dimensions={0}, use_global_device_ids=true | all-gather | bytes 540672 | tf_op jit(solution)/shard_map/all_gather | solution.py:291
  58.3 29.2 %all-gather = bf16[1024,384]{1,0:T(8,128)(2,1)S(1)} all-gather(bf16[32,384]{1,0:T(8,128)(2,1)S(1)} %get-tuple-element.85), channel_id=2, replica_groups=mesh['pipe'=16,'tp'=32] {'tp'}, dimensions={0}, use_global_device_ids=true | all-gather | bytes 811008 | tf_op jit(solution)/shard_map/all_gather | solution.py:302
  88.8 29.8 %all-gather.1 = bf16[1024,256]{1,0:T(8,128)(2,1)S(1)} all-gather(bf16[32,256]{1,0:T(8,128)(2,1)S(1)} %get-tuple-element.88.here.above_own), channel_id=3, replica_groups=mesh['pipe'=16,'tp'=32] {'tp'}, dimensions={0}, use_global_device_ids=true | all-gather | bytes 540672 | tf_op jit(solution)/shard_map/all_gather | solution.py:309
  120.5 7.8 %expand.1 = (bf16[32,256,256]{2,1,0:T(8,128)(2,1)S(1)}, bf16[32,256,256]{2,1,0:T(8,128)(2,1)S(1)}, bf16[32,256,256]{2,1,0:T(8,128)(2,1)}, bf16[32,256,256]{2,1,0:T(8,128)(2,1)}) custom-call(s32[288]{0:T(512)S(1)} %reshape.80.code_ref, bf16[4,72,128,128]{3,2,1,0:T(8,128)(2,1)} %all-gather.21.cloned.1.call-done.came), custom_call_target="tpu_custom_call" | custom-call | tf_op jit(solution)/shard_map/expand/pallas_call | solution.py:74
  130.3 3.7 copy-done.1
  136.2 29.4 %all-gather.2 = bf16[1024,256]{1,0:T(8,128)(2,1)S(1)} all-gather(bf16[32,256]{1,0:T(8,128)(2,1)S(1)} %get-tuple-element.92), channel_id=4, replica_groups=mesh['pipe'=16,'tp'=32] {'tp'}, dimensions={0}, use_global_device_ids=true | all-gather | bytes 540672 | tf_op jit(solution)/shard_map/all_gather | solution.py:336
  169.3 29.6 %all-gather.3 = bf16[1024,256]{1,0:T(8,128)(2,1)S(1)} all-gather(bf16[32,256]{1,0:T(8,128)(2,1)S(1)} %get-tuple-element.96), channel_id=5, replica_groups=mesh['pipe'=16,'tp'=32] {'tp'}, dimensions={0}, use_global_device_ids=true | all-gather | bytes 540672 | tf_op jit(solution)/shard_map/all_gather | solution.py:336
  204.3 29.9 %all-gather.5 = bf16[1024,256]{1,0:T(8,128)(2,1)S(1)} all-gather(bf16[32,256]{1,0:T(8,128)(2,1)S(1)} %get-tuple-element.103), channel_id=7, replica_groups=mesh['pipe'=16,'tp'=32] {'tp'}, dimensions={0}, use_global_device_ids=true | all-gather | bytes 540672 | tf_op jit(solution)/shard_map/all_gather | solution.py:336
  241.9 30.9 %all-gather.6 = bf16[1024,384]{1,0:T(8,128)(2,1)S(1)} all-gather(bf16[32,384]{1,0:T(8,128)(2,1)S(1)} %convert_element_type.93), channel_id=8, replica_groups=mesh['pipe'=16,'tp'=32] {'tp'}, dimensions={0}, use_global_device_ids=true | all-gather | bytes 811008 | tf_op jit(solution)/shard_map/all_gather | solution.py:336
  274.9 29.3 %all-gather.7 = bf16[1024,256]{1,0:T(8,128)(2,1)S(1)} all-gather(bf16[32,256]{1,0:T(8,128)(2,1)S(1)} %get-tuple-element.110), channel_id=9, replica_groups=mesh['pipe'=16,'tp'=32] {'tp'}, dimensions={0}, use_global_device_ids=true | all-gather | bytes 540672 | tf_op jit(solution)/shard_map/all_gather | solution.py:336
  306.4 29.2 %all-gather.8 = bf16[1024,256]{1,0:T(8,128)(2,1)S(1)} all-gather(bf16[32,256]{1,0:T(8,128)(2,1)S(1)} %get-tuple-element.114), channel_id=10, replica_groups=mesh['pipe'=16,'tp'=32] {'tp'}, dimensions={0}, use_global_device_ids=true | all-gather | bytes 540672 | tf_op jit(solution)/shard_map/all_gather | solution.py:336
  338.5 29.3 %all-gather.9 = bf16[1024,256]{1,0:T(8,128)(2,1)S(1)} all-gather(bf16[32,256]{1,0:T(8,128)(2,1)S(1)} %get-tuple-element.118), channel_id=11, replica_groups=mesh['pipe'=16,'tp'=32] {'tp'}, dimensions={0}, use_global_device_ids=true | all-gather | bytes 540672 | tf_op jit(solution)/shard_map/all_gather | solution.py:336
  375.9 30.9 %all-gather.10 = bf16[1024,384]{1,0:T(8,128)(2,1)S(1)} all-gather(bf16[32,384]{1,0:T(8,128)(2,1)S(1)} %convert_element_type.94), channel_id=12, replica_groups=mesh['pipe'=16,'tp'=32] {'tp'}, dimensions={0}, use_global_device_ids=true | all-gather | bytes 811008 | tf_op jit(solution)/shard_map/all_gather | solution.py:336
  411.1 29.3 %all-gather.11 = bf16[1024,256]{1,0:T(8,128)(2,1)S(1)} all-gather(bf16[32,256]{1,0:T(8,128)(2,1)S(1)} %get-tuple-element.124), channel_id=13, replica_groups=mesh['pipe'=16,'tp'=32] {'tp'}, dimensions={0}, use_global_device_ids=true | all-gather | bytes 540672 | tf_op jit(solution)/shard_map/all_gather | solution.py:336
  442.6 29.0 %all-gather.12 = bf16[1024,256]{1,0:T(8,128)(2,1)S(1)} all-gather(bf16[32,256]{1,0:T(8,128)(2,1)S(1)} %get-tuple-element.128), channel_id=14, replica_groups=mesh['pipe'=16,'tp'=32] {'tp'}, dimensions={0}, use_global_device_ids=true | all-gather | bytes 540672 | tf_op jit(solution)/shard_map/all_gather | solution.py:336
  473.8 29.3 %all-gather.13 = bf16[1024,256]{1,0:T(8,128)(2,1)S(1)} all-gather(bf16[32,256]{1,0:T(8,128)(2,1)S(1)} %get-tuple-element.132), channel_id=15, replica_groups=mesh['pipe'=16,'tp'=32] {'tp'}, dimensions={0}, use_global_device_ids=true | all-gather | bytes 540672 | tf_op jit(solution)/shard_map/all_gather | solution.py:336
  511.0 30.9 %all-gather.14 = bf16[1024,384]{1,0:T(8,128)(2,1)S(1)} all-gather(bf16[32,384]{1,0:T(8,128)(2,1)S(1)} %convert_element_type.95), channel_id=16, replica_groups=mesh['pipe'=16,'tp'=32] {'tp'}, dimensions={0}, use_global_device_ids=true | all-gather | bytes 811008 | tf_op jit(solution)/shard_map/all_gather | solution.py:336
  544.0 29.3 %all-gather.15 = bf16[1024,256]{1,0:T(8,128)(2,1)S(1)} all-gather(bf16[32,256]{1,0:T(8,128)(2,1)S(1)} %get-tuple-element.138), channel_id=17, replica_groups=mesh['pipe'=16,'tp'=32] {'tp'}, dimensions={0}, use_global_device_ids=true | all-gather | bytes 540672 | tf_op jit(solution)/shard_map/all_gather | solution.py:336
  575.5 29.1 %all-gather.16 = bf16[1024,256]{1,0:T(8,128)(2,1)S(1)} all-gather(bf16[32,256]{1,0:T(8,128)(2,1)S(1)} %get-tuple-element.142), channel_id=18, replica_groups=mesh['pipe'=16,'tp'=32] {'tp'}, dimensions={0}, use_global_device_ids=true | all-gather | bytes 540672 | tf_op jit(solution)/shard_map/all_gather | solution.py:336
  606.7 29.3 %all-gather.17 = bf16[1024,256]{1,0:T(8,128)(2,1)S(1)} all-gather(bf16[32,256]{1,0:T(8,128)(2,1)S(1)} %get-tuple-element.146), channel_id=19, replica_groups=mesh['pipe'=16,'tp'=32] {'tp'}, dimensions={0}, use_global_device_ids=true | all-gather | bytes 540672 | tf_op jit(solution)/shard_map/all_gather | solution.py:336
  639.1 18.7 %all_to_all.10.mine = bf16[4,17,32,256]{3,2,1,0:T(8,128)(2,1)S(1)} all-to-all(bf16[4,17,32,256]{3,2,1,0:T(8,128)(2,1)S(1)} %pad_maximum_fusion), channel_id=1, replica_groups={{0,32,64,96},{128,160,192,224},{256,288,320,352},{384,416,448,480},{1,3..., dimensions={0} | all-to-all | bytes 2228224 | tf_op jit(solution)/shard_map/all_to_all | solution.py:352
  663.7 6.9 %slot_grads.1 = (bf16[72,128,128]{2,1,0:T(8,128)(2,1)}, f32[256,1]{1,0:T(8,128)S(1)}) custom-call(s32[73]{0:T(128)S(1)} %pad_add_fusion.code_ref, bf16[4,17,32,256]{3,2,1,0:T(8,128)(2,1)S(1)} %all_to_all.10.mine, bf16[4,17,32,256]{3,2,1,0:T(8,128)(2,1)S(1)} %collective-permute-done.4.other, bf16[4,32,256]{2,1,0:T(8,128)(2,1)S(1)} %bitcast.120, ...), custom_call_target="tpu_custom_call" | custom-call | tf_op jit(solution)/shard_map/slot_grads/pallas_call | solution.py:236
  (151 shorter events, 73.6 us)
Async XLA Ops:
  7.2 112.0 %all-gather.21.cloned.1.call-start = ((), (), s32[]{:S(2)}) async-start(), calls=%async_computation.2 | async-start | bytes 11796480 | tf_op jit(solution)/shard_map/all_gather | solution.py:290
  8.9 9.5 %all-to-all-start = ((bf16[4,48,256]{2,1,0:T(8,128)(2,1)}), bf16[4,48,256]{2,1,0:T(8,128)(2,1)S(1)}, u32[]{:S(2)}, u32[]{:S(2)}) async-start(bf16[4,48,256]{2,1,0:T(8,128)(2,1)} %pad_maximum_fusion.1), calls=%async_computation | async-start | bytes 196608 | tf_op jit(solution)/shard_map/all_to_all | solution.py:283
  13.7 185.2 %all-gather.23.cloned.1.call-start = ((), (), s32[]{:S(2)}) async-start(), calls=%async_computation.3 | async-start | bytes 1622016 | tf_op jit(solution)/shard_map/all_gather | solution.py:313
  87.5 31.1 %collective-permute-start = (bf16[32,256]{1,0:T(8,128)(2,1)S(1)}, bf16[32,256]{1,0:T(8,128)(2,1)S(1)}, u32[]{:S(2)}, u32[]{:S(2)}) collective-permute-start(bf16[32,256]{1,0:T(8,128)(2,1)S(1)} %get-tuple-element.162.here), channel_id=1, source_target_pairs={{128,0},{160,32},{192,64},{224,96},{256,128},{288,160},{320,192},{... | collective-permute-start | bytes 49160 | tf_op jit(solution)/shard_map/ppermute | solution.py:289
  134.0 31.6 %copy-start.12 = (bf16[32,256,256]{2,1,0:T(8,128)(2,1)S(1)}, bf16[32,256,256]{2,1,0:T(8,128)(2,1)}, u32[]{:S(2)}) copy-start(bf16[32,256,256]{2,1,0:T(8,128)(2,1)} %get-tuple-element.94.weight) | copy-start | bytes 12582916
  202.1 32.1 %copy-start = (bf16[3072,256]{1,0:T(8,128)(2,1)S(1)}, bf16[3072,256]{1,0:T(8,128)(2,1)}, u32[]{:S(2)}) copy-start(bf16[3072,256]{1,0:T(8,128)(2,1)} %all-gather.23.cloned.1.call-done) | copy-start | bytes 4718596
  202.1 32.1 %copy-start.6 = (bf16[32,256,256]{2,1,0:T(8,128)(2,1)S(1)}, bf16[32,256,256]{2,1,0:T(8,128)(2,1)}, u32[]{:S(2)}) copy-start(bf16[32,256,256]{2,1,0:T(8,128)(2,1)} %copy-done.5) | copy-start | bytes 12582916
  234.2 38.6 %copy-start.2 = (bf16[32,256,256]{2,1,0:T(8,128)(2,1)S(1)}, bf16[32,256,256]{2,1,0:T(8,128)(2,1)}, u32[]{:S(2)}) copy-start(bf16[32,256,256]{2,1,0:T(8,128)(2,1)} %get-tuple-element.91.weight) | copy-start | bytes 12582916
  234.2 38.6 %copy-start.20 = (bf16[16,32,256]{2,1,0:T(8,128)(2,1)S(1)}, bf16[16,32,256]{2,1,0:T(8,128)(2,1)}, u32[]{:S(2)}) copy-start(bf16[16,32,256]{2,1,0:T(8,128)(2,1)} %copy-done.19) | copy-start | bytes 786436
  237.1 4.8 collective-permute-start.1
  272.8 31.5 %copy-start.13 = (bf16[32,256,256]{2,1,0:T(8,128)(2,1)S(1)}, bf16[32,256,256]{2,1,0:T(8,128)(2,1)}, u32[]{:S(2)}) copy-start(bf16[32,256,256]{2,1,0:T(8,128)(2,1)} %get-tuple-element.94.weight) | copy-start | bytes 12582916
  272.8 31.5 %copy-start.28 = (bf16[16,32,256]{2,1,0:T(8,128)(2,1)S(1)}, bf16[16,32,256]{2,1,0:T(8,128)(2,1)}, u32[]{:S(2)}) copy-start(bf16[16,32,256]{2,1,0:T(8,128)(2,1)} %copy-done.27) | copy-start | bytes 786436
  304.3 31.4 %copy-start.10 = (bf16[32,256,256]{2,1,0:T(8,128)(2,1)S(1)}, bf16[32,256,256]{2,1,0:T(8,128)(2,1)}, u32[]{:S(2)}) copy-start(bf16[32,256,256]{2,1,0:T(8,128)(2,1)} %copy-done.8) | copy-start | bytes 12582916
  370.9 40.2 %copy-start.21 = (bf16[16,32,256]{2,1,0:T(8,128)(2,1)}, bf16[16,32,256]{2,1,0:T(8,128)(2,1)S(1)}, u32[]{:S(2)}) copy-start(bf16[16,32,256]{2,1,0:T(8,128)(2,1)S(1)} %get-tuple-element.135.rest_1_) | copy-start | bytes 786436
  370.9 5.0 collective-permute-start.2
  409.0 31.5 %copy-start.14 = (bf16[32,256,256]{2,1,0:T(8,128)(2,1)S(1)}, bf16[32,256,256]{2,1,0:T(8,128)(2,1)}, u32[]{:S(2)}) copy-start(bf16[32,256,256]{2,1,0:T(8,128)(2,1)} %get-tuple-element.94.weight) | copy-start | bytes 12582916
  409.0 31.5 %copy-start.24 = (bf16[16,32,256]{2,1,0:T(8,128)(2,1)S(1)}, bf16[16,32,256]{2,1,0:T(8,128)(2,1)}, u32[]{:S(2)}) copy-start(bf16[16,32,256]{2,1,0:T(8,128)(2,1)} %copy-done.23) | copy-start | bytes 786436
  440.5 31.2 %copy-start.11 = (bf16[32,256,256]{2,1,0:T(8,128)(2,1)S(1)}, bf16[32,256,256]{2,1,0:T(8,128)(2,1)}, u32[]{:S(2)}) copy-start(bf16[32,256,256]{2,1,0:T(8,128)(2,1)} %copy-done.8) | copy-start | bytes 12582916
  440.5 31.2 %copy-start.26 = (bf16[16,32,256]{2,1,0:T(8,128)(2,1)S(1)}, bf16[16,32,256]{2,1,0:T(8,128)(2,1)}, u32[]{:S(2)}) copy-start(bf16[16,32,256]{2,1,0:T(8,128)(2,1)} %copy-done.25) | copy-start | bytes 786436
  471.7 31.5 %copy-start.7 = (bf16[32,256,256]{2,1,0:T(8,128)(2,1)S(1)}, bf16[32,256,256]{2,1,0:T(8,128)(2,1)}, u32[]{:S(2)}) copy-start(bf16[32,256,256]{2,1,0:T(8,128)(2,1)} %copy-done.5) | copy-start | bytes 12582916
  471.7 31.5 %copy-start.22 = (bf16[16,32,256]{2,1,0:T(8,128)(2,1)S(1)}, bf16[16,32,256]{2,1,0:T(8,128)(2,1)}, u32[]{:S(2)}) copy-start(bf16[16,32,256]{2,1,0:T(8,128)(2,1)} %copy-done.21) | copy-start | bytes 786436
  503.2 38.7 %copy-start.4 = (bf16[32,256,256]{2,1,0:T(8,128)(2,1)S(1)}, bf16[32,256,256]{2,1,0:T(8,128)(2,1)}, u32[]{:S(2)}) copy-start(bf16[32,256,256]{2,1,0:T(8,128)(2,1)} %get-tuple-element.91.weight) | copy-start | bytes 12582916
  506.2 4.8 collective-permute-start.3
  657.8 5.8 collective-permute-start.4
  (18 other events, 119.2 us)
Sparse Core Ops, SparseCore 0:
  10.2 104.9 all-gather.20
  119.4 70.8 all-gather.22
